TPU v7x, 32 devices: a whole 2x2x4 slice. The times are simulated.
32 devices in a mesh: seq: 4 (over y, core), fsdp: 8 (over z, x).
Axes of the slice: x: 2, y: 2, z: 4, core: 2. Of those that a mesh axis runs over, the one named last changes fastest.
Arguments:
- tokens: bfloat16 [8, 4096, 768], P('fsdp', 'seq'), may hold values from -6 to 6
- lengths: int32 [8], P('fsdp'), may hold values from 3073 to 4096
- attn_gain: bfloat16 [768], P('fsdp'), may hold values from 0.5 to 1.5
- qkv_weight: bfloat16 [768, 2304], P('fsdp'), may hold values from -0.21875 to 0.21875
- proj_weight: bfloat16 [768, 768], P('fsdp'), may hold values from -6 to 6
- ffn_gain: bfloat16 [768], P('fsdp'), may hold values from 0.5 to 1.5
- in_weight: bfloat16 [768, 2304], P('fsdp'), may hold values from -0.21875 to 0.21875
- out_weight: bfloat16 [1152, 768], P('fsdp'), may hold values from -0.1875 to 0.1875
- out_grad: bfloat16 [8, 4096, 768], P('fsdp', 'seq'), may hold values from -6 to 6
Outputs:
- block_out: bfloat16 [8, 4096, 768], P('fsdp', 'seq')
- tokens_grad: float32 [8, 4096, 768], P('fsdp', 'seq')
- attn_gain_grad: float32 [768], P('fsdp')
- qkv_weight_grad: float32 [768, 2304], P('fsdp')
- proj_weight_grad: float32 [768, 768], P('fsdp')
- ffn_gain_grad: float32 [768], P('fsdp')
- in_weight_grad: float32 [768, 2304], P('fsdp')
- out_weight_grad: float32 [1152, 768], P('fsdp')
Inputs may be any that keep to these rules, and one draw needn't show every extreme that they name: `lengths`: positions at or beyond a sequence's length are padding, which no query attends to.
All inputs are finite; a program needn't handle non-finite values.
Results may differ from a plain program's by a relative error of at most 0.017.
Values may be sent and summed in bfloat16 or wider, within the bound.
No kernel may reach another device: no remote copies, remote signals or barrier semaphores. Data moves between devices by JAX's collectives and lax.ppermute only.
A program may use at most 192 MiB of HBM per device.

v0:
```python
import functools

import jax
import jax.numpy as jnp
from jax import lax
from jax.experimental import pallas as pl
from jax.experimental.pallas import tpu as pltpu
from jax.sharding import PartitionSpec as P

D = 768
HEADS = 12
HD = 64

epsilon = 1e-05
rope_base = 160000.0
masked_score = -1e30
LOG2E = 1.4426950408889634
LN2 = 0.6931471805599453

bf = jnp.bfloat16
f32 = jnp.float32
NN = ((1,), (0,))
NT = ((1,), (1,))
TN = ((0,), (0,))


def dg(a, b, dims):
    return lax.dot_general(a, b, (dims, ((), ())), preferred_element_type=f32)


def unit_rows_of(x):
    centred = x - jnp.mean(x, axis=-1, keepdims=True)
    inverse = lax.rsqrt(jnp.mean(centred * centred, axis=-1, keepdims=True) + epsilon)
    return centred * inverse, inverse


def qkv_kernel(heads, info_ref, x_ref, cos_ref, sin_ref, w_ref, *refs):
    n_ref, k_ref, v_ref, qt_ref, kt_ref, vt_ref, g_ref = refs[-7:]
    rb = x_ref.shape[0]
    value_at = heads * 128

    @pl.when(pl.program_id(0) == 0)
    def _():
        last = w_ref[:, w_ref.shape[1] - 128 :].astype(f32).T
        g_ref[...] = last[HD : HD + 8]

    unit, _ = unit_rows_of(x_ref[...].astype(f32))
    normed = (unit * g_ref[:1]).astype(bf)
    n_ref[...] = normed
    lane = lax.broadcasted_iota(jnp.int32, (rb, 128), 1)
    row = lax.broadcasted_iota(jnp.int32, (rb, 128), 0)
    position = info_ref[0] + pl.program_id(0) * rb + row
    bias = jnp.where(position < info_ref[1], 0.0, masked_score)
    key_tail = jnp.where(lane == HD, bias, 0.0)
    value_tail = jnp.where(lane < HD + 2, -1.0, 0.0)
    head_lane = lane < HD
    lower = (lane & (HD - 1)) < HD // 2
    one_row = jnp.where(lax.broadcasted_iota(jnp.int32, (HD, rb), 0) == 0, 1.0, 0.0).astype(bf)
    y = dg(normed, w_ref[...], NN)
    for h in range(heads):
        t = y[:, h * 128 : (h + 1) * 128]
        turned = jnp.where(lower, pltpu.roll(t, 128 - HD // 2, 1), pltpu.roll(t, HD // 2, 1))
        t = t * cos_ref[...] + turned * sin_ref[...]
        k_ref[h] = jnp.where(head_lane, pltpu.roll(t, HD, 1), key_tail).astype(bf)
        t = t.T.astype(bf)
        qt_ref[h, :HD] = t[:HD]
        qt_ref[h, HD:] = one_row
        kt_ref[h] = t[HD:]
    for h in range(heads):
        at = value_at + h // 2 * 128
        t = y[:, at : at + 128]
        turned = t if h % 2 == 0 else pltpu.roll(t, HD, 1)
        v_ref[h] = jnp.where(head_lane, turned, value_tail).astype(bf)
        if h % 2 == 0:
            t_rows = t.T.astype(bf)
        vt_ref[h, :HD] = t_rows[:HD] if h % 2 == 0 else t_rows[HD:]
        vt_ref[h, HD:] = one_row[:16]


def qkv_call(block, blocks, heads, info, x, cos, sin, w, carried):
    rows = x.shape[0]
    S = rows * blocks
    rb = min(256, rows)
    steps = rows // rb
    width = w.shape[1]
    at = lambda i: block * steps + i
    outs = (
        jax.ShapeDtypeStruct((S, D), bf),
        jax.ShapeDtypeStruct((heads, S, 128), bf),
        jax.ShapeDtypeStruct((heads, S, 128), bf),
        jax.ShapeDtypeStruct((heads, 128, S), bf),
        jax.ShapeDtypeStruct((heads, HD, S), bf),
        jax.ShapeDtypeStruct((heads, 80, S), bf),
    )
    in_specs = [
        pl.BlockSpec(memory_space=pltpu.SMEM),
        pl.BlockSpec((rb, D), lambda i: (i, 0)),
        pl.BlockSpec((rb, 128), lambda i: (at(i), 0)),
        pl.BlockSpec((rb, 128), lambda i: (at(i), 0)),
        pl.BlockSpec((D, width), lambda i: (0, 0)),
    ]
    aliases = {}
    if carried is not None:
        first = len(in_specs)
        in_specs += [pl.BlockSpec(memory_space=pl.ANY)] * 6
        aliases = {first + n: n for n in range(6)}
    return pl.pallas_call(
        functools.partial(qkv_kernel, heads),
        grid=(steps,),
        out_shape=outs,
        in_specs=in_specs,
        out_specs=(
            pl.BlockSpec((rb, D), lambda i: (at(i), 0)),
            pl.BlockSpec((heads, rb, 128), lambda i: (0, at(i), 0)),
            pl.BlockSpec((heads, rb, 128), lambda i: (0, at(i), 0)),
            pl.BlockSpec((heads, 128, rb), lambda i: (0, 0, at(i))),
            pl.BlockSpec((heads, HD, rb), lambda i: (0, 0, at(i))),
            pl.BlockSpec((heads, 80, rb), lambda i: (0, 0, at(i))),
        ),
        scratch_shapes=[pltpu.VMEM((8, D), f32)],
        input_output_aliases=aliases,
        compiler_params=pltpu.CompilerParams(vmem_limit_bytes=48 * 2**20),
        cost_estimate=pl.CostEstimate(
            flops=4 * rows * D * width, bytes_accessed=rows * 8192, transcendentals=0
        ),
        name="qkv",
    )(info, x, cos, sin, w, *(carried or ()))


def attend_kernel(kc, half, count, k_ref, qa_ref, qb_ref, v_ref, *refs):
    refs = refs[count:]
    pa_ref, pb_ref, oa_ref, ob_ref, la_ref, lb_ref = refs[:6]
    chunks = refs[6 : 6 + half]
    sa_ref, sb_ref, m_ref = refs[6 + half :]
    i = pl.program_id(0)
    rows = k_ref.shape[1]
    bq = qa_ref.shape[2]

    def stage(new, old):
        if new is not None:
            q_ref, s_new, new_slot = new
            q = q_ref[0]
            m = jnp.full((8, bq), -jnp.inf, f32)
        if old is not None:
            s_old, old_slot, p_ref, o_ref, l_ref, block = old
            top = jnp.max(m_ref[old_slot], axis=0, keepdims=True)
            acc = jnp.zeros((v_ref.shape[1], bq), f32)
        for c in range(rows // kc):
            at = slice(c * kc, (c + 1) * kc)
            if new is not None:
                s = dg(k_ref[0, at, :], q, NN)
                s_new[at, :] = s
                m = jnp.maximum(m, jnp.max(s.reshape(kc // 8, 8, bq), axis=0))
            if old is not None:
                p = jnp.exp2(s_old[at, :] - top).astype(bf)
                p_ref[0, at, :] = p
                acc = acc + dg(v_ref[0, :, at], p, NN)
        if new is not None:
            m_ref[new_slot] = m
        if old is not None:
            linv = 1.0 / acc[HD : HD + 1, :]
            o = acc[:HD, :] * linv
            o_ref[...] = o
            l_ref[0] = linv
            low = o.astype(bf)
            for j in range(half):

                @pl.when(block // 2 == j)
                def _():
                    chunks[j][:, old_slot * bq : (old_slot + 1) * bq] = low

    first = (qa_ref, sa_ref, 0)
    odd = (sb_ref, 1, pb_ref, ob_ref, lb_ref, 2 * i - 1)

    @pl.when(i == 0)
    def _():
        stage(first, None)

    @pl.when((i > 0) & (i < half))
    def _():
        stage(first, odd)

    @pl.when(i == half)
    def _():
        stage(None, odd)

    @pl.when(i < half)
    def _():
        stage((qb_ref, sb_ref, 1), (sa_ref, 0, pa_ref, oa_ref, la_ref, 2 * i))


def attend(h, k, qt, vt, groups, after, kc=256):
    S = k.shape[1]
    bq = S // groups // 2
    a = lambda i: jnp.minimum(i, groups - 1)
    b = lambda i: jnp.maximum(i - 1, 0)
    outs = pl.pallas_call(
        functools.partial(attend_kernel, kc, groups, len(after)),
        grid=(groups + 1,),
        out_shape=(jax.ShapeDtypeStruct((groups, S, bq), bf),) * 2
        + (jax.ShapeDtypeStruct((HD, S // 2), f32),) * 2
        + (jax.ShapeDtypeStruct((groups, 1, bq), f32),) * 2
        + (jax.ShapeDtypeStruct((HD, 2 * bq), bf),) * groups,
        in_specs=[
            pl.BlockSpec((1, S, 128), lambda i: (h, 0, 0)),
            pl.BlockSpec((1, 128, bq), lambda i: (h, 0, 2 * a(i))),
            pl.BlockSpec((1, 128, bq), lambda i: (h, 0, 2 * a(i) + 1)),
            pl.BlockSpec((1, 80, S), lambda i: (h, 0, 0)),
        ]
        + [pl.BlockSpec(memory_space=pl.ANY)] * len(after),
        out_specs=(
            pl.BlockSpec((1, S, bq), lambda i: (a(i), 0, 0)),
            pl.BlockSpec((1, S, bq), lambda i: (b(i), 0, 0)),
            pl.BlockSpec((HD, bq), lambda i: (0, a(i))),
            pl.BlockSpec((HD, bq), lambda i: (0, b(i))),
            pl.BlockSpec((1, 1, bq), lambda i: (a(i), 0, 0)),
            pl.BlockSpec((1, 1, bq), lambda i: (b(i), 0, 0)),
        )
        + (pl.BlockSpec((HD, 2 * bq), lambda i: (0, 0)),) * groups,
        scratch_shapes=[
            pltpu.VMEM((S, bq), f32),
            pltpu.VMEM((S, bq), f32),
            pltpu.VMEM((2, 8, bq), f32),
        ],
        compiler_params=pltpu.CompilerParams(vmem_limit_bytes=58 * 2**20),
        cost_estimate=pl.CostEstimate(
            flops=16 * HD * S * S, bytes_accessed=2 * S * S, transcendentals=S * S
        ),
        name="attend",
    )(k, qt, qt, vt, *after)
    return outs[:6], list(outs[6:])


def attend_back_kernel(kc, groups, v_ref, kt_ref, q_ref, *refs):
    oa_ref, ob_ref, la_ref, lb_ref, pa_ref, pb_ref, cos_ref, sin_ref, n_ref = refs[:9]
    do_refs = refs[9 : 9 + groups]
    outs = refs[-5 - groups : -5]
    grad_ref, acc_ref, do_ref, held_ref, sem = refs[-5:]
    i = pl.program_id(0)
    rows = v_ref.shape[1]
    width = q_ref.shape[2]
    bq = width // 2
    fetch = pltpu.make_async_copy(n_ref, held_ref, sem)

    @pl.when(i == 0)
    def _():
        fetch.start()
        acc_ref[...] = jnp.zeros_like(acc_ref)

    for j in range(groups):

        @pl.when(i == j)
        def _():
            do_ref[...] = do_refs[j][...]

    zero = jnp.zeros((HD, bq), bf)
    r = lax.broadcasted_iota(jnp.int32, (16, bq), 0)
    sides = []
    for n, (o_ref, l_ref, p_ref) in enumerate(((oa_ref, la_ref, pa_ref), (ob_ref, lb_ref, pb_ref))):
        at = slice(n * bq, (n + 1) * bq)
        dop = (do_ref[:, at].astype(f32) * l_ref[0]).astype(bf)
        delta = jnp.sum(dop.astype(f32) * o_ref[...], axis=0, keepdims=True)
        high = delta.astype(bf).astype(f32)
        tail = jnp.where(r == 0, high, jnp.where(r == 1, delta - high, 0.0)).astype(bf)
        doe = jnp.concatenate([dop, tail, jnp.zeros((128 - HD - 16, bq), bf)], axis=0)
        right_v = jnp.concatenate([dop, zero], axis=0)
        right_k = jnp.concatenate([zero, q_ref[0, :HD, at]], axis=0)
        sides.append((p_ref, doe, right_v, right_k))
    dq = [jnp.zeros((HD, bq), f32), jnp.zeros((HD, bq), f32)]
    for n, (p_ref, doe, right_v, right_k) in enumerate(sides):
        for c in range(rows // kc):
            at = slice(c * kc, (c + 1) * kc)
            p = p_ref[0, at, :]
            ds = p * dg(v_ref[0, at, :], doe, NN).astype(bf)
            acc_ref[at, :] = acc_ref[at, :] + dg(p, right_v, NT) + dg(ds, right_k, NT)
            dq[n] = dq[n] + dg(kt_ref[0, :, at], ds, NN)
    dq = jnp.concatenate(dq, axis=1) * HD**-0.5
    turned = jnp.concatenate([dq[HD // 2 :], -dq[: HD // 2]], axis=0)
    here = pl.ds(pl.multiple_of(i * width, width), width)
    dq = (dq * cos_ref[:, here] + turned * sin_ref[:, here]).astype(bf)
    for j in range(groups):

        @pl.when(i == j)
        def _():
            outs[j][:HD] = dq

    @pl.when(i == groups - 1)
    def _():
        fetch.wait()
        grad = jnp.zeros((3 * HD, D), f32)
        for j in range(groups):
            at = slice(j * width, (j + 1) * width)
            t = acc_ref[at, :].T
            dk = t[HD:] * LN2
            turned_k = jnp.concatenate([dk[HD // 2 :], -dk[: HD // 2]], axis=0)
            dk = dk * cos_ref[:, at] + turned_k * sin_ref[:, at]
            outs[j][HD : 2 * HD] = dk.astype(bf)
            outs[j][2 * HD :] = t[:HD].astype(bf)
            grad = grad + dg(outs[j][...], held_ref[at, :], NN)
        grad_ref[:, : 3 * HD] = grad.T.astype(bf)
        grad_ref[:, 3 * HD :] = jnp.zeros((D, HD), bf)


def attend_back(h, v, kt, qt, do, kept, cos, sin, normed, groups, place, after, kc=512):
    S = v.shape[1]
    width = S // groups
    bq = width // 2
    pa, pb, oa, ob, la, lb = kept
    columns, column, earlier = place
    extra = list(after) if earlier is None else [earlier] + list(after)
    whole = lambda i: (0, 0)
    by_block = lambda i: (i, 0, 0)
    outs = pl.pallas_call(
        functools.partial(attend_back_kernel, kc, groups),
        grid=(groups,),
        out_shape=(jax.ShapeDtypeStruct((3 * HD, width), bf),) * groups
        + (jax.ShapeDtypeStruct((D, columns), bf),),
        in_specs=[
            pl.BlockSpec((1, S, 128), lambda i: (h, 0, 0)),
            pl.BlockSpec((1, HD, S), lambda i: (h, 0, 0)),
            pl.BlockSpec((1, 128, width), lambda i: (h, 0, i)),
            pl.BlockSpec((HD, bq), lambda i: (0, i)),
            pl.BlockSpec((HD, bq), lambda i: (0, i)),
            pl.BlockSpec((1, 1, bq), by_block),
            pl.BlockSpec((1, 1, bq), by_block),
            pl.BlockSpec((1, S, bq), by_block),
            pl.BlockSpec((1, S, bq), by_block),
            pl.BlockSpec((HD, S), whole),
            pl.BlockSpec((HD, S), whole),
            pl.BlockSpec(memory_space=pl.ANY),
        ]
        + [pl.BlockSpec((HD, width), lambda i: (h, 0))] * groups
        + [pl.BlockSpec(memory_space=pl.ANY)] * len(extra),
        out_specs=(pl.BlockSpec((3 * HD, width), whole),) * groups
        + (pl.BlockSpec((D, 256), lambda i: (0, column)),),
        scratch_shapes=[
            pltpu.VMEM((S, 128), f32),
            pltpu.VMEM((HD, width), bf),
            pltpu.VMEM((S, D), bf),
            pltpu.SemaphoreType.DMA,
        ],
        input_output_aliases={} if earlier is None else {12 + groups: groups},
        compiler_params=pltpu.CompilerParams(vmem_limit_bytes=58 * 2**20),
        cost_estimate=pl.CostEstimate(
            flops=24 * HD * S * S, bytes_accessed=2 * S * S, transcendentals=0
        ),
        name="attend_back",
    )(v, kt, qt, oa, ob, la, lb, pa, pb, cos, sin, normed, *do, *extra)
    return list(outs[:groups]), outs[groups]


def normalize_back(gradient, unit_rows, inverse, gain_row):
    scaled = gradient * gain_row
    return inverse * (
        scaled
        - jnp.mean(scaled, axis=-1, keepdims=True)
        - unit_rows * jnp.mean(scaled * unit_rows, axis=-1, keepdims=True)
    )


def column(row_ref):
    row = row_ref[...].astype(f32)
    return jnp.broadcast_to(row, (8, row.shape[1])).T[:, :1]


def row_of(total):
    return jnp.broadcast_to(total, (total.shape[0], 128)).T[:1]


def half_kernel(packed, info_ref, in_ref, proj_ref, gain_ref, out_w_ref, *refs):
    half_ref = refs[-1]
    side = info_ref[0] & 1

    @pl.when(side == 0)
    def _():
        half_ref[...] = in_ref[...]

    @pl.when(side == 1)
    def _():
        short = in_ref.shape[0]
        half_ref[:, :D] = proj_ref[...]
        gain = jnp.broadcast_to(column(gain_ref), (short, 128)).astype(bf)
        half_ref[:, D : D + 128] = gain
        if packed:
            one, two, three = D + 128, 2 * D + 128, 2 * D + D // 2 + 128
            tall = out_w_ref.shape[0]
            half_ref[:, one:two] = out_w_ref[:short, :]
            half_ref[: tall - short, two:three] = out_w_ref[short:, : D // 2]
            half_ref[tall - short :, two:three] = out_w_ref[short:, D // 2 :]


def own_half(packed, info, in_w, proj_w, gain, out_w, after):
    vmem = pl.BlockSpec(memory_space=pltpu.VMEM)
    return pl.pallas_call(
        functools.partial(half_kernel, packed),
        out_shape=jax.ShapeDtypeStruct(in_w.shape, bf),
        in_specs=[pl.BlockSpec(memory_space=pltpu.SMEM)]
        + [vmem] * 4
        + [pl.BlockSpec(memory_space=pl.ANY)] * len(after),
        out_specs=vmem,
        name="own_half",
    )(info, in_w, proj_w, gain, out_w, *after)


def hold(array, after):
    def kernel(*refs):
        pass

    return pl.pallas_call(
        kernel,
        out_shape=jax.ShapeDtypeStruct(array.shape, array.dtype),
        in_specs=[pl.BlockSpec(memory_space=pl.ANY)] * (1 + len(after)),
        out_specs=pl.BlockSpec(memory_space=pl.ANY),
        input_output_aliases={0: 0},
        name="hold",
    )(array, *after)


def middle_kernel(groups, heads, ff, shards, info_ref, x_ref, dy_ref, mine_ref, other_ref, *refs):
    count = groups * heads
    given = len(refs) - count - groups - 13
    out_given = refs[:given]
    chunks = refs[given : given + count]
    d_chunks = refs[given + count : given + count + groups]
    (result_ref, dh_ref, mixed_ref, second_ref, dgu_ref, inner_ref, branch_ref,
     g_ref, t_ref, out_w_ref, w_ref, rest_ref, sems) = refs[given + count + groups :]
    width = heads * HD
    me = info_ref[0]

    @pl.when(pl.program_id(0) == 0)
    def _():
        def fetch(first, second):
            copies = [
                pltpu.make_async_copy(first, w_ref, sems.at[0]),
                pltpu.make_async_copy(second, rest_ref, sems.at[1]),
            ]
            for copy in copies:
                copy.start()
            for copy in copies:
                copy.wait()

        @pl.when((me & 1) == 0)
        def _():
            fetch(mine_ref, other_ref)

        @pl.when((me & 1) == 1)
        def _():
            fetch(other_ref, mine_ref)

        g_ref[...] = rest_ref[:, D : D + 128].astype(f32).T[:8]
        if given:
            out_w_ref[...] = out_given[0][...]
        else:
            tall, short = ff // shards, D // shards
            rest = tall - short
            one, two, three = D + 128, 2 * D + 128, 2 * D + D // 2 + 128
            for f in range(shards):
                src = slice(f * short, (f + 1) * short)
                out_w_ref[f * tall : f * tall + short, :] = rest_ref[src, one:two]
                dst = slice(f * tall + short, (f + 1) * tall)
                src = slice(f * short, f * short + rest)
                out_w_ref[dst, : D // 2] = rest_ref[src, two:three]
                src = slice(f * short + rest, f * short + 2 * rest)
                out_w_ref[dst, D // 2 :] = rest_ref[src, two:three]

    for h in range(heads):
        for j in range(groups):
            start = pl.multiple_of((me ^ j) * width + h * HD, HD)
            mixed_ref[pl.ds(start, HD), :] = chunks[h * groups + j][...]
    gain = g_ref[:1]
    proj = rest_ref[:, :D]
    hidden = x_ref[...].astype(f32) + dg(mixed_ref[...], proj, TN)
    unit, inverse = unit_rows_of(hidden)
    second = (unit * gain).astype(bf)
    second_ref[...] = second
    dy = dy_ref[...]
    result = hidden
    d_second = jnp.zeros_like(hidden)
    step = 384
    for c in range(ff // step):
        a = slice(c * step, (c + 1) * step)
        b = slice(ff + c * step, ff + (c + 1) * step)
        gate = dg(second, w_ref[:, a], NN)
        up = dg(second, w_ref[:, b], NN)
        d_inner = dg(dy, out_w_ref[a, :], NT)
        bell = 0.5 + 0.5 * lax.erf(gate * 0.7071067811865476)
        gelu = gate * bell
        inner = (gelu * up).astype(bf)
        inner_ref[:, a] = inner
        result = result + dg(inner, out_w_ref[a, :], NN)
        slope = bell + gate * (jnp.exp(-0.5 * gate * gate) * 0.3989422804014327)
        d_gate = (d_inner * up * slope).astype(bf)
        d_up = (d_inner * gelu).astype(bf)
        dgu_ref[:, a] = d_gate
        dgu_ref[:, b] = d_up
        d_second = d_second + dg(d_gate, w_ref[:, a], NT) + dg(d_up, w_ref[:, b], NT)
    result_ref[...] = result.astype(bf)
    d_hidden = dy.astype(f32) + normalize_back(d_second, unit, inverse, gain)
    dh_ref[...] = d_hidden
    branch = d_hidden.astype(bf)
    branch_ref[...] = branch
    t_ref[...] = dg(proj, branch, NT).astype(bf)
    for j in range(groups):
        start = pl.multiple_of((me ^ j) * width, HD)
        d_chunks[j][...] = t_ref[pl.ds(start, width), :]


def middle(groups, heads, shards, ff, info, x, dy, mine, other, out_w, chunks):
    rows = x.shape[0]
    rb = min(256, rows)
    by_row = lambda i: (i, 0)
    by_column = lambda i: (0, i)
    whole = lambda i: (0, 0)
    outs = pl.pallas_call(
        functools.partial(middle_kernel, groups, heads, ff, shards),
        grid=(rows // rb,),
        out_shape=(jax.ShapeDtypeStruct((heads * HD, rows), bf),) * groups
        + (
            jax.ShapeDtypeStruct((rows, D), bf),
            jax.ShapeDtypeStruct((rows, D), f32),
            jax.ShapeDtypeStruct((D, rows), bf),
            jax.ShapeDtypeStruct((rows, D), bf),
            jax.ShapeDtypeStruct((rows, 2 * ff), bf),
            jax.ShapeDtypeStruct((rows, ff), bf),
            jax.ShapeDtypeStruct((rows, D), bf),
        ),
        in_specs=[
            pl.BlockSpec(memory_space=pltpu.SMEM),
            pl.BlockSpec((rb, D), by_row),
            pl.BlockSpec((rb, D), by_row),
            pl.BlockSpec(memory_space=pl.ANY),
            pl.BlockSpec(memory_space=pl.ANY),
        ]
        + [pl.BlockSpec(w.shape, whole, pipeline_mode=pl.Buffered(1)) for w in out_w]
        + [pl.BlockSpec((HD, rb), by_column)] * (groups * heads),
        out_specs=(pl.BlockSpec((heads * HD, rb), by_column),) * groups
        + (
            pl.BlockSpec((rb, D), by_row),
            pl.BlockSpec((rb, D), by_row),
            pl.BlockSpec((D, rb), by_column),
            pl.BlockSpec((rb, D), by_row),
            pl.BlockSpec((rb, 2 * ff), by_row),
            pl.BlockSpec((rb, ff), by_row),
            pl.BlockSpec((rb, D), by_row),
        ),
        scratch_shapes=[
            pltpu.VMEM((8, D), f32),
            pltpu.VMEM((D, rb), bf),
            pltpu.VMEM((ff, D), bf),
            pltpu.VMEM(mine.shape, bf),
            pltpu.VMEM(mine.shape, bf),
            pltpu.SemaphoreType.DMA((2,)),
        ],
        compiler_params=pltpu.CompilerParams(vmem_limit_bytes=58 * 2**20),
        cost_estimate=pl.CostEstimate(
            flops=rows * D * (14 * ff + 4 * D), bytes_accessed=30 * 2**20, transcendentals=rows * ff
        ),
        name="middle",
    )(info, x, dy, mine, other, *out_w, *chunks)
    return list(outs[:groups]), outs[groups:]


def last_kernel(groups, chosen, x_ref, base_ref, gain_ref, *refs):
    count = groups * len(chosen)
    chunks = refs[:count]
    pairs = refs[count : 2 * count]
    value_refs = refs[2 * count : 3 * count]
    out_ref, dp_ref, wh_ref, g_ref = refs[-4:]
    both = groups * 2 * HD

    @pl.when(pl.program_id(0) == 0)
    def _():
        g_ref[...] = gain_ref[...].astype(f32).T[HD : HD + 8]
        for n, h in enumerate(chosen):
            side = (h & 1) * HD
            pieces = [ref[...] for ref in pairs[n * groups : (n + 1) * groups]]
            pieces += [ref[:, side : side + HD] for ref in value_refs[n * groups : (n + 1) * groups]]
            wh_ref[:, n * D : (n + 1) * D] = jnp.concatenate(pieces, axis=1)

    for n in range(len(chosen)):
        for j in range(groups):
            chunk = chunks[n * groups + j]
            start = n * D + j * 2 * HD
            dp_ref[start : start + 2 * HD, :] = chunk[: 2 * HD, :]
            start = n * D + both + j * HD
            dp_ref[start : start + HD, :] = chunk[2 * HD :, :]
    d_normed = dg(wh_ref[...], dp_ref[...], NN).T
    unit, inverse = unit_rows_of(x_ref[...].astype(f32))
    out_ref[...] = base_ref[...] + normalize_back(d_normed, unit, inverse, g_ref[:1])


def last(groups, heads, chosen, x, base, peers, chunks, after):
    rows = chunks[0].shape[1]
    rb = min(256, rows)
    by_row = lambda i: (i, 0)

    def tile(n):
        return pl.BlockSpec((D, 128), lambda i: (0, n), pipeline_mode=pl.Buffered(1))

    pairs = [tile(h) for h in chosen for _ in peers]
    value_tiles = [tile(heads + h // 2) for h in chosen for _ in peers]
    return pl.pallas_call(
        functools.partial(last_kernel, groups, chosen),
        grid=(rows // rb,),
        out_shape=jax.ShapeDtypeStruct((rows, D), f32),
        in_specs=[
            pl.BlockSpec((rb, D), by_row),
            pl.BlockSpec((rb, D), by_row),
            tile(peers[0].shape[1] // 128 - 1),
        ]
        + [pl.BlockSpec((3 * HD, rb), lambda i: (0, i))] * len(chunks)
        + pairs
        + value_tiles
        + [pl.BlockSpec(memory_space=pl.ANY)] * len(after),
        out_specs=pl.BlockSpec((rb, D), by_row),
        scratch_shapes=[
            pltpu.VMEM((len(chosen) * D, rb), bf),
            pltpu.VMEM((D, len(chosen) * D), bf),
            pltpu.VMEM((8, D), f32),
        ],
        compiler_params=pltpu.CompilerParams(vmem_limit_bytes=58 * 2**20),
        cost_estimate=pl.CostEstimate(
            flops=2 * len(chosen) * rows * D * D, bytes_accessed=12 * 2**20, transcendentals=0
        ),
        name="last",
    )(x, base, peers[0], *chunks, *(list(peers) * (2 * len(chosen))), *after)


def pass_on(arrays, after):
    vmem = pl.BlockSpec(memory_space=pltpu.VMEM)
    count = len(arrays)

    def kernel(*refs):
        for source, target in zip(refs[:count], refs[-count:]):
            target[...] = source[...]

    return pl.pallas_call(
        kernel,
        out_shape=tuple(jax.ShapeDtypeStruct(a.shape, a.dtype) for a in arrays),
        in_specs=[vmem] * count + [pl.BlockSpec(memory_space=pl.ANY)] * len(after),
        out_specs=(vmem,) * count,
        compiler_params=pltpu.CompilerParams(vmem_limit_bytes=58 * 2**20),
        name="pass_on",
    )(*arrays, *after)


def own_kernel(groups, heads, info_ref, w_ref, gain_ref, out_ref):
    for g in range(groups):

        @pl.when(info_ref[0] == g)
        def _():
            def piece(t, h):
                start = t * D + (g * heads + h) * HD
                return w_ref[:, start : start + HD]

            pieces = []
            for h in range(heads):
                pieces += [piece(0, h), piece(1, h)]
            pieces += [piece(2, h) for h in range(heads)] + [column(gain_ref).astype(bf)]
            missing = out_ref.shape[2] - 3 * heads * HD - 1
            pieces.append(jnp.zeros((w_ref.shape[0], missing), bf))
            own = jnp.concatenate(pieces, axis=1)
            for f in range(out_ref.shape[0]):
                out_ref[f] = own


def own_columns(groups, heads, shards, info, w, gain):
    width = (3 * heads * HD + 128) // 128 * 128
    return pl.pallas_call(
        functools.partial(own_kernel, groups, heads),
        out_shape=jax.ShapeDtypeStruct((shards, w.shape[0], width), bf),
        in_specs=[
            pl.BlockSpec(memory_space=pltpu.SMEM),
            pl.BlockSpec(memory_space=pltpu.VMEM),
            pl.BlockSpec(memory_space=pltpu.VMEM),
        ],
        out_specs=pl.BlockSpec(memory_space=pltpu.VMEM),
        name="own_columns",
    )(info, w, gain)


def tables_kernel(cos_ref, sin_ref, cos_rows_ref, sin_rows_ref, cos_t_ref, sin_t_ref):
    c, s = cos_ref[...], sin_ref[...]
    cos_t_ref[...] = jnp.concatenate([c, c], axis=0)
    sin_t_ref[...] = jnp.concatenate([s, s], axis=0)
    scale = HD**-0.5 * LOG2E
    cos_rows_ref[...] = jnp.concatenate([c * scale, c * scale, c, c], axis=0).T
    sin_rows_ref[...] = jnp.concatenate([s * -scale, s * scale, -s, s], axis=0).T


def tables(cosine, sine):
    half, S = cosine.shape
    rb = min(1024, S)
    return pl.pallas_call(
        tables_kernel,
        grid=(S // rb,),
        out_shape=(jax.ShapeDtypeStruct((S, 4 * half), f32),) * 2
        + (jax.ShapeDtypeStruct((2 * half, S), f32),) * 2,
        in_specs=[pl.BlockSpec((half, rb), lambda i: (0, i))] * 2,
        out_specs=(pl.BlockSpec((rb, 4 * half), lambda i: (i, 0)),) * 2
        + (pl.BlockSpec((2 * half, rb), lambda i: (0, i)),) * 2,
        name="tables",
    )(cosine, sine)


def wide_kernel(second_ref, dgu_ref, mixed_ref, branch_ref, out_ref):
    g = pl.program_id(0)
    end = pl.num_programs(0) - 1

    @pl.when(g < end)
    def _():
        out_ref[0] = dg(second_ref[...], dgu_ref[...], TN).astype(bf)

    @pl.when(g == end)
    def _():
        out_ref[0] = dg(mixed_ref[...], branch_ref[...], NN).astype(bf)


def wide_grads(second, d_gate_up, mixed_t, branch):
    rows = second.shape[0]
    steps = d_gate_up.shape[1] // D
    whole = lambda i: (0, 0)
    return pl.pallas_call(
        wide_kernel,
        grid=(steps + 1,),
        in_specs=[
            pl.BlockSpec((rows, D), whole),
            pl.BlockSpec((rows, D), lambda i: (0, jnp.minimum(i, steps - 1))),
            pl.BlockSpec((D, rows), whole),
            pl.BlockSpec((rows, D), whole),
        ],
        out_specs=pl.BlockSpec((1, D, D), lambda i: (i, 0, 0)),
        out_shape=jax.ShapeDtypeStruct((steps + 1, D, D), bf),
        compiler_params=pltpu.CompilerParams(vmem_limit_bytes=58 * 2**20),
        cost_estimate=pl.CostEstimate(
            flops=2 * rows * D * D * (steps + 1), bytes_accessed=16 * 2**20, transcendentals=0
        ),
        name="wide_grads",
    )(second, d_gate_up, mixed_t, branch)


def tall_kernel(inner_ref, dy_ref, *refs):
    refs[-2][...] = dg(inner_ref[...], dy_ref[...], TN).astype(bf)


def tall_grads(inner, dy, wide, after):
    rows, ff = inner.shape
    step = ff // 3
    return pl.pallas_call(
        tall_kernel,
        grid=(3,),
        in_specs=[
            pl.BlockSpec((rows, step), lambda i: (0, i)),
            pl.BlockSpec((rows, D), lambda i: (0, 0)),
        ]
        + [pl.BlockSpec(memory_space=pl.ANY)] * (1 + len(after)),
        out_specs=(
            pl.BlockSpec((step, D), lambda i: (i, 0)),
            pl.BlockSpec(memory_space=pl.ANY),
        ),
        out_shape=(
            jax.ShapeDtypeStruct((ff, D), bf),
            jax.ShapeDtypeStruct(wide.shape, bf),
        ),
        input_output_aliases={2: 1},
        compiler_params=pltpu.CompilerParams(vmem_limit_bytes=58 * 2**20),
        cost_estimate=pl.CostEstimate(
            flops=2 * rows * D * ff, bytes_accessed=6 * 2**20, transcendentals=0
        ),
        name="tall_grads",
    )(inner, dy, wide, *after)


def add_kernel(count, *refs):
    total = None
    for ref in refs[:count]:
        for j in range(ref.shape[0]):
            term = ref[j].astype(f32)
            total = term if total is None else total + term
    out_ref = refs[-1]
    out_ref[...] = total.astype(out_ref.dtype)


def add_up(arrays, after, dtype=bf):
    arrays = [a if a.ndim == 3 else a[None] for a in arrays]
    rows, columns = arrays[0].shape[1:]
    rb = 256 if rows % 256 == 0 else rows
    return pl.pallas_call(
        functools.partial(add_kernel, len(arrays)),
        grid=(rows // rb,),
        out_shape=jax.ShapeDtypeStruct((rows, columns), dtype),
        in_specs=[pl.BlockSpec((n, rb, columns), lambda i: (0, i, 0)) for n in [a.shape[0] for a in arrays]]
        + [pl.BlockSpec(memory_space=pl.ANY)] * len(after),
        out_specs=pl.BlockSpec((rb, columns), lambda i: (i, 0)),
        compiler_params=pltpu.CompilerParams(vmem_limit_bytes=58 * 2**20),
        name="add_up",
    )(*arrays, *after)


def up16(n):
    return -(-n // 16) * 16


def owned_kernel(wide_ref, tall_ref, *refs):
    out_ref = refs[-1]
    start = 0
    for ref in (wide_ref, tall_ref):
        total = ref[0].astype(f32)
        for f in range(1, ref.shape[0]):
            total = total + ref[f].astype(f32)
        out_ref[start : start + ref.shape[1], :] = total.astype(bf)
        start += up16(ref.shape[1])


def owned(wide, tall, after):
    vmem = pl.BlockSpec(memory_space=pltpu.VMEM)
    return pl.pallas_call(
        owned_kernel,
        out_shape=jax.ShapeDtypeStruct((up16(wide.shape[1]) + up16(tall.shape[1]), D), bf),
        in_specs=[vmem, vmem] + [pl.BlockSpec(memory_space=pl.ANY)] * len(after),
        out_specs=vmem,
        compiler_params=pltpu.CompilerParams(vmem_limit_bytes=58 * 2**20),
        name="owned",
    )(wide, tall, *after)


def finish_wide_kernel(groups, info_ref, w_ref, gain_ref, *refs):
    in_ref, proj_ref, dgain_ref, out_ref, held_ref = refs[groups:]
    shard = w_ref.shape[0]
    start = up16(shard)
    tall = 0.0
    for j in range(groups):
        held_ref[info_ref[0] ^ j] = refs[j][...]
        tall = tall + refs[j][start : start + out_ref.shape[0], :].astype(f32)
    out_ref[...] = tall
    total = 0.0
    for g in range(groups - 1):
        at = slice(g * D, (g + 1) * D)
        grad = held_ref[g, :shard, :].astype(f32)
        in_ref[:, at] = grad
        total = total + jnp.sum(w_ref[:, at].astype(f32) * grad, axis=1, keepdims=True)
    proj_ref[...] = held_ref[groups - 1, :shard, :].astype(f32)
    dgain_ref[...] = row_of(total / column(gain_ref))


def finish_qkv_kernel(groups, heads, info_ref, w_ref, gain_ref, *refs):
    out_ref, dgain_ref, held_ref = refs[groups : groups + 3]
    for j in range(groups):
        held_ref[info_ref[0] ^ j] = refs[j][...]
    pieces = []
    for t in range(3):
        for g in range(groups):
            for h in range(heads):
                start = h * 256 + t * HD
                pieces.append(held_ref[g, :, start : start + HD].astype(f32))
    grad = jnp.concatenate(pieces, axis=1)
    out_ref[...] = grad
    total = jnp.sum(w_ref[...].astype(f32) * grad, axis=1, keepdims=True)
    dgain_ref[...] = row_of(total / column(gain_ref))


def finish(kernel, groups, info, w, gain, parts, shapes, name):
    vmem = pl.BlockSpec(memory_space=pltpu.VMEM)
    return pl.pallas_call(
        kernel,
        out_shape=tuple(jax.ShapeDtypeStruct(shape, f32) for shape in shapes),
        in_specs=[pl.BlockSpec(memory_space=pltpu.SMEM)] + [vmem] * (2 + groups),
        out_specs=(vmem,) * len(shapes),
        scratch_shapes=[pltpu.VMEM((groups,) + parts[0].shape, bf)],
        compiler_params=pltpu.CompilerParams(vmem_limit_bytes=58 * 2**20),
        name=name,
    )(info, w, gain, *parts)


def body(
    tokens, lengths, attn_gain, qkv_weight, proj_weight, ffn_gain, in_weight, out_weight, out_grad
):
    rows = tokens.shape[1]
    groups = lax.axis_size("seq")
    shards = lax.axis_size("fsdp")
    heads = HEADS // groups
    shard = D // shards
    me = lax.axis_index("seq")

    def swap(array, j, axis="seq"):
        size = lax.axis_size(axis)
        return lax.ppermute(array, axis, [(i, i ^ j) for i in range(size)])

    def exchange(chunks):
        return [chunks[0]] + [swap(chunks[j], j) for j in range(1, groups)]

    def gather(array):
        return lax.all_gather(array, "fsdp", axis=0, tiled=True)

    place = jnp.stack([me]).astype(jnp.int32)
    x0 = tokens[0]
    across = swap(x0, 2)
    near = swap(x0, 1)
    attn_row = attn_gain[None, :]
    ffn_row = ffn_gain[None, :]
    own = own_columns(groups, heads, shards, place, qkv_weight, attn_row)
    own = lax.all_to_all(own, "fsdp", split_axis=0, concat_axis=0, tiled=True).reshape(D, -1)

    half = HD // 2
    frequency = rope_base ** (-(lax.iota(f32, half) * 2.0) / HD)
    starts = [(me ^ j) * rows for j in range(groups)]
    positions = jnp.concatenate([s + lax.iota(jnp.int32, rows) for s in starts]).astype(f32)
    angles = frequency[:, None] * positions[None, :]
    cos_rows, sin_rows, cos_t, sin_t = tables(jnp.cos(angles), jnp.sin(angles))

    def project(j, block, carried):
        info = jnp.stack([starts[j], lengths[0]]).astype(jnp.int32)
        return qkv_call(j, groups, heads, info, block, cos_rows, sin_rows, own, carried)

    diagonal = swap(across, 1)
    carried = project(2, across, None)
    carried = project(0, x0, carried)
    carried = project(1, near, carried)
    normed, k, v, qt, kt, vt = project(3, diagonal, carried)

    ff = in_weight.shape[1] // 2
    tall = out_weight.shape[0]
    packed = shards <= 8
    mine = gather(own_half(packed, place, in_weight, proj_weight, ffn_row, out_weight, [own, cos_t]))
    out_full = [] if packed else [gather(out_weight)]

    own = hold(own, [normed])
    own_near, own_across = swap(own, 1), swap(own, 2)
    own_diagonal = swap(own_across, 1)
    peers = [own, own_near, own_across, own_diagonal]

    kept = []
    chunks = []
    orders = [[], [own_near, own_across], [own_diagonal]]
    for h in range(heads):
        before = [kept[-1][2]] if kept else []
        if h == 2:
            before += chunks[1:groups]
        saved, mixed = attend(h, k, qt, vt, groups, orders[h] + before)
        kept.append(saved)
        chunks += exchange(mixed)
        if h == heads - 2:
            mine = hold(mine, [saved[2]])
            other = swap(mine, 1)

    dy = out_grad[0]
    d_mixed, (result, d_hidden, mixed_t, second, d_gate_up, inner, branch) = middle(
        groups, heads, shards, ff, place, x0, dy, mine, other, out_full, chunks
    )
    d_mixed = exchange(d_mixed)

    def to_owner(array):
        parts = array.reshape(shards, array.shape[0] // shards, -1)
        return lax.all_to_all(parts, "fsdp", split_axis=0, concat_axis=0, tiled=True)

    def from_peers(array):
        return [array] + [swap(array, j) for j in range(1, groups)]

    wide_grad = wide_grads(second, d_gate_up, mixed_t, branch)
    tall_grad, wide_grad = tall_grads(inner, dy, wide_grad, d_mixed[1:])
    wide_sent = lax.all_to_all(wide_grad, "seq", split_axis=0, concat_axis=0, tiled=True)
    tall_parts = to_owner(tall_grad)

    def back(h, grad_place, after):
        return attend_back(
            h, v, kt, qt, d_mixed, kept[h], cos_t, sin_t, normed, groups, grad_place, after
        )

    sent_0, qkv_first = back(0, (512, 0, None), [tall_grad])
    wide_sum = add_up([wide_sent], [qkv_first])
    wide_parts = to_owner(wide_sum)
    received_0 = exchange(sent_0)

    sent_1, qkv_first = back(1, (512, 1, qkv_first), [wide_sum])
    both = owned(wide_parts, tall_parts, [qkv_first] + received_0[1:])
    both_peers = from_peers(both)
    received_1 = exchange(sent_1)
    qkv_parts = to_owner(qkv_first)

    sent_2, qkv_second = back(2, (256, 0, None), [both])
    *others, qkv_second = pass_on(sent_2[1:] + [qkv_second], received_1[1:] + both_peers[1:] + [qkv_parts])
    sent_2 = sent_2[:1] + others
    received_2 = exchange(sent_2)
    qkv_second_parts = to_owner(qkv_second)

    base = last(
        groups, heads, (0, 1), x0, d_hidden, peers, received_0 + received_1, [qkv_second]
    )
    first_sum = add_up([qkv_parts], [qkv_second])
    in_weight_grad, proj_weight_grad, ffn_gain_grad, out_weight_grad = finish(
        functools.partial(finish_wide_kernel, groups),
        groups, place, in_weight, ffn_row, both_peers,
        ((shard, 2 * ff), (shard, D), (1, shard), (tall, D)), "finish_wide",
    )
    second_sum = add_up([qkv_second_parts], [])
    qkv_peers = from_peers(jnp.concatenate([first_sum, second_sum], axis=1))
    tokens_grad = last(groups, heads, (2,), x0, base, peers, received_2, [])
    qkv_weight_grad, attn_gain_grad = finish(
        functools.partial(finish_qkv_kernel, groups, heads),
        groups, place, qkv_weight, attn_row, qkv_peers,
        ((shard, 3 * D), (1, shard)), "finish_qkv",
    )
    return (
        result[None],
        tokens_grad[None],
        attn_gain_grad[0],
        qkv_weight_grad,
        proj_weight_grad,
        ffn_gain_grad[0],
        in_weight_grad,
        out_weight_grad,
    )


def solution(mesh):
    in_specs = (
        P("fsdp", "seq", None),
        P("fsdp"),
        P("fsdp"),
        P("fsdp", None),
        P("fsdp", None),
        P("fsdp"),
        P("fsdp", None),
        P("fsdp", None),
        P("fsdp", "seq", None),
    )
    out_specs = (
        P("fsdp", "seq", None),
        P("fsdp", "seq", None),
        P("fsdp"),
        P("fsdp", None),
        P("fsdp", None),
        P("fsdp"),
        P("fsdp", None),
        P("fsdp", None),
    )
    return jax.shard_map(body, mesh=mesh, in_specs=in_specs, out_specs=out_specs, check_vma=False)
```

profile of v0, /device:TPU:1, one launch (start us, length us, event | category | flops | bytes accessed | tf_op | source)
XLA Modules:
  0.0 503.9 jit_solution(17922956293042481217)
XLA Ops:
  7.2 2.2 own_columns.1
  9.3 6.4 %all-to-all-start = ((bf16[8,96,640]{2,1,0:T(8,128)(2,1)}), bf16[8,96,640]{2,1,0:T(8,128)(2,1)S(1)}, u32[]{:S(2)}, u32[]{:S(2)}) async-start(bf16[8,96,640]{2,1,0:T(8,128)(2,1)} %own_columns.1), calls=%async_computation | async-start | bytes 1966080 | tf_op jit(solution)/shard_map/all_to_all | solution.py:902
  17.1 2.8 multiply_sine_fusion
  19.9 4.8 tables.1
  24.6 14.3 %all-to-all-done = bf16[8,96,640]{2,1,0:T(8,128)(2,1)S(1)} async-done(((bf16[8,96,640]{2,1,0:T(8,128)(2,1)}), bf16[8,96,640]{2,1,0:T(8,128)(2,1)S(1)}, u32[]{:S(2)}, u32[]{:S(2)}) %all-to-all-start) | async-done | bytes 983072 | tf_op jit(solution)/shard_map/all_to_all | solution.py:902
  39.9 2.3 own_half.1
  42.2 2.0 collective-permute-start.2
  44.3 6.8 %collective-permute-done.x_ref = bf16[1024,768]{1,0:T(8,128)(2,1)} collective-permute-done((bf16[1024,768]{1,0:T(8,128)(2,1)}, bf16[1024,768]{1,0:T(8,128)(2,1)}, u32[]{:S(2)}, u32[]{:S(2)}) %collective-permute-start) | collective-permute-done | bytes 1572896 | tf_op jit(solution)/shard_map/ppermute | solution.py:887
  51.1 1.9 collective-permute-start.1
  55.0 6.3 %qkv.4 = (bf16[4096,768]{1,0:T(8,128)(2,1)}, bf16[3,4096,128]{2,1,0:T(8,128)(2,1)}, bf16[3,4096,128]{2,1,0:T(8,128)(2,1)}, bf16[3,128,4096]{2,1,0:T(8,128)(2,1)}...) custom-call(s32[2]{0:T(128)S(1)} %get-tuple-element.205.info_ref, ...), custom_call_target="tpu_custom_call" | custom-call | flops 2013265920 | bytes 8388608 | tf_op jit(solution)/shard_map/qkv/pallas_call | solution.py:107
  61.3 6.3 %qkv.5 = (bf16[4096,768]{1,0:T(8,128)(2,1)}, bf16[3,4096,128]{2,1,0:T(8,128)(2,1)}, bf16[3,4096,128]{2,1,0:T(8,128)(2,1)}, bf16[3,128,4096]{2,1,0:T(8,128)(2,1)}...) custom-call(s32[2]{0:T(128)S(1)} %get-tuple-element.204.info_ref, ...), custom_call_target="tpu_custom_call", output_to_operand_aliasing={{0}: (5, {}), {1}: (6, {}), {2}: (7, {}), {3}: (8, {}), {4}... | custom-call | flops 2013265920 | bytes 8388608 | tf_op jit(solution)/shard_map/qkv/pallas_call | solution.py:107
  67.6 6.1 %qkv.6 = (bf16[4096,768]{1,0:T(8,128)(2,1)}, bf16[3,4096,128]{2,1,0:T(8,128)(2,1)}, bf16[3,4096,128]{2,1,0:T(8,128)(2,1)}, bf16[3,128,4096]{2,1,0:T(8,128)(2,1)}...) custom-call(s32[2]{0:T(128)S(1)} %pad_add_fusion.1.info_ref, ...), custom_call_target="tpu_custom_call", output_to_operand_aliasing={{0}: (5, {}), {1}: (6, {}), {2}: (7, {}), {3}: (8, {}), {4}... | custom-call | flops 2013265920 | bytes 8388608 | tf_op jit(solution)/shard_map/qkv/pallas_call | solution.py:107
  73.7 6.2 %qkv.7 = (bf16[4096,768]{1,0:T(8,128)(2,1)}, bf16[3,4096,128]{2,1,0:T(8,128)(2,1)}, bf16[3,4096,128]{2,1,0:T(8,128)(2,1)}, bf16[3,128,4096]{2,1,0:T(8,128)(2,1)}...) custom-call(s32[2]{0:T(128)S(1)} %pad_add_fusion.info_ref, ...), custom_call_target="tpu_custom_call", output_to_operand_aliasing={{0}: (5, {}), {1}: (6, {}), {2}: (7, {}), {3}: (8, {}), {4}... | custom-call | flops 2013265920 | bytes 8388608 | tf_op jit(solution)/shard_map/qkv/pallas_call | solution.py:107
  83.2 20.5 %attend.3 = (bf16[4,4096,512]{2,1,0:T(8,128)(2,1)}, bf16[4,4096,512]{2,1,0:T(8,128)(2,1)}, f32[64,2048]{1,0:T(8,128)}, f32[64,2048]{1,0:T(8,128)}, f32[4,1,512]{...) custom-call(bf16[3,4096,128]{2,1,0:T(8,128)(2,1)} %get-tuple-element, ...), custom_call_target="tpu_custom_call" | custom-call | flops 17179869184 | bytes 33554432 | tf_op jit(solution)/shard_map/attend/pallas_call | solution.py:197
  103.7 1.7 collective-permute-done.4.refs_1_.refs_10_.refs_14_.refs_18_.refs_22_.refs_6_
  106.7 20.9 %attend.4 = (bf16[4,4096,512]{2,1,0:T(8,128)(2,1)}, bf16[4,4096,512]{2,1,0:T(8,128)(2,1)}, f32[64,2048]{1,0:T(8,128)}, f32[64,2048]{1,0:T(8,128)}, f32[4,1,512]{...) custom-call(bf16[3,4096,128]{2,1,0:T(8,128)(2,1)} %get-tuple-element, ...), custom_call_target="tpu_custom_call" | custom-call | flops 17179869184 | bytes 33554432 | tf_op jit(solution)/shard_map/attend/pallas_call | solution.py:197
  131.7 4.2 collective-permute-done.6.refs_2_.refs_1_
  139.7 21.0 %attend.5 = (bf16[4,4096,512]{2,1,0:T(8,128)(2,1)}, bf16[4,4096,512]{2,1,0:T(8,128)(2,1)}, f32[64,2048]{1,0:T(8,128)}, f32[64,2048]{1,0:T(8,128)}, f32[4,1,512]{...) custom-call(bf16[3,4096,128]{2,1,0:T(8,128)(2,1)} %get-tuple-element, ...), custom_call_target="tpu_custom_call" | custom-call | flops 17179869184 | bytes 33554432 | tf_op jit(solution)/shard_map/attend/pallas_call | solution.py:197
  161.8 1.4 collective-permute-start.15
  163.2 3.5 collective-permute-done.14.refs_10_
  166.7 3.0 collective-permute-done.15.refs_11_
  170.3 28.6 %middle.1 = (bf16[192,1024]{1,0:T(8,128)(2,1)}, bf16[192,1024]{1,0:T(8,128)(2,1)}, bf16[192,1024]{1,0:T(8,128)(2,1)}, bf16[192,1024]{1,0:T(8,128)(2,1)}, bf16[10...) custom-call(s32[1]{0:T(128)} %bitcast.info_ref, ...), custom_call_target="tpu_custom_call" | custom-call | flops 15099494400 | bytes 31457280 | tf_op jit(solution)/shard_map/middle/pallas_call | solution.py:514
  199.5 1.7 collective-permute-start.18
  201.2 10.2 %wide_grads.1.refs_0_ = bf16[4,768,768]{2,1,0:T(8,128)(2,1)} custom-call(bf16[1024,768]{1,0:T(8,128)(2,1)} %get-tuple-element.158.second_ref, bf16[1024,2304]{1,0:T(8,128)(2,1)} %get-tuple-element.159.dgu_ref, bf16[768,1024]{1,0:T(8,128)(2,1)} %get-tuple-element.160.mixed_ref, bf16[1024,768]{1,0:T(8,128)(2,1)} %get-tuple-element.161.branch_ref), custom_call_target="tpu_custom_call" | custom-call | flops 4831838208 | bytes 16777216 | tf_op jit(solution)/shard_map/wide_grads/pallas_call | solution.py:723
  211.4 7.3 %collective-permute-done.18.refs_3_.refs_12_ = bf16[192,1024]{1,0:T(8,128)(2,1)S(1)} collective-permute-done((bf16[192,1024]{1,0:T(8,128)(2,1)}, bf16[192,1024]{1,0:T(8,128)(2,1)S(1)}, u32[]{:S(2)}, u32[]{:S(2)}) %collective-permute-start.18) | collective-permute-done | bytes 393248 | tf_op jit(solution)/shard_map/ppermute | solution.py:887
  219.5 5.5 %tall_grads.1 = (bf16[1152,768]{1,0:T(8,128)(2,1)}, bf16[4,768,768]{2,1,0:T(8,128)(2,1)}) custom-call(bf16[1024,1152]{1,0:T(8,128)(2,1)} %get-tuple-element.157.inner_ref, bf16[1024,768]{1,0:T(8,128)(2,1)} %bitcast.29, bf16[4,768,768]{2,1,0:T(8,128)(2,1)} %wide_grads.1.refs_0_, bf16[192,1024]{1,0:T(8,128)(2,1)} %copy-done.19, ...), custom_call_target="tpu_custom_call", output_to_operand_aliasing={{1}: (2, {})} | custom-call | flops 1811939328 | bytes 6291456 | tf_op jit(solution)/shard_map/tall_grads/pallas_call | solution.py:749
  225.0 58.7 %all_to_all.30.refs_0_ = bf16[4,768,768]{2,1,0:T(8,128)(2,1)} all-to-all(bf16[4,768,768]{2,1,0:T(8,128)(2,1)} %get-tuple-element.173), channel_id=1, replica_groups=mesh['seq'=4,'fsdp'=8] {'seq'}, dimensions={0} | all-to-all | bytes 9437184 | tf_op jit(solution)/shard_map/all_to_all | solution.py:961
  283.7 5.3 %all-to-all-start.3 = ((bf16[8,144,768]{2,1,0:T(8,128)(2,1)}), bf16[8,144,768]{2,1,0:T(8,128)(2,1)S(1)}, u32[]{:S(2)}, u32[]{:S(2)}) async-start(bf16[8,144,768]{2,1,0:T(8,128)(2,1)} %bitcast.12), calls=%async_computation.3 | async-start | bytes 3538944 | tf_op jit(solution)/shard_map/all_to_all | solution.py:954
  289.0 42.7 %attend_back.3 = (bf16[192,1024]{1,0:T(8,128)(2,1)}, bf16[192,1024]{1,0:T(8,128)(2,1)}, bf16[192,1024]{1,0:T(8,128)(2,1)}, bf16[192,1024]{1,0:T(8,128)(2,1)}, bf16[768,512]{1,0:T(8,128)(2,1)}) custom-call(bf16[3,4096,128]{2,1,0:T(8,128)(2,1)} %get-tuple-element.145.v_ref, bf16[3,64,4096]{2,1,0:T(8,128)(2,1)} %copy-done.3, ...), custom_call_target="tpu_custom_call" | custom-call | flops 25769803776 | bytes 33554432 | tf_op jit(solution)/shard_map/attend_back/pallas_call | solution.py:313
  331.8 1.4 collective-permute-start.19
  333.3 1.6 collective-permute-start.21
  334.9 4.3 add_up.3.refs_14_
  339.2 6.0 %all-to-all-start.2 = ((bf16[8,96,768]{2,1,0:T(8,128)(2,1)}), bf16[8,96,768]{2,1,0:T(8,128)(2,1)S(1)}, u32[]{:S(2)}, u32[]{:S(2)}) async-start(bf16[8,96,768]{2,1,0:T(8,128)(2,1)} %bitcast.25), calls=%async_computation.2 | async-start | bytes 2359296 | tf_op jit(solution)/shard_map/all_to_all | solution.py:954
  345.2 42.7 %attend_back.4 = (bf16[192,1024]{1,0:T(8,128)(2,1)}, bf16[192,1024]{1,0:T(8,128)(2,1)}, bf16[192,1024]{1,0:T(8,128)(2,1)}, bf16[192,1024]{1,0:T(8,128)(2,1)}, bf16[768,512]{1,0:T(8,128)(2,1)}) custom-call(bf16[3,4096,128]{2,1,0:T(8,128)(2,1)} %get-tuple-element.145.v_ref, bf16[3,64,4096]{2,1,0:T(8,128)(2,1)} %copy-done.3, ...), custom_call_target="tpu_custom_call", output_to_operand_aliasing={{4}: (16, {})} | custom-call | flops 25769803776 | bytes 33554432 | tf_op jit(solution)/shard_map/attend_back/pallas_call | solution.py:313
  388.6 6.0 %all-to-all-start.4 = ((bf16[8,96,512]{2,1,0:T(8,128)(2,1)}), bf16[8,96,512]{2,1,0:T(8,128)(2,1)S(1)}, u32[]{:S(2)}, u32[]{:S(2)}) async-start(bf16[8,96,512]{2,1,0:T(8,128)(2,1)} %bitcast.24), calls=%async_computation.4 | async-start | bytes 1572864 | tf_op jit(solution)/shard_map/all_to_all | solution.py:954
  394.6 1.9 collective-permute-start.24
  396.5 2.9 owned.1.refs_13_.refs_0_
  401.6 42.6 %attend_back.5 = (bf16[192,1024]{1,0:T(8,128)(2,1)}, bf16[192,1024]{1,0:T(8,128)(2,1)}, bf16[192,1024]{1,0:T(8,128)(2,1)}, bf16[192,1024]{1,0:T(8,128)(2,1)}, bf16[768,256]{1,0:T(8,128)(2,1)}) custom-call(bf16[3,4096,128]{2,1,0:T(8,128)(2,1)} %get-tuple-element.145.v_ref, bf16[3,64,4096]{2,1,0:T(8,128)(2,1)} %copy-done.3, ...), custom_call_target="tpu_custom_call" | custom-call | flops 25769803776 | bytes 33554432 | tf_op jit(solution)/shard_map/attend_back/pallas_call | solution.py:313
  445.7 2.5 pass_on.1
  448.2 6.0 %all-to-all-start.5 = ((bf16[8,96,256]{2,1,0:T(8,128)(2,1)}), bf16[8,96,256]{2,1,0:T(8,128)(2,1)S(1)}, u32[]{:S(2)}, u32[]{:S(2)}) async-start(bf16[8,96,256]{2,1,0:T(8,128)(2,1)} %bitcast.26), calls=%async_computation.5 | async-start | bytes 786432 | tf_op jit(solution)/shard_map/all_to_all | solution.py:954
  455.1 1.4 collective-permute-start.30
  456.5 1.9 add_up.4
  458.3 7.3 %all-to-all-done.5.refs_0_ = bf16[8,96,256]{2,1,0:T(8,128)(2,1)S(1)} async-done(((bf16[8,96,256]{2,1,0:T(8,128)(2,1)}), bf16[8,96,256]{2,1,0:T(8,128)(2,1)S(1)}, u32[]{:S(2)}, u32[]{:S(2)}) %all-to-all-start.5) | async-done | bytes 393248 | tf_op jit(solution)/shard_map/all_to_all | solution.py:954
  466.4 1.7 add_up.5
  471.6 9.7 %last.2.base_ref = f32[1024,768]{1,0:T(8,128)} custom-call(bf16[1024,768]{1,0:T(8,128)(2,1)} %bitcast.1.x_ref, f32[1024,768]{1,0:T(8,128)} %get-tuple-element.144.base_ref, bf16[768,640]{1,0:T(8,128)(2,1)} %hold.2.gain_ref.refs_8_.refs_12_.refs_16_.refs_20_.refs_4_, bf16[192,1024]{1,0:T(8,128)(2,1)} %get-tuple-element.163.refs_0_, ...), custom_call_target="tpu_custom_call" | custom-call | flops 2415919104 | bytes 12582912 | tf_op jit(solution)/shard_map/last/pallas_call | solution.py:602
  481.4 2.8 finish_wide.1
  485.1 7.7 %last.3 = f32[1024,768]{1,0:T(8,128)} custom-call(bf16[1024,768]{1,0:T(8,128)(2,1)} %bitcast.1.x_ref, f32[1024,768]{1,0:T(8,128)} %last.2.base_ref, bf16[768,640]{1,0:T(8,128)(2,1)} %hold.2.gain_ref.refs_8_.refs_12_.refs_16_.refs_20_.refs_4_, bf16[192,1024]{1,0:T(8,128)(2,1)} %get-tuple-element.190.refs_0_, bf16[192,1024]{1,0:T(8,128)(2,1)} %copy-done.22, ...), custom_call_target="tpu_custom_call" | custom-call | flops 1207959552 | bytes 12582912 | tf_op jit(solution)/shard_map/last/pallas_call | solution.py:602
  494.2 2.4 finish_qkv.1
  (157 shorter events, 30.6 us)
Async XLA Ops:
  9.3 29.6 %all-to-all-start = ((bf16[8,96,640]{2,1,0:T(8,128)(2,1)}), bf16[8,96,640]{2,1,0:T(8,128)(2,1)S(1)}, u32[]{:S(2)}, u32[]{:S(2)}) async-start(bf16[8,96,640]{2,1,0:T(8,128)(2,1)} %own_columns.1), calls=%async_computation | async-start | bytes 1966080 | tf_op jit(solution)/shard_map/all_to_all | solution.py:902
  15.7 112.0 %all-gather.2.cloned.1.call-start = ((), (), s32[]{:S(2)}) async-start(), calls=%async_computation.6 | async-start | bytes 3981312 | tf_op jit(solution)/shard_map/all_gather | solution.py:893
  15.7 35.3 %collective-permute-start = (bf16[1024,768]{1,0:T(8,128)(2,1)}, bf16[1024,768]{1,0:T(8,128)(2,1)}, u32[]{:S(2)}, u32[]{:S(2)}) collective-permute-start(bf16[1024,768]{1,0:T(8,128)(2,1)} %bitcast.1.x_ref), channel_id=1, source_target_pairs={{0,16},{8,24},{16,0},{24,8},{1,17},{9,25},{17,1},{25,9},{2,18},{10... | collective-permute-start | bytes 4718600 | tf_op jit(solution)/shard_map/ppermute | solution.py:887
  42.2 25.4 %collective-permute-start.2 = (bf16[1024,768]{1,0:T(8,128)(2,1)}, bf16[1024,768]{1,0:T(8,128)(2,1)S(1)}, u32[]{:S(2)}, u32[]{:S(2)}) collective-permute-start(bf16[1024,768]{1,0:T(8,128)(2,1)} %bitcast.1.x_ref), channel_id=1, source_target_pairs={{0,8},{8,0},{16,24},{24,16},{1,9},{9,1},{17,25},{25,17},{2,10},{10... | collective-permute-start | bytes 4718600 | tf_op jit(solution)/shard_map/ppermute | solution.py:887
  51.1 22.7 %collective-permute-start.1 = (bf16[1024,768]{1,0:T(8,128)(2,1)}, bf16[1024,768]{1,0:T(8,128)(2,1)S(1)}, u32[]{:S(2)}, u32[]{:S(2)}) collective-permute-start(bf16[1024,768]{1,0:T(8,128)(2,1)} %collective-permute-done.x_ref), channel_id=1, source_target_pairs={{0,8},{8,0},{16,24},{24,16},{1,9},{9,1},{17,25},{25,17},{2,10},{10... | collective-permute-start | bytes 4718600 | tf_op jit(solution)/shard_map/ppermute | solution.py:887
  81.7 23.7 %collective-permute-start.4 = (bf16[768,640]{1,0:T(8,128)(2,1)}, bf16[768,640]{1,0:T(8,128)(2,1)S(1)}, u32[]{:S(2)}, u32[]{:S(2)}) collective-permute-start(bf16[768,640]{1,0:T(8,128)(2,1)} %hold.2.gain_ref.refs_8_.refs_12_.refs_16_.refs_20_.refs_4_), channel_id=1, source_target_pairs={{0,16},{8,24},{16,0},{24,8},{1,17},{9,25},{17,1},{25,9},{2,18},{10... | collective-permute-start | bytes 2949128 | tf_op jit(solution)/shard_map/ppermute | solution.py:887
  83.0 22.4 %collective-permute-start.3 = (bf16[768,640]{1,0:T(8,128)(2,1)}, bf16[768,640]{1,0:T(8,128)(2,1)S(1)}, u32[]{:S(2)}, u32[]{:S(2)}) collective-permute-start(bf16[768,640]{1,0:T(8,128)(2,1)} %hold.2.gain_ref.refs_8_.refs_12_.refs_16_.refs_20_.refs_4_), channel_id=1, source_target_pairs={{0,8},{8,0},{16,24},{24,16},{1,9},{9,1},{17,25},{25,17},{2,10},{10... | collective-permute-start | bytes 2949128 | tf_op jit(solution)/shard_map/ppermute | solution.py:887
  127.7 8.3 %copy-start.35 = (bf16[64,1024]{1,0:T(8,128)(2,1)S(1)}, bf16[64,1024]{1,0:T(8,128)(2,1)}, u32[]{:S(2)}) copy-start(bf16[64,1024]{1,0:T(8,128)(2,1)} %get-tuple-element.136) | copy-start | bytes 393220
  127.7 8.6 %copy-start.33 = (bf16[64,1024]{1,0:T(8,128)(2,1)S(1)}, bf16[64,1024]{1,0:T(8,128)(2,1)}, u32[]{:S(2)}) copy-start(bf16[64,1024]{1,0:T(8,128)(2,1)} %get-tuple-element.137) | copy-start | bytes 393220
  127.8 10.0 %copy-start.31 = (bf16[64,1024]{1,0:T(8,128)(2,1)S(1)}, bf16[64,1024]{1,0:T(8,128)(2,1)}, u32[]{:S(2)}) copy-start(bf16[64,1024]{1,0:T(8,128)(2,1)} %get-tuple-element.138) | copy-start | bytes 393220
  127.8 41.9 %collective-permute-start.5 = (bf16[768,2304]{1,0:T(8,128)(2,1)}, bf16[768,2304]{1,0:T(8,128)(2,1)}, u32[]{:S(2)}, u32[]{:S(2)}) collective-permute-start(bf16[768,2304]{1,0:T(8,128)(2,1)} %hold.3.mine_ref), channel_id=1, source_target_pairs={{0,8},{8,0},{16,24},{24,16},{1,9},{9,1},{17,25},{25,17},{2,10},{10... | collective-permute-start | bytes 10616840 | tf_op jit(solution)/shard_map/ppermute | solution.py:887
  128.9 9.8 %collective-permute-start.12 = (bf16[768,640]{1,0:T(8,128)(2,1)S(1)}, bf16[768,640]{1,0:T(8,128)(2,1)S(1)}, u32[]{:S(2)}, u32[]{:S(2)}) collective-permute-start(bf16[768,640]{1,0:T(8,128)(2,1)S(1)} %copy-done.5), channel_id=1, source_target_pairs={{0,8},{8,0},{16,24},{24,16},{1,9},{9,1},{17,25},{25,17},{2,10},{10... | collective-permute-start | bytes 2949128 | tf_op jit(solution)/shard_map/ppermute | solution.py:887
  129.6 6.4 %collective-permute-start.6 = (bf16[64,1024]{1,0:T(8,128)(2,1)S(1)}, bf16[64,1024]{1,0:T(8,128)(2,1)S(1)}, u32[]{:S(2)}, u32[]{:S(2)}) collective-permute-start(bf16[64,1024]{1,0:T(8,128)(2,1)S(1)} %copy-done.40), channel_id=1, source_target_pairs={{0,8},{8,0},{16,24},{24,16},{1,9},{9,1},{17,25},{25,17},{2,10},{10... | collective-permute-start | bytes 393224 | tf_op jit(solution)/shard_map/ppermute | solution.py:887
  129.6 6.8 %collective-permute-start.7 = (bf16[64,1024]{1,0:T(8,128)(2,1)S(1)}, bf16[64,1024]{1,0:T(8,128)(2,1)S(1)}, u32[]{:S(2)}, u32[]{:S(2)}) collective-permute-start(bf16[64,1024]{1,0:T(8,128)(2,1)S(1)} %copy-done.38), channel_id=1, source_target_pairs={{0,16},{8,24},{16,0},{24,8},{1,17},{9,25},{17,1},{25,9},{2,18},{10... | collective-permute-start | bytes 393224 | tf_op jit(solution)/shard_map/ppermute | solution.py:887
  130.9 6.8 %collective-permute-start.8 = (bf16[64,1024]{1,0:T(8,128)(2,1)S(1)}, bf16[64,1024]{1,0:T(8,128)(2,1)S(1)}, u32[]{:S(2)}, u32[]{:S(2)}) collective-permute-start(bf16[64,1024]{1,0:T(8,128)(2,1)S(1)} %copy-done.37), channel_id=1, source_target_pairs={{0,24},{8,16},{16,8},{24,0},{1,25},{9,17},{17,9},{25,1},{2,26},{10... | collective-permute-start | bytes 393224 | tf_op jit(solution)/shard_map/ppermute | solution.py:887
  136.0 25.5 %collective-permute-start.9 = (bf16[64,1024]{1,0:T(8,128)(2,1)S(1)}, bf16[64,1024]{1,0:T(8,128)(2,1)S(1)}, u32[]{:S(2)}, u32[]{:S(2)}) collective-permute-start(bf16[64,1024]{1,0:T(8,128)(2,1)S(1)} %copy-done.35), channel_id=1, source_target_pairs={{0,8},{8,0},{16,24},{24,16},{1,9},{9,1},{17,25},{25,17},{2,10},{10... | collective-permute-start | bytes 393224 | tf_op jit(solution)/shard_map/ppermute | solution.py:887
  136.4 25.4 %collective-permute-start.10 = (bf16[64,1024]{1,0:T(8,128)(2,1)S(1)}, bf16[64,1024]{1,0:T(8,128)(2,1)S(1)}, u32[]{:S(2)}, u32[]{:S(2)}) collective-permute-start(bf16[64,1024]{1,0:T(8,128)(2,1)S(1)} %copy-done.33), channel_id=1, source_target_pairs={{0,16},{8,24},{16,0},{24,8},{1,17},{9,25},{17,1},{25,9},{2,18},{10... | collective-permute-start | bytes 393224 | tf_op jit(solution)/shard_map/ppermute | solution.py:887
  137.7 25.5 %collective-permute-start.11 = (bf16[64,1024]{1,0:T(8,128)(2,1)S(1)}, bf16[64,1024]{1,0:T(8,128)(2,1)S(1)}, u32[]{:S(2)}, u32[]{:S(2)}) collective-permute-start(bf16[64,1024]{1,0:T(8,128)(2,1)S(1)} %copy-done.31), channel_id=1, source_target_pairs={{0,24},{8,16},{16,8},{24,0},{1,25},{9,17},{17,9},{25,1},{2,26},{10... | collective-permute-start | bytes 393224 | tf_op jit(solution)/shard_map/ppermute | solution.py:887
  160.7 2.5 collective-permute-start.13
  161.4 8.3 %copy-start.32 = (bf16[64,1024]{1,0:T(8,128)(2,1)}, bf16[64,1024]{1,0:T(8,128)(2,1)S(1)}, u32[]{:S(2)}) copy-start(bf16[64,1024]{1,0:T(8,128)(2,1)S(1)} %collective-permute-done.9.refs_5_) | copy-start | bytes 393220
  161.4 5.3 %collective-permute-start.14 = (bf16[64,1024]{1,0:T(8,128)(2,1)}, bf16[64,1024]{1,0:T(8,128)(2,1)S(1)}, u32[]{:S(2)}, u32[]{:S(2)}) collective-permute-start(bf16[64,1024]{1,0:T(8,128)(2,1)} %get-tuple-element.141), channel_id=1, source_target_pairs={{0,16},{8,24},{16,0},{24,8},{1,17},{9,25},{17,1},{25,9},{2,18},{10... | collective-permute-start | bytes 393224 | tf_op jit(solution)/shard_map/ppermute | solution.py:887
  161.8 7.9 %collective-permute-start.15 = (bf16[64,1024]{1,0:T(8,128)(2,1)}, bf16[64,1024]{1,0:T(8,128)(2,1)S(1)}, u32[]{:S(2)}, u32[]{:S(2)}) collective-permute-start(bf16[64,1024]{1,0:T(8,128)(2,1)} %get-tuple-element.142), channel_id=1, source_target_pairs={{0,24},{8,16},{16,8},{24,0},{1,25},{9,17},{17,9},{25,1},{2,26},{10... | collective-permute-start | bytes 393224 | tf_op jit(solution)/shard_map/ppermute | solution.py:887
  199.0 12.4 %collective-permute-start.16 = (bf16[192,1024]{1,0:T(8,128)(2,1)}, bf16[192,1024]{1,0:T(8,128)(2,1)S(1)}, u32[]{:S(2)}, u32[]{:S(2)}) collective-permute-start(bf16[192,1024]{1,0:T(8,128)(2,1)} %get-tuple-element.154), channel_id=1, source_target_pairs={{0,8},{8,0},{16,24},{24,16},{1,9},{9,1},{17,25},{25,17},{2,10},{10... | collective-permute-start | bytes 1179656 | tf_op jit(solution)/shard_map/ppermute | solution.py:887
  199.2 12.1 %collective-permute-start.17 = (bf16[192,1024]{1,0:T(8,128)(2,1)}, bf16[192,1024]{1,0:T(8,128)(2,1)S(1)}, u32[]{:S(2)}, u32[]{:S(2)}) collective-permute-start(bf16[192,1024]{1,0:T(8,128)(2,1)} %get-tuple-element.155), channel_id=1, source_target_pairs={{0,16},{8,24},{16,0},{24,8},{1,17},{9,25},{17,1},{25,9},{2,18},{10... | collective-permute-start | bytes 1179656 | tf_op jit(solution)/shard_map/ppermute | solution.py:887
  199.5 19.3 %collective-permute-start.18 = (bf16[192,1024]{1,0:T(8,128)(2,1)}, bf16[192,1024]{1,0:T(8,128)(2,1)S(1)}, u32[]{:S(2)}, u32[]{:S(2)}) collective-permute-start(bf16[192,1024]{1,0:T(8,128)(2,1)} %get-tuple-element.156), channel_id=1, source_target_pairs={{0,24},{8,16},{16,8},{24,0},{1,25},{9,17},{17,9},{25,1},{2,26},{10... | collective-permute-start | bytes 1179656 | tf_op jit(solution)/shard_map/ppermute | solution.py:887
  283.7 55.5 %all-to-all-start.3 = ((bf16[8,144,768]{2,1,0:T(8,128)(2,1)}), bf16[8,144,768]{2,1,0:T(8,128)(2,1)S(1)}, u32[]{:S(2)}, u32[]{:S(2)}) async-start(bf16[8,144,768]{2,1,0:T(8,128)(2,1)} %bitcast.12), calls=%async_computation.3 | async-start | bytes 3538944 | tf_op jit(solution)/shard_map/all_to_all | solution.py:954
  331.8 62.8 %collective-permute-start.19 = (bf16[192,1024]{1,0:T(8,128)(2,1)}, bf16[192,1024]{1,0:T(8,128)(2,1)S(1)}, u32[]{:S(2)}, u32[]{:S(2)}) collective-permute-start(bf16[192,1024]{1,0:T(8,128)(2,1)} %get-tuple-element.164), channel_id=1, source_target_pairs={{0,8},{8,0},{16,24},{24,16},{1,9},{9,1},{17,25},{25,17},{2,10},{10... | collective-permute-start | bytes 1179656 | tf_op jit(solution)/shard_map/ppermute | solution.py:887
  333.2 63.4 %collective-permute-start.20 = (bf16[192,1024]{1,0:T(8,128)(2,1)}, bf16[192,1024]{1,0:T(8,128)(2,1)}, u32[]{:S(2)}, u32[]{:S(2)}) collective-permute-start(bf16[192,1024]{1,0:T(8,128)(2,1)} %get-tuple-element.165), channel_id=1, source_target_pairs={{0,16},{8,24},{16,0},{24,8},{1,17},{9,25},{17,1},{25,9},{2,18},{10... | collective-permute-start | bytes 1179656 | tf_op jit(solution)/shard_map/ppermute | solution.py:887
  333.3 63.2 %collective-permute-start.21 = (bf16[192,1024]{1,0:T(8,128)(2,1)}, bf16[192,1024]{1,0:T(8,128)(2,1)}, u32[]{:S(2)}, u32[]{:S(2)}) collective-permute-start(bf16[192,1024]{1,0:T(8,128)(2,1)} %get-tuple-element.166), channel_id=1, source_target_pairs={{0,24},{8,16},{16,8},{24,0},{1,25},{9,17},{17,9},{25,1},{2,26},{10... | collective-permute-start | bytes 1179656 | tf_op jit(solution)/shard_map/ppermute | solution.py:887
  339.2 48.7 %copy-start.8 = (bf16[8,144,768]{2,1,0:T(8,128)(2,1)}, bf16[8,144,768]{2,1,0:T(8,128)(2,1)S(1)}, u32[]{:S(2)}) copy-start(bf16[8,144,768]{2,1,0:T(8,128)(2,1)S(1)} %all-to-all-done.3.tall_ref) | copy-start | bytes 5308420
  339.2 49.4 %all-to-all-start.2 = ((bf16[8,96,768]{2,1,0:T(8,128)(2,1)}), bf16[8,96,768]{2,1,0:T(8,128)(2,1)S(1)}, u32[]{:S(2)}, u32[]{:S(2)}) async-start(bf16[8,96,768]{2,1,0:T(8,128)(2,1)} %bitcast.25), calls=%async_computation.2 | async-start | bytes 2359296 | tf_op jit(solution)/shard_map/all_to_all | solution.py:954
  387.9 12.8 %collective-permute-start.22 = (bf16[192,1024]{1,0:T(8,128)(2,1)}, bf16[192,1024]{1,0:T(8,128)(2,1)S(1)}, u32[]{:S(2)}, u32[]{:S(2)}) collective-permute-start(bf16[192,1024]{1,0:T(8,128)(2,1)} %get-tuple-element.175), channel_id=1, source_target_pairs={{0,8},{8,0},{16,24},{24,16},{1,9},{9,1},{17,25},{25,17},{2,10},{10... | collective-permute-start | bytes 1179656 | tf_op jit(solution)/shard_map/ppermute | solution.py:887
  388.4 55.9 %collective-permute-start.23 = (bf16[192,1024]{1,0:T(8,128)(2,1)}, bf16[192,1024]{1,0:T(8,128)(2,1)S(1)}, u32[]{:S(2)}, u32[]{:S(2)}) collective-permute-start(bf16[192,1024]{1,0:T(8,128)(2,1)} %get-tuple-element.176), channel_id=1, source_target_pairs={{0,16},{8,24},{16,0},{24,8},{1,17},{9,25},{17,1},{25,9},{2,18},{10... | collective-permute-start | bytes 1179656 | tf_op jit(solution)/shard_map/ppermute | solution.py:887
  388.6 55.8 %all-to-all-start.4 = ((bf16[8,96,512]{2,1,0:T(8,128)(2,1)}), bf16[8,96,512]{2,1,0:T(8,128)(2,1)S(1)}, u32[]{:S(2)}, u32[]{:S(2)}) async-start(bf16[8,96,512]{2,1,0:T(8,128)(2,1)} %bitcast.24), calls=%async_computation.4 | async-start | bytes 1572864 | tf_op jit(solution)/shard_map/all_to_all | solution.py:954
  394.6 49.7 %collective-permute-start.24 = (bf16[192,1024]{1,0:T(8,128)(2,1)}, bf16[192,1024]{1,0:T(8,128)(2,1)}, u32[]{:S(2)}, u32[]{:S(2)}) collective-permute-start(bf16[192,1024]{1,0:T(8,128)(2,1)} %get-tuple-element.177), channel_id=1, source_target_pairs={{0,24},{8,16},{16,8},{24,0},{1,25},{9,17},{17,9},{25,1},{2,26},{10... | collective-permute-start | bytes 1179656 | tf_op jit(solution)/shard_map/ppermute | solution.py:887
  399.5 44.9 %collective-permute-start.27 = (bf16[240,768]{1,0:T(8,128)(2,1)}, bf16[240,768]{1,0:T(8,128)(2,1)S(1)}, u32[]{:S(2)}, u32[]{:S(2)}) collective-permute-start(bf16[240,768]{1,0:T(8,128)(2,1)} %owned.1.refs_13_.refs_0_), channel_id=1, source_target_pairs={{0,24},{8,16},{16,8},{24,0},{1,25},{9,17},{17,9},{25,1},{2,26},{10... | collective-permute-start | bytes 1105928 | tf_op jit(solution)/shard_map/ppermute | solution.py:887
  400.1 44.2 %collective-permute-start.26 = (bf16[240,768]{1,0:T(8,128)(2,1)}, bf16[240,768]{1,0:T(8,128)(2,1)S(1)}, u32[]{:S(2)}, u32[]{:S(2)}) collective-permute-start(bf16[240,768]{1,0:T(8,128)(2,1)} %owned.1.refs_13_.refs_0_), channel_id=1, source_target_pairs={{0,16},{8,24},{16,0},{24,8},{1,17},{9,25},{17,1},{25,9},{2,18},{10... | collective-permute-start | bytes 1105928 | tf_op jit(solution)/shard_map/ppermute | solution.py:887
  400.7 43.6 %copy-start.13 = (bf16[192,1024]{1,0:T(8,128)(2,1)}, bf16[192,1024]{1,0:T(8,128)(2,1)S(1)}, u32[]{:S(2)}) copy-start(bf16[192,1024]{1,0:T(8,128)(2,1)S(1)} %collective-permute-done.22.refs_4_.refs_5_) | copy-start | bytes 1179652
  400.7 43.7 %collective-permute-start.25 = (bf16[240,768]{1,0:T(8,128)(2,1)}, bf16[240,768]{1,0:T(8,128)(2,1)S(1)}, u32[]{:S(2)}, u32[]{:S(2)}) collective-permute-start(bf16[240,768]{1,0:T(8,128)(2,1)} %owned.1.refs_13_.refs_0_), channel_id=1, source_target_pairs={{0,8},{8,0},{16,24},{24,16},{1,9},{9,1},{17,25},{25,17},{2,10},{10... | collective-permute-start | bytes 1105928 | tf_op jit(solution)/shard_map/ppermute | solution.py:887
  448.2 17.4 %all-to-all-start.5 = ((bf16[8,96,256]{2,1,0:T(8,128)(2,1)}), bf16[8,96,256]{2,1,0:T(8,128)(2,1)S(1)}, u32[]{:S(2)}, u32[]{:S(2)}) async-start(bf16[8,96,256]{2,1,0:T(8,128)(2,1)} %bitcast.26), calls=%async_computation.5 | async-start | bytes 786432 | tf_op jit(solution)/shard_map/all_to_all | solution.py:954
  454.3 17.4 %collective-permute-start.28 = (bf16[192,1024]{1,0:T(8,128)(2,1)}, bf16[192,1024]{1,0:T(8,128)(2,1)S(1)}, u32[]{:S(2)}, u32[]{:S(2)}) collective-permute-start(bf16[192,1024]{1,0:T(8,128)(2,1)} %get-tuple-element.191), channel_id=1, source_target_pairs={{0,8},{8,0},{16,24},{24,16},{1,9},{9,1},{17,25},{25,17},{2,10},{10... | collective-permute-start | bytes 1179656 | tf_op jit(solution)/shard_map/ppermute | solution.py:887
  454.7 29.5 %collective-permute-start.29 = (bf16[192,1024]{1,0:T(8,128)(2,1)}, bf16[192,1024]{1,0:T(8,128)(2,1)S(1)}, u32[]{:S(2)}, u32[]{:S(2)}) collective-permute-start(bf16[192,1024]{1,0:T(8,128)(2,1)} %get-tuple-element.192), channel_id=1, source_target_pairs={{0,16},{8,24},{16,0},{24,8},{1,17},{9,25},{17,1},{25,9},{2,18},{10... | collective-permute-start | bytes 1179656 | tf_op jit(solution)/shard_map/ppermute | solution.py:887
  455.1 29.1 %collective-permute-start.30 = (bf16[192,1024]{1,0:T(8,128)(2,1)}, bf16[192,1024]{1,0:T(8,128)(2,1)S(1)}, u32[]{:S(2)}, u32[]{:S(2)}) collective-permute-start(bf16[192,1024]{1,0:T(8,128)(2,1)} %get-tuple-element.193), channel_id=1, source_target_pairs={{0,24},{8,16},{16,8},{24,0},{1,25},{9,17},{17,9},{25,1},{2,26},{10... | collective-permute-start | bytes 1179656 | tf_op jit(solution)/shard_map/ppermute | solution.py:887
  469.0 12.4 %copy-start.18 = (bf16[96,768]{1,0:T(8,128)(2,1)}, bf16[96,768]{1,0:T(8,128)(2,1)S(1)}, u32[]{:S(2)}) copy-start(bf16[96,768]{1,0:T(8,128)(2,1)S(1)} %pad_maximum_fusion.refs_0_) | copy-start | bytes 442372
  469.0 23.8 %collective-permute-start.33 = (bf16[96,768]{1,0:T(8,128)(2,1)S(1)}, bf16[96,768]{1,0:T(8,128)(2,1)S(1)}, u32[]{:S(2)}, u32[]{:S(2)}) collective-permute-start(bf16[96,768]{1,0:T(8,128)(2,1)S(1)} %pad_maximum_fusion.refs_0_), channel_id=1, source_target_pairs={{0,24},{8,16},{16,8},{24,0},{1,25},{9,17},{17,9},{25,1},{2,26},{10... | collective-permute-start | bytes 442376 | tf_op jit(solution)/shard_map/ppermute | solution.py:887
  470.3 22.6 %collective-permute-start.32 = (bf16[96,768]{1,0:T(8,128)(2,1)S(1)}, bf16[96,768]{1,0:T(8,128)(2,1)S(1)}, u32[]{:S(2)}, u32[]{:S(2)}) collective-permute-start(bf16[96,768]{1,0:T(8,128)(2,1)S(1)} %pad_maximum_fusion.refs_0_), channel_id=1, source_target_pairs={{0,16},{8,24},{16,0},{24,8},{1,17},{9,25},{17,1},{25,9},{2,18},{10... | collective-permute-start | bytes 442376 | tf_op jit(solution)/shard_map/ppermute | solution.py:887
  471.6 9.7 %copy-start.22 = (bf16[192,1024]{1,0:T(8,128)(2,1)}, bf16[192,1024]{1,0:T(8,128)(2,1)S(1)}, u32[]{:S(2)}) copy-start(bf16[192,1024]{1,0:T(8,128)(2,1)S(1)} %collective-permute-done.28.refs_1_) | copy-start | bytes 1179652
  471.6 21.2 %collective-permute-start.31 = (bf16[96,768]{1,0:T(8,128)(2,1)S(1)}, bf16[96,768]{1,0:T(8,128)(2,1)S(1)}, u32[]{:S(2)}, u32[]{:S(2)}) collective-permute-start(bf16[96,768]{1,0:T(8,128)(2,1)S(1)} %pad_maximum_fusion.refs_0_), channel_id=1, source_target_pairs={{0,8},{8,0},{16,24},{24,16},{1,9},{9,1},{17,25},{25,17},{2,10},{10... | collective-permute-start | bytes 442376 | tf_op jit(solution)/shard_map/ppermute | solution.py:887
  (35 other events, 82.4 us)
Sparse Core Ops, SparseCore 0:
  42.3 64.4 all-gather.1
where the time goes:
time: 508 us; the launch traced here: 504 us
  Pallas kernels  305 us (60%)
  starting transfers between devices  60 us (12%)
  blocking collectives  58.7 us (12%)
  waiting for transfers between devices  48.3 us (10%)
  between operations  15.7 us (3%)
  local copies, waits for them, and re-layouts  12.3 us (2%)
    pallas_call x3, Pallas kernels, attend_back(): pl.pallas_call(functools.partial(attend_back_kernel, kc, groups), grid=(g...  128 us
    pallas_call x3, Pallas kernels, attend(): pl.pallas_call(functools.partial(attend_kernel, kc, groups, len(after)),...  62.4 us
    all_to_all x1, blocking collectives, body(): lax.all_to_all(wide_grad, 'seq', split_axis=0, concat_axis=0, tiled=True)  58.7 us
    ppermute x34, starting transfers between devices, swap(): return lax.ppermute(array, axis, [(i, i ^ j) for i in range(size)])  30.2 us
    pallas_call x1, Pallas kernels, middle(): pl.pallas_call(functools.partial(middle_kernel, groups, heads, ff, shards...  28.6 us
    ppermute x34, waiting for transfers between devices, swap(): return lax.ppermute(array, axis, [(i, i ^ j) for i in range(size)])  26.7 us
    pallas_call x4, Pallas kernels, qkv_call(): pl.pallas_call(functools.partial(qkv_kernel, heads), grid=(steps,), out_s...  24.9 us
    all_to_all x4, starting transfers between devices, to_owner(): lax.all_to_all(parts, 'fsdp', split_axis=0, concat_axis=0, tiled=True)  23.3 us
  transfers between devices with their start and end apart: 40, of which 8 were waited for; matrix products, arithmetic and copies ran while one was open for 1% of the time, Pallas kernels for 52%

commit v1 on v0

--- a/solution.py
+++ b/solution.py
@@ -263,16 +263,16 @@
         high = delta.astype(bf).astype(f32)
         tail = jnp.where(r == 0, high, jnp.where(r == 1, delta - high, 0.0)).astype(bf)
         doe = jnp.concatenate([dop, tail, jnp.zeros((128 - HD - 16, bq), bf)], axis=0)
-        right_v = jnp.concatenate([dop, zero], axis=0)
-        right_k = jnp.concatenate([zero, q_ref[0, :HD, at]], axis=0)
-        sides.append((p_ref, doe, right_v, right_k))
+        right_v = jnp.concatenate([dop, zero], axis=0).T
+        right_k = jnp.concatenate([zero, q_ref[0, :HD, at]], axis=0).T
+        sides.append((p_ref, doe, jnp.concatenate([right_v, right_k], axis=0)))
     dq = [jnp.zeros((HD, bq), f32), jnp.zeros((HD, bq), f32)]
-    for n, (p_ref, doe, right_v, right_k) in enumerate(sides):
+    for n, (p_ref, doe, right) in enumerate(sides):
         for c in range(rows // kc):
             at = slice(c * kc, (c + 1) * kc)
             p = p_ref[0, at, :]
             ds = p * dg(v_ref[0, at, :], doe, NN).astype(bf)
-            acc_ref[at, :] = acc_ref[at, :] + dg(p, right_v, NT) + dg(ds, right_k, NT)
+            acc_ref[at, :] = acc_ref[at, :] + dg(jnp.concatenate([p, ds], axis=1), right, NN)
             dq[n] = dq[n] + dg(kt_ref[0, :, at], ds, NN)
     dq = jnp.concatenate(dq, axis=1) * HD**-0.5
     turned = jnp.concatenate([dq[HD // 2 :], -dq[: HD // 2]], axis=0)
@@ -301,7 +301,7 @@
         grad_ref[:, 3 * HD :] = jnp.zeros((D, HD), bf)
 
 
-def attend_back(h, v, kt, qt, do, kept, cos, sin, normed, groups, place, after, kc=512):
+def attend_back(h, v, kt, qt, do, kept, cos, sin, normed, groups, place, after, kc=256):
     S = v.shape[1]
     width = S // groups
     bq = width // 2
@@ -626,24 +626,6 @@
     )(x, base, peers[0], *chunks, *(list(peers) * (2 * len(chosen))), *after)
 
 
-def pass_on(arrays, after):
-    vmem = pl.BlockSpec(memory_space=pltpu.VMEM)
-    count = len(arrays)
-
-    def kernel(*refs):
-        for source, target in zip(refs[:count], refs[-count:]):
-            target[...] = source[...]
-
-    return pl.pallas_call(
-        kernel,
-        out_shape=tuple(jax.ShapeDtypeStruct(a.shape, a.dtype) for a in arrays),
-        in_specs=[vmem] * count + [pl.BlockSpec(memory_space=pl.ANY)] * len(after),
-        out_specs=(vmem,) * count,
-        compiler_params=pltpu.CompilerParams(vmem_limit_bytes=58 * 2**20),
-        name="pass_on",
-    )(*arrays, *after)
-
-
 def own_kernel(groups, heads, info_ref, w_ref, gain_ref, out_ref):
     for g in range(groups):
 
@@ -703,102 +685,149 @@
     )(cosine, sine)
 
 
-def wide_kernel(second_ref, dgu_ref, mixed_ref, branch_ref, out_ref):
-    g = pl.program_id(0)
+def wide_kernel(place_ref, second_ref, dgu_ref, mixed_ref, branch_ref, *refs):
+    outs, held_ref = refs[:-1], refs[-1]
+    i = pl.program_id(0)
+    group = i ^ place_ref[0]
     end = pl.num_programs(0) - 1
 
-    @pl.when(g < end)
-    def _():
-        out_ref[0] = dg(second_ref[...], dgu_ref[...], TN).astype(bf)
-
-    @pl.when(g == end)
-    def _():
-        out_ref[0] = dg(mixed_ref[...], branch_ref[...], NN).astype(bf)
-
-
-def wide_grads(second, d_gate_up, mixed_t, branch):
+    @pl.when(group < end)
+    def _():
+        held_ref[...] = dg(second_ref[...], dgu_ref[...], TN).astype(bf)
+
+    @pl.when(group == end)
+    def _():
+        held_ref[...] = dg(mixed_ref[...], branch_ref[...], NN).astype(bf)
+
+    for j in range(len(outs)):
+
+        @pl.when(i == j)
+        def _():
+            outs[j][...] = held_ref[...]
+
+
+def wide_grads(place, second, d_gate_up, mixed_t, branch):
     rows = second.shape[0]
     steps = d_gate_up.shape[1] // D
-    whole = lambda i: (0, 0)
+    whole = lambda i, p: (0, 0)
     return pl.pallas_call(
         wide_kernel,
-        grid=(steps + 1,),
-        in_specs=[
-            pl.BlockSpec((rows, D), whole),
-            pl.BlockSpec((rows, D), lambda i: (0, jnp.minimum(i, steps - 1))),
-            pl.BlockSpec((D, rows), whole),
-            pl.BlockSpec((rows, D), whole),
-        ],
-        out_specs=pl.BlockSpec((1, D, D), lambda i: (i, 0, 0)),
-        out_shape=jax.ShapeDtypeStruct((steps + 1, D, D), bf),
+        grid_spec=pltpu.PrefetchScalarGridSpec(
+            num_scalar_prefetch=1,
+            grid=(steps + 1,),
+            in_specs=[
+                pl.BlockSpec((rows, D), whole),
+                pl.BlockSpec((rows, D), lambda i, p: (0, jnp.minimum(i ^ p[0], steps - 1))),
+                pl.BlockSpec((D, rows), whole),
+                pl.BlockSpec((rows, D), whole),
+            ],
+            out_specs=(pl.BlockSpec((D, D), whole),) * (steps + 1),
+            scratch_shapes=[pltpu.VMEM((D, D), bf)],
+        ),
+        out_shape=(jax.ShapeDtypeStruct((D, D), bf),) * (steps + 1),
         compiler_params=pltpu.CompilerParams(vmem_limit_bytes=58 * 2**20),
         cost_estimate=pl.CostEstimate(
             flops=2 * rows * D * D * (steps + 1), bytes_accessed=16 * 2**20, transcendentals=0
         ),
         name="wide_grads",
-    )(second, d_gate_up, mixed_t, branch)
-
-
-def tall_kernel(inner_ref, dy_ref, *refs):
-    refs[-2][...] = dg(inner_ref[...], dy_ref[...], TN).astype(bf)
+    )(place, second, d_gate_up, mixed_t, branch)
 
 
 def tall_grads(inner, dy, wide, after):
     rows, ff = inner.shape
     step = ff // 3
-    return pl.pallas_call(
-        tall_kernel,
+    many = len(wide)
+
+    def kernel(inner_ref, dy_ref, *refs):
+        refs[many + len(after)][...] = dg(inner_ref[...], dy_ref[...], TN).astype(bf)
+
+    anywhere = pl.BlockSpec(memory_space=pl.ANY)
+    outs = pl.pallas_call(
+        kernel,
         grid=(3,),
         in_specs=[
             pl.BlockSpec((rows, step), lambda i: (0, i)),
             pl.BlockSpec((rows, D), lambda i: (0, 0)),
         ]
-        + [pl.BlockSpec(memory_space=pl.ANY)] * (1 + len(after)),
-        out_specs=(
-            pl.BlockSpec((step, D), lambda i: (i, 0)),
-            pl.BlockSpec(memory_space=pl.ANY),
-        ),
-        out_shape=(
-            jax.ShapeDtypeStruct((ff, D), bf),
-            jax.ShapeDtypeStruct(wide.shape, bf),
-        ),
-        input_output_aliases={2: 1},
+        + [anywhere] * (many + len(after)),
+        out_specs=(pl.BlockSpec((step, D), lambda i: (i, 0)),) + (anywhere,) * many,
+        out_shape=(jax.ShapeDtypeStruct((ff, D), bf),)
+        + tuple(jax.ShapeDtypeStruct(w.shape, bf) for w in wide),
+        input_output_aliases={2 + n: 1 + n for n in range(many)},
         compiler_params=pltpu.CompilerParams(vmem_limit_bytes=58 * 2**20),
         cost_estimate=pl.CostEstimate(
             flops=2 * rows * D * ff, bytes_accessed=6 * 2**20, transcendentals=0
         ),
         name="tall_grads",
-    )(inner, dy, wide, *after)
-
-
-def add_kernel(count, *refs):
-    total = None
-    for ref in refs[:count]:
-        for j in range(ref.shape[0]):
-            term = ref[j].astype(f32)
-            total = term if total is None else total + term
-    out_ref = refs[-1]
-    out_ref[...] = total.astype(out_ref.dtype)
-
-
-def add_up(arrays, after, dtype=bf):
-    arrays = [a if a.ndim == 3 else a[None] for a in arrays]
-    rows, columns = arrays[0].shape[1:]
-    rb = 256 if rows % 256 == 0 else rows
-    return pl.pallas_call(
-        functools.partial(add_kernel, len(arrays)),
-        grid=(rows // rb,),
-        out_shape=jax.ShapeDtypeStruct((rows, columns), dtype),
-        in_specs=[pl.BlockSpec((n, rb, columns), lambda i: (0, i, 0)) for n in [a.shape[0] for a in arrays]]
-        + [pl.BlockSpec(memory_space=pl.ANY)] * len(after),
-        out_specs=pl.BlockSpec((rb, columns), lambda i: (i, 0)),
+    )(inner, dy, *wide, *after)
+    return outs[0], list(outs[1:])
+
+
+def ordered(kernel, arrays, after, carry, out_shape, in_specs, out_specs, name, grid=()):
+    first = len(arrays) + len(after)
+    own = len(out_shape)
+    anywhere = pl.BlockSpec(memory_space=pl.ANY)
+
+    def call(*refs):
+        outs = refs[first + len(carry) :]
+        kernel(*refs[: len(arrays)], *outs[:own])
+
+    outs = pl.pallas_call(
+        call,
+        grid=grid,
+        out_shape=tuple(out_shape) + tuple(jax.ShapeDtypeStruct(a.shape, a.dtype) for a in carry),
+        in_specs=list(in_specs) + [anywhere] * (len(after) + len(carry)),
+        out_specs=tuple(out_specs) + (anywhere,) * len(carry),
+        input_output_aliases={first + n: own + n for n in range(len(carry))},
         compiler_params=pltpu.CompilerParams(vmem_limit_bytes=58 * 2**20),
-        name="add_up",
-    )(*arrays, *after)
+        name=name,
+    )(*arrays, *after, *carry)
+    return list(outs[:own]), list(outs[own:])
+
+
+def add_kernel(*refs):
+    total = refs[0][...].astype(f32)
+    for ref in refs[1:-1]:
+        total = total + ref[...].astype(f32)
+    refs[-1][...] = total.astype(bf)
+
+
+def add_up(arrays, after, carry):
+    rows, columns = arrays[0].shape
+    rb = 256
+    spec = pl.BlockSpec((rb, columns), lambda i: (i, 0))
+    (total,), carried = ordered(
+        add_kernel, arrays, after, carry, [jax.ShapeDtypeStruct((rows, columns), bf)],
+        [spec] * len(arrays), [spec], "add_up", grid=(rows // rb,),
+    )
+    return total, carried
 
 
 def up16(n):
     return -(-n // 16) * 16
+
+
+def beside_kernel(first_ref, second_ref, *refs):
+    out_ref = refs[-1]
+    start = 0
+    for ref in (first_ref, second_ref):
+        total = ref[0].astype(f32)
+        for f in range(1, ref.shape[0]):
+            total = total + ref[f].astype(f32)
+        out_ref[:, start : start + ref.shape[2]] = total.astype(bf)
+        start += ref.shape[2]
+
+
+def beside(first, second, after):
+    vmem = pl.BlockSpec(memory_space=pltpu.VMEM)
+    return pl.pallas_call(
+        beside_kernel,
+        out_shape=jax.ShapeDtypeStruct((first.shape[1], first.shape[2] + second.shape[2]), bf),
+        in_specs=[vmem, vmem] + [pl.BlockSpec(memory_space=pl.ANY)] * len(after),
+        out_specs=vmem,
+        compiler_params=pltpu.CompilerParams(vmem_limit_bytes=58 * 2**20),
+        name="beside",
+    )(first, second, *after)
 
 
 def owned_kernel(wide_ref, tall_ref, *refs):
@@ -812,16 +841,14 @@
         start += up16(ref.shape[1])
 
 
-def owned(wide, tall, after):
+def owned(wide, tall, after, carry):
     vmem = pl.BlockSpec(memory_space=pltpu.VMEM)
-    return pl.pallas_call(
-        owned_kernel,
-        out_shape=jax.ShapeDtypeStruct((up16(wide.shape[1]) + up16(tall.shape[1]), D), bf),
-        in_specs=[vmem, vmem] + [pl.BlockSpec(memory_space=pl.ANY)] * len(after),
-        out_specs=vmem,
-        compiler_params=pltpu.CompilerParams(vmem_limit_bytes=58 * 2**20),
-        name="owned",
-    )(wide, tall, *after)
+    shape = (up16(wide.shape[1]) + up16(tall.shape[1]), D)
+    (total,), carried = ordered(
+        owned_kernel, [wide, tall], after, carry, [jax.ShapeDtypeStruct(shape, bf)],
+        [vmem] * 2, [vmem], "owned",
+    )
+    return total, carried
 
 
 def finish_wide_kernel(groups, info_ref, w_ref, gain_ref, *refs):
@@ -859,17 +886,24 @@
     dgain_ref[...] = row_of(total / column(gain_ref))
 
 
-def finish(kernel, groups, info, w, gain, parts, shapes, name):
+def finish(kernel, groups, info, w, gain, parts, shapes, name, after=()):
     vmem = pl.BlockSpec(memory_space=pltpu.VMEM)
+    first = 3 + groups
+
+    def call(*refs):
+        kernel(*refs[:first], *refs[first + len(after) :])
+
     return pl.pallas_call(
-        kernel,
+        call,
         out_shape=tuple(jax.ShapeDtypeStruct(shape, f32) for shape in shapes),
-        in_specs=[pl.BlockSpec(memory_space=pltpu.SMEM)] + [vmem] * (2 + groups),
+        in_specs=[pl.BlockSpec(memory_space=pltpu.SMEM)]
+        + [vmem] * (2 + groups)
+        + [pl.BlockSpec(memory_space=pl.ANY)] * len(after),
         out_specs=(vmem,) * len(shapes),
         scratch_shapes=[pltpu.VMEM((groups,) + parts[0].shape, bf)],
         compiler_params=pltpu.CompilerParams(vmem_limit_bytes=58 * 2**20),
         name=name,
-    )(info, w, gain, *parts)
+    )(info, w, gain, *parts, *after)
 
 
 def body(
@@ -956,9 +990,9 @@
     def from_peers(array):
         return [array] + [swap(array, j) for j in range(1, groups)]
 
-    wide_grad = wide_grads(second, d_gate_up, mixed_t, branch)
-    tall_grad, wide_grad = tall_grads(inner, dy, wide_grad, d_mixed[1:])
-    wide_sent = lax.all_to_all(wide_grad, "seq", split_axis=0, concat_axis=0, tiled=True)
+    wide_own, *wide_rest = wide_grads(place, second, d_gate_up, mixed_t, branch)
+    tall_grad, wide_rest = tall_grads(inner, dy, wide_rest, d_mixed[1:])
+    wide_all = exchange([wide_own] + wide_rest)
     tall_parts = to_owner(tall_grad)
 
     def back(h, grad_place, after):
@@ -967,38 +1001,40 @@
         )
 
     sent_0, qkv_first = back(0, (512, 0, None), [tall_grad])
-    wide_sum = add_up([wide_sent], [qkv_first])
+    wide_sum, others = add_up(wide_all, [qkv_first, tall_parts], sent_0[1:])
     wide_parts = to_owner(wide_sum)
-    received_0 = exchange(sent_0)
+    received_0 = exchange(sent_0[:1] + others)
 
     sent_1, qkv_first = back(1, (512, 1, qkv_first), [wide_sum])
-    both = owned(wide_parts, tall_parts, [qkv_first] + received_0[1:])
-    both_peers = from_peers(both)
-    received_1 = exchange(sent_1)
-    qkv_parts = to_owner(qkv_first)
+    both, carried = owned(wide_parts, tall_parts, received_0[1:], sent_1[1:] + [qkv_first])
+    received_1 = exchange(sent_1[:1] + carried[:-1])
+    both_far = [swap(both, j) for j in range(2, groups)]
+    qkv_parts = to_owner(carried[-1])
 
     sent_2, qkv_second = back(2, (256, 0, None), [both])
-    *others, qkv_second = pass_on(sent_2[1:] + [qkv_second], received_1[1:] + both_peers[1:] + [qkv_parts])
-    sent_2 = sent_2[:1] + others
-    received_2 = exchange(sent_2)
+    _, carried = ordered(
+        lambda: None, [], received_1[1:] + both_far + [qkv_parts],
+        sent_2[1:] + [qkv_second, both], [], [], [], "pass_on",
+    )
+    qkv_second, both = carried[-2:]
+    received_2 = exchange(sent_2[:1] + carried[:-2])
+    both_peers = [both, swap(both, 1)] + both_far
     qkv_second_parts = to_owner(qkv_second)
 
     base = last(
         groups, heads, (0, 1), x0, d_hidden, peers, received_0 + received_1, [qkv_second]
     )
-    first_sum = add_up([qkv_parts], [qkv_second])
     in_weight_grad, proj_weight_grad, ffn_gain_grad, out_weight_grad = finish(
         functools.partial(finish_wide_kernel, groups),
         groups, place, in_weight, ffn_row, both_peers,
         ((shard, 2 * ff), (shard, D), (1, shard), (tall, D)), "finish_wide",
     )
-    second_sum = add_up([qkv_second_parts], [])
-    qkv_peers = from_peers(jnp.concatenate([first_sum, second_sum], axis=1))
+    qkv_peers = from_peers(beside(qkv_parts, qkv_second_parts, [base] + received_2[1:]))
     tokens_grad = last(groups, heads, (2,), x0, base, peers, received_2, [])
     qkv_weight_grad, attn_gain_grad = finish(
         functools.partial(finish_qkv_kernel, groups, heads),
         groups, place, qkv_weight, attn_row, qkv_peers,
-        ((shard, 3 * D), (1, shard)), "finish_qkv",
+        ((shard, 3 * D), (1, shard)), "finish_qkv", [tokens_grad],
     )
     return (
         result[None],

time: 508 us -> 450 us (0.89)
  blocking collectives: 58.7 us -> 0 us
  Pallas kernels: 305 us -> 291 us
  waiting for transfers between devices: 48.3 us -> 59 us
    all_to_all x1 -> x0, blocking collectives: 58.7 us -> none  [body(): lax.all_to_all(wide_grad, 'seq', split_axis=0, concat_axis=0, tiled=True)]
    ppermute x34 -> x37, waiting for transfers between devices: 26.7 us -> 44.6 us  [swap(): return lax.ppermute(array, axis, [(i, i ^ j) for i in range(size)])]
    pallas_call x3, Pallas kernels: 128 us -> 117 us  [attend_back(): pl.pallas_call(functools.partial(attend_back_kernel, kc, groups), grid=(g...]
    all_to_all x4, waiting for transfers between devices: 7.28 us -> 0.01 us  [to_owner(): lax.all_to_all(parts, 'fsdp', split_axis=0, concat_axis=0, tiled=True)]
    unnamed x86 -> x100, local copies, waits for them, and re-layouts: 12.3 us -> 16.6 us
    pallas_call x9 -> x8, Pallas kernels: 34.2 us -> 31.3 us  [the longest x1 11.3 us: wide_grads(): pl.pallas_call(wide_kernel, grid_spec=pltpu.PrefetchScalarGridSpec(num_sc...]
    ppermute x34 -> x37, starting transfers between devices: 30.2 us -> 30.7 us  [swap(): return lax.ppermute(array, axis, [(i, i ^ j) for i in range(size)])]
  transfers between devices with their start and end apart: 40 -> 43, of which waited for: 8 -> 9; matrix products, arithmetic and copies ran while one was open for 1% -> 1% of each run, Pallas kernels for 52% -> 55%
where the time goes in v1:
time: 450 us; the launch traced here: 446 us
  Pallas kernels  291 us (65%)
  starting transfers between devices  60.6 us (13%)
  waiting for transfers between devices  59 us (13%)
  local copies, waits for them, and re-layouts  16.6 us (4%)
  between operations  15.5 us (3%)
    pallas_call x3, Pallas kernels, attend_back(): pl.pallas_call(functools.partial(attend_back_kernel, kc, groups), grid=(g...  117 us
    pallas_call x3, Pallas kernels, attend(): pl.pallas_call(functools.partial(attend_kernel, kc, groups, len(after)),...  62.6 us
    ppermute x37, waiting for transfers between devices, swap(): return lax.ppermute(array, axis, [(i, i ^ j) for i in range(size)])  44.6 us
    ppermute x37, starting transfers between devices, swap(): return lax.ppermute(array, axis, [(i, i ^ j) for i in range(size)])  30.7 us
    pallas_call x1, Pallas kernels, middle(): pl.pallas_call(functools.partial(middle_kernel, groups, heads, ff, shards...  28.6 us
    pallas_call x4, Pallas kernels, qkv_call(): pl.pallas_call(functools.partial(qkv_kernel, heads), grid=(steps,), out_s...  25 us
    all_to_all x4, starting transfers between devices, to_owner(): lax.all_to_all(parts, 'fsdp', split_axis=0, concat_axis=0, tiled=True)  23.5 us
    pallas_call x2, Pallas kernels, last(): pl.pallas_call(functools.partial(last_kernel, groups, chosen), grid=(rows...  17.3 us
  transfers between devices with their start and end apart: 43, of which 9 were waited for; matrix products, arithmetic and copies ran while one was open for 1% of the time, Pallas kernels for 55%

profile of v1, /device:TPU:1, one launch (start us, length us, event | category | flops | bytes accessed | tf_op | source)
XLA Modules:
  0.0 446.0 jit_solution(16906137672868568111)
XLA Ops:
  7.2 2.2 own_columns.1
  9.3 6.4 %all-to-all-start = ((bf16[8,96,640]{2,1,0:T(8,128)(2,1)}), bf16[8,96,640]{2,1,0:T(8,128)(2,1)S(1)}, u32[]{:S(2)}, u32[]{:S(2)}) async-start(bf16[8,96,640]{2,1,0:T(8,128)(2,1)} %own_columns.1), calls=%async_computation | async-start | bytes 1966080 | tf_op jit(solution)/shard_map/all_to_all | solution.py:936
  17.1 2.8 multiply_sine_fusion
  19.9 4.7 %tables.1 = (f32[4096,128]{1,0:T(8,128)}, f32[4096,128]{1,0:T(8,128)}, f32[64,4096]{1,0:T(8,128)}, f32[64,4096]{1,0:T(8,128)}) custom-call(f32[32,4096]{1,0:T(8,128)} %get-tuple-element.233.cos_ref, f32[32,4096]{1,0:T(8,128)} %get-tuple-element.232.sin_ref), custom_call_target="tpu_custom_call" | custom-call | tf_op jit(solution)/shard_map/tables/pallas_call | solution.py:676
  24.6 14.3 %all-to-all-done = bf16[8,96,640]{2,1,0:T(8,128)(2,1)S(1)} async-done(((bf16[8,96,640]{2,1,0:T(8,128)(2,1)}), bf16[8,96,640]{2,1,0:T(8,128)(2,1)S(1)}, u32[]{:S(2)}, u32[]{:S(2)}) %all-to-all-start) | async-done | bytes 983072 | tf_op jit(solution)/shard_map/all_to_all | solution.py:936
  39.9 2.4 own_half.1
  42.3 2.0 collective-permute-start.2
  44.3 6.7 %collective-permute-done.x_ref = bf16[1024,768]{1,0:T(8,128)(2,1)} collective-permute-done((bf16[1024,768]{1,0:T(8,128)(2,1)}, bf16[1024,768]{1,0:T(8,128)(2,1)}, u32[]{:S(2)}, u32[]{:S(2)}) %collective-permute-start) | collective-permute-done | bytes 1572896 | tf_op jit(solution)/shard_map/ppermute | solution.py:921
  51.1 1.9 collective-permute-start.1
  55.0 6.3 %qkv.4 = (bf16[4096,768]{1,0:T(8,128)(2,1)}, bf16[3,4096,128]{2,1,0:T(8,128)(2,1)}, bf16[3,4096,128]{2,1,0:T(8,128)(2,1)}, bf16[3,128,4096]{2,1,0:T(8,128)(2,1)}...) custom-call(s32[2]{0:T(128)S(1)} %get-tuple-element.237.info_ref, ...), custom_call_target="tpu_custom_call" | custom-call | flops 2013265920 | bytes 8388608 | tf_op jit(solution)/shard_map/qkv/pallas_call | solution.py:107
  61.3 6.3 %qkv.5 = (bf16[4096,768]{1,0:T(8,128)(2,1)}, bf16[3,4096,128]{2,1,0:T(8,128)(2,1)}, bf16[3,4096,128]{2,1,0:T(8,128)(2,1)}, bf16[3,128,4096]{2,1,0:T(8,128)(2,1)}...) custom-call(s32[2]{0:T(128)S(1)} %get-tuple-element.236.info_ref, ...), custom_call_target="tpu_custom_call", output_to_operand_aliasing={{0}: (5, {}), {1}: (6, {}), {2}: (7, {}), {3}: (8, {}), {4}... | custom-call | flops 2013265920 | bytes 8388608 | tf_op jit(solution)/shard_map/qkv/pallas_call | solution.py:107
  67.7 6.1 %qkv.6 = (bf16[4096,768]{1,0:T(8,128)(2,1)}, bf16[3,4096,128]{2,1,0:T(8,128)(2,1)}, bf16[3,4096,128]{2,1,0:T(8,128)(2,1)}, bf16[3,128,4096]{2,1,0:T(8,128)(2,1)}...) custom-call(s32[2]{0:T(128)S(1)} %pad_add_fusion.1.info_ref, ...), custom_call_target="tpu_custom_call", output_to_operand_aliasing={{0}: (5, {}), {1}: (6, {}), {2}: (7, {}), {3}: (8, {}), {4}... | custom-call | flops 2013265920 | bytes 8388608 | tf_op jit(solution)/shard_map/qkv/pallas_call | solution.py:107
  73.7 6.2 %qkv.7 = (bf16[4096,768]{1,0:T(8,128)(2,1)}, bf16[3,4096,128]{2,1,0:T(8,128)(2,1)}, bf16[3,4096,128]{2,1,0:T(8,128)(2,1)}, bf16[3,128,4096]{2,1,0:T(8,128)(2,1)}...) custom-call(s32[2]{0:T(128)S(1)} %pad_add_fusion.info_ref, ...), custom_call_target="tpu_custom_call", output_to_operand_aliasing={{0}: (5, {}), {1}: (6, {}), {2}: (7, {}), {3}: (8, {}), {4}... | custom-call | flops 2013265920 | bytes 8388608 | tf_op jit(solution)/shard_map/qkv/pallas_call | solution.py:107
  83.1 20.5 %attend.3 = (bf16[4,4096,512]{2,1,0:T(8,128)(2,1)}, bf16[4,4096,512]{2,1,0:T(8,128)(2,1)}, f32[64,2048]{1,0:T(8,128)}, f32[64,2048]{1,0:T(8,128)}, f32[4,1,512]{...) custom-call(bf16[3,4096,128]{2,1,0:T(8,128)(2,1)} %get-tuple-element, ...), custom_call_target="tpu_custom_call" | custom-call | flops 17179869184 | bytes 33554432 | tf_op jit(solution)/shard_map/attend/pallas_call | solution.py:197
  103.7 1.7 collective-permute-done.4.refs_1_.refs_10_.refs_14_.refs_18_.refs_22_.refs_6_
  106.7 21.0 %attend.4 = (bf16[4,4096,512]{2,1,0:T(8,128)(2,1)}, bf16[4,4096,512]{2,1,0:T(8,128)(2,1)}, f32[64,2048]{1,0:T(8,128)}, f32[64,2048]{1,0:T(8,128)}, f32[4,1,512]{...) custom-call(bf16[3,4096,128]{2,1,0:T(8,128)(2,1)} %get-tuple-element, ...), custom_call_target="tpu_custom_call" | custom-call | flops 17179869184 | bytes 33554432 | tf_op jit(solution)/shard_map/attend/pallas_call | solution.py:197
  131.8 4.2 collective-permute-done.6.refs_2_.refs_1_
  139.7 21.1 %attend.5 = (bf16[4,4096,512]{2,1,0:T(8,128)(2,1)}, bf16[4,4096,512]{2,1,0:T(8,128)(2,1)}, f32[64,2048]{1,0:T(8,128)}, f32[64,2048]{1,0:T(8,128)}, f32[4,1,512]{...) custom-call(bf16[3,4096,128]{2,1,0:T(8,128)(2,1)} %get-tuple-element, ...), custom_call_target="tpu_custom_call" | custom-call | flops 17179869184 | bytes 33554432 | tf_op jit(solution)/shard_map/attend/pallas_call | solution.py:197
  161.9 1.4 collective-permute-start.15
  163.3 3.5 collective-permute-done.14.refs_10_
  166.8 3.0 collective-permute-done.15.refs_11_
  170.5 28.6 %middle.1 = (bf16[192,1024]{1,0:T(8,128)(2,1)}, bf16[192,1024]{1,0:T(8,128)(2,1)}, bf16[192,1024]{1,0:T(8,128)(2,1)}, bf16[192,1024]{1,0:T(8,128)(2,1)}, bf16[10...) custom-call(s32[1]{0:T(128)} %bitcast.info_ref.place_ref.refs_0_, ...), custom_call_target="tpu_custom_call" | custom-call | flops 15099494400 | bytes 31457280 | tf_op jit(solution)/shard_map/middle/pallas_call | solution.py:514
  199.6 1.8 collective-permute-start.18
  201.3 11.3 %wide_grads.1 = (bf16[768,768]{1,0:T(8,128)(2,1)}, bf16[768,768]{1,0:T(8,128)(2,1)}, bf16[768,768]{1,0:T(8,128)(2,1)}, bf16[768,768]{1,0:T(8,128)(2,1)}) custom-call(s32[1]{0:T(128)} %bitcast.info_ref.place_ref.refs_0_, bf16[1024,768]{1,0:T(8,128)(2,1)} %get-tuple-element.174.second_ref, bf16[1024,2304]{1,0:T(8,128)(2,1)} %get-tuple-element.175.dgu_ref, ...), custom_call_target="tpu_custom_call" | custom-call | flops 4831838208 | bytes 16777216 | tf_op jit(solution)/shard_map/wide_grads/pallas_call | solution.py:713
  212.7 6.2 %collective-permute-done.18.refs_5_.refs_12_ = bf16[192,1024]{1,0:T(8,128)(2,1)S(1)} collective-permute-done((bf16[192,1024]{1,0:T(8,128)(2,1)}, bf16[192,1024]{1,0:T(8,128)(2,1)S(1)}, u32[]{:S(2)}, u32[]{:S(2)}) %collective-permute-start.18) | collective-permute-done | bytes 393248 | tf_op jit(solution)/shard_map/ppermute | solution.py:921
  219.6 5.5 %tall_grads.1 = (bf16[1152,768]{1,0:T(8,128)(2,1)}, bf16[768,768]{1,0:T(8,128)(2,1)}, bf16[768,768]{1,0:T(8,128)(2,1)}, bf16[768,768]{1,0:T(8,128)(2,1)}) custom-call(bf16[1024,1152]{1,0:T(8,128)(2,1)} %get-tuple-element.173.inner_ref, bf16[1024,768]{1,0:T(8,128)(2,1)} %bitcast.29, ...), custom_call_target="tpu_custom_call", output_to_operand_aliasing={{1}: (2, {}), {2}: (3, {}), {3}: (4, {})} | custom-call | flops 1811939328 | bytes 6291456 | tf_op jit(solution)/shard_map/tall_grads/pallas_call | solution.py:745
  225.1 5.4 %all-to-all-start.1 = ((bf16[8,144,768]{2,1,0:T(8,128)(2,1)}), bf16[8,144,768]{2,1,0:T(8,128)(2,1)S(1)}, u32[]{:S(2)}, u32[]{:S(2)}) async-start(bf16[8,144,768]{2,1,0:T(8,128)(2,1)} %bitcast.27), calls=%async_computation.1 | async-start | bytes 3538944 | tf_op jit(solution)/shard_map/all_to_all | solution.py:988
  230.8 1.8 collective-permute-start.21
  232.6 39.1 %attend_back.3 = (bf16[192,1024]{1,0:T(8,128)(2,1)}, bf16[192,1024]{1,0:T(8,128)(2,1)}, bf16[192,1024]{1,0:T(8,128)(2,1)}, bf16[192,1024]{1,0:T(8,128)(2,1)}, bf16[768,512]{1,0:T(8,128)(2,1)}) custom-call(bf16[3,4096,128]{2,1,0:T(8,128)(2,1)} %get-tuple-element.161.v_ref, bf16[3,64,4096]{2,1,0:T(8,128)(2,1)} %copy-done.3, ...), custom_call_target="tpu_custom_call" | custom-call | flops 25769803776 | bytes 33554432 | tf_op jit(solution)/shard_map/attend_back/pallas_call | solution.py:313
  272.9 11.1 %collective-permute-done.21.refs_3_ = bf16[768,768]{1,0:T(8,128)(2,1)} collective-permute-done((bf16[768,768]{1,0:T(8,128)(2,1)}, bf16[768,768]{1,0:T(8,128)(2,1)}, u32[]{:S(2)}, u32[]{:S(2)}) %collective-permute-start.21) | collective-permute-done | bytes 1179680 | tf_op jit(solution)/shard_map/ppermute | solution.py:921
  285.2 4.2 add_up.1
  289.4 6.1 %all-to-all-start.2 = ((bf16[8,96,768]{2,1,0:T(8,128)(2,1)}), bf16[8,96,768]{2,1,0:T(8,128)(2,1)S(1)}, u32[]{:S(2)}, u32[]{:S(2)}) async-start(bf16[8,96,768]{2,1,0:T(8,128)(2,1)} %bitcast.30), calls=%async_computation.2 | async-start | bytes 2359296 | tf_op jit(solution)/shard_map/all_to_all | solution.py:988
  296.3 1.6 collective-permute-start.24
  297.9 38.9 %attend_back.4 = (bf16[192,1024]{1,0:T(8,128)(2,1)}, bf16[192,1024]{1,0:T(8,128)(2,1)}, bf16[192,1024]{1,0:T(8,128)(2,1)}, bf16[192,1024]{1,0:T(8,128)(2,1)}, bf16[768,512]{1,0:T(8,128)(2,1)}) custom-call(bf16[3,4096,128]{2,1,0:T(8,128)(2,1)} %get-tuple-element.161.v_ref, bf16[3,64,4096]{2,1,0:T(8,128)(2,1)} %copy-done.3, ...), custom_call_target="tpu_custom_call", output_to_operand_aliasing={{4}: (16, {})} | custom-call | flops 25769803776 | bytes 33554432 | tf_op jit(solution)/shard_map/attend_back/pallas_call | solution.py:313
  338.3 3.0 owned.1
  341.4 1.4 collective-permute-start.28
  342.8 6.1 %all-to-all-start.3 = ((bf16[8,96,512]{2,1,0:T(8,128)(2,1)}), bf16[8,96,512]{2,1,0:T(8,128)(2,1)S(1)}, u32[]{:S(2)}, u32[]{:S(2)}) async-start(bf16[8,96,512]{2,1,0:T(8,128)(2,1)} %bitcast.25), calls=%async_computation.3 | async-start | bytes 1572864 | tf_op jit(solution)/shard_map/all_to_all | solution.py:988
  350.0 1.6 collective-permute-start.27
  351.6 39.1 %attend_back.5 = (bf16[192,1024]{1,0:T(8,128)(2,1)}, bf16[192,1024]{1,0:T(8,128)(2,1)}, bf16[192,1024]{1,0:T(8,128)(2,1)}, bf16[192,1024]{1,0:T(8,128)(2,1)}, bf16[768,256]{1,0:T(8,128)(2,1)}) custom-call(bf16[3,4096,128]{2,1,0:T(8,128)(2,1)} %get-tuple-element.161.v_ref, bf16[3,64,4096]{2,1,0:T(8,128)(2,1)} %copy-done.3, ...), custom_call_target="tpu_custom_call" | custom-call | flops 25769803776 | bytes 33554432 | tf_op jit(solution)/shard_map/attend_back/pallas_call | solution.py:313
  392.3 5.9 %all-to-all-start.4 = ((bf16[8,96,256]{2,1,0:T(8,128)(2,1)}), bf16[8,96,256]{2,1,0:T(8,128)(2,1)S(1)}, u32[]{:S(2)}, u32[]{:S(2)}) async-start(bf16[8,96,256]{2,1,0:T(8,128)(2,1)} %bitcast.26), calls=%async_computation.4 | async-start | bytes 786432 | tf_op jit(solution)/shard_map/all_to_all | solution.py:988
  398.8 1.6 collective-permute-start.32
  400.6 9.6 %last.2.base_ref.refs_0_ = f32[1024,768]{1,0:T(8,128)} custom-call(bf16[1024,768]{1,0:T(8,128)(2,1)} %bitcast.1.x_ref, f32[1024,768]{1,0:T(8,128)} %get-tuple-element.160.base_ref, bf16[768,640]{1,0:T(8,128)(2,1)} %hold.2.gain_ref.refs_8_.refs_12_.refs_16_.refs_20_.refs_4_, bf16[192,1024]{1,0:T(8,128)(2,1)} %get-tuple-element.182.refs_0_, ...), custom_call_target="tpu_custom_call" | custom-call | flops 2415919104 | bytes 12582912 | tf_op jit(solution)/shard_map/last/pallas_call | solution.py:602
  410.3 8.0 %collective-permute-done.32.refs_3_ = bf16[192,1024]{1,0:T(8,128)(2,1)S(1)} collective-permute-done((bf16[192,1024]{1,0:T(8,128)(2,1)}, bf16[192,1024]{1,0:T(8,128)(2,1)S(1)}, u32[]{:S(2)}, u32[]{:S(2)}) %collective-permute-start.32) | collective-permute-done | bytes 393248 | tf_op jit(solution)/shard_map/ppermute | solution.py:921
  419.7 2.0 beside.1.refs_3_
  422.0 1.4 collective-permute-start.34
  424.6 2.8 finish_wide.1
  427.5 7.7 %last.3.refs_7_ = f32[1024,768]{1,0:T(8,128)} custom-call(bf16[1024,768]{1,0:T(8,128)(2,1)} %bitcast.1.x_ref, f32[1024,768]{1,0:T(8,128)} %last.2.base_ref.refs_0_, bf16[768,640]{1,0:T(8,128)(2,1)} %hold.2.gain_ref.refs_8_.refs_12_.refs_16_.refs_20_.refs_4_, bf16[192,1024]{1,0:T(8,128)(2,1)} %get-tuple-element.221.refs_0_, bf16[192,1024]{1,0:T(8,128)(2,1)} %copy-done.18, ...), custom_call_target="tpu_custom_call" | custom-call | flops 1207959552 | bytes 12582912 | tf_op jit(solution)/shard_map/last/pallas_call | solution.py:602
  436.6 2.4 finish_qkv.1
  (174 shorter events, 31.3 us)
Async XLA Ops:
  9.3 29.6 %all-to-all-start = ((bf16[8,96,640]{2,1,0:T(8,128)(2,1)}), bf16[8,96,640]{2,1,0:T(8,128)(2,1)S(1)}, u32[]{:S(2)}, u32[]{:S(2)}) async-start(bf16[8,96,640]{2,1,0:T(8,128)(2,1)} %own_columns.1), calls=%async_computation | async-start | bytes 1966080 | tf_op jit(solution)/shard_map/all_to_all | solution.py:936
  15.7 112.0 %all-gather.2.cloned.1.call-start = ((), (), s32[]{:S(2)}) async-start(), calls=%async_computation.5 | async-start | bytes 3981312 | tf_op jit(solution)/shard_map/all_gather | solution.py:927
  15.7 35.3 %collective-permute-start = (bf16[1024,768]{1,0:T(8,128)(2,1)}, bf16[1024,768]{1,0:T(8,128)(2,1)}, u32[]{:S(2)}, u32[]{:S(2)}) collective-permute-start(bf16[1024,768]{1,0:T(8,128)(2,1)} %bitcast.1.x_ref), channel_id=1, source_target_pairs={{0,16},{8,24},{16,0},{24,8},{1,17},{9,25},{17,1},{25,9},{2,18},{10... | collective-permute-start | bytes 4718600 | tf_op jit(solution)/shard_map/ppermute | solution.py:921
  42.3 25.3 %collective-permute-start.2 = (bf16[1024,768]{1,0:T(8,128)(2,1)}, bf16[1024,768]{1,0:T(8,128)(2,1)S(1)}, u32[]{:S(2)}, u32[]{:S(2)}) collective-permute-start(bf16[1024,768]{1,0:T(8,128)(2,1)} %bitcast.1.x_ref), channel_id=1, source_target_pairs={{0,8},{8,0},{16,24},{24,16},{1,9},{9,1},{17,25},{25,17},{2,10},{10... | collective-permute-start | bytes 4718600 | tf_op jit(solution)/shard_map/ppermute | solution.py:921
  51.1 22.7 %collective-permute-start.1 = (bf16[1024,768]{1,0:T(8,128)(2,1)}, bf16[1024,768]{1,0:T(8,128)(2,1)S(1)}, u32[]{:S(2)}, u32[]{:S(2)}) collective-permute-start(bf16[1024,768]{1,0:T(8,128)(2,1)} %collective-permute-done.x_ref), channel_id=1, source_target_pairs={{0,8},{8,0},{16,24},{24,16},{1,9},{9,1},{17,25},{25,17},{2,10},{10... | collective-permute-start | bytes 4718600 | tf_op jit(solution)/shard_map/ppermute | solution.py:921
  81.7 23.7 %collective-permute-start.4 = (bf16[768,640]{1,0:T(8,128)(2,1)}, bf16[768,640]{1,0:T(8,128)(2,1)S(1)}, u32[]{:S(2)}, u32[]{:S(2)}) collective-permute-start(bf16[768,640]{1,0:T(8,128)(2,1)} %hold.2.gain_ref.refs_8_.refs_12_.refs_16_.refs_20_.refs_4_), channel_id=1, source_target_pairs={{0,16},{8,24},{16,0},{24,8},{1,17},{9,25},{17,1},{25,9},{2,18},{10... | collective-permute-start | bytes 2949128 | tf_op jit(solution)/shard_map/ppermute | solution.py:921
  83.0 22.5 %collective-permute-start.3 = (bf16[768,640]{1,0:T(8,128)(2,1)}, bf16[768,640]{1,0:T(8,128)(2,1)S(1)}, u32[]{:S(2)}, u32[]{:S(2)}) collective-permute-start(bf16[768,640]{1,0:T(8,128)(2,1)} %hold.2.gain_ref.refs_8_.refs_12_.refs_16_.refs_20_.refs_4_), channel_id=1, source_target_pairs={{0,8},{8,0},{16,24},{24,16},{1,9},{9,1},{17,25},{25,17},{2,10},{10... | collective-permute-start | bytes 2949128 | tf_op jit(solution)/shard_map/ppermute | solution.py:921
  127.8 8.3 %copy-start.42 = (bf16[64,1024]{1,0:T(8,128)(2,1)S(1)}, bf16[64,1024]{1,0:T(8,128)(2,1)}, u32[]{:S(2)}) copy-start(bf16[64,1024]{1,0:T(8,128)(2,1)} %get-tuple-element.152) | copy-start | bytes 393220
  127.8 8.6 %copy-start.40 = (bf16[64,1024]{1,0:T(8,128)(2,1)S(1)}, bf16[64,1024]{1,0:T(8,128)(2,1)}, u32[]{:S(2)}) copy-start(bf16[64,1024]{1,0:T(8,128)(2,1)} %get-tuple-element.153) | copy-start | bytes 393220
  127.8 10.0 %copy-start.38 = (bf16[64,1024]{1,0:T(8,128)(2,1)S(1)}, bf16[64,1024]{1,0:T(8,128)(2,1)}, u32[]{:S(2)}) copy-start(bf16[64,1024]{1,0:T(8,128)(2,1)} %get-tuple-element.154) | copy-start | bytes 393220
  127.8 42.0 %collective-permute-start.5 = (bf16[768,2304]{1,0:T(8,128)(2,1)}, bf16[768,2304]{1,0:T(8,128)(2,1)}, u32[]{:S(2)}, u32[]{:S(2)}) collective-permute-start(bf16[768,2304]{1,0:T(8,128)(2,1)} %hold.3.mine_ref), channel_id=1, source_target_pairs={{0,8},{8,0},{16,24},{24,16},{1,9},{9,1},{17,25},{25,17},{2,10},{10... | collective-permute-start | bytes 10616840 | tf_op jit(solution)/shard_map/ppermute | solution.py:921
  128.9 9.7 %collective-permute-start.12 = (bf16[768,640]{1,0:T(8,128)(2,1)S(1)}, bf16[768,640]{1,0:T(8,128)(2,1)S(1)}, u32[]{:S(2)}, u32[]{:S(2)}) collective-permute-start(bf16[768,640]{1,0:T(8,128)(2,1)S(1)} %copy-done.5), channel_id=1, source_target_pairs={{0,8},{8,0},{16,24},{24,16},{1,9},{9,1},{17,25},{25,17},{2,10},{10... | collective-permute-start | bytes 2949128 | tf_op jit(solution)/shard_map/ppermute | solution.py:921
  129.6 6.4 %collective-permute-start.6 = (bf16[64,1024]{1,0:T(8,128)(2,1)S(1)}, bf16[64,1024]{1,0:T(8,128)(2,1)S(1)}, u32[]{:S(2)}, u32[]{:S(2)}) collective-permute-start(bf16[64,1024]{1,0:T(8,128)(2,1)S(1)} %copy-done.47), channel_id=1, source_target_pairs={{0,8},{8,0},{16,24},{24,16},{1,9},{9,1},{17,25},{25,17},{2,10},{10... | collective-permute-start | bytes 393224 | tf_op jit(solution)/shard_map/ppermute | solution.py:921
  129.7 6.8 %collective-permute-start.7 = (bf16[64,1024]{1,0:T(8,128)(2,1)S(1)}, bf16[64,1024]{1,0:T(8,128)(2,1)S(1)}, u32[]{:S(2)}, u32[]{:S(2)}) collective-permute-start(bf16[64,1024]{1,0:T(8,128)(2,1)S(1)} %copy-done.45), channel_id=1, source_target_pairs={{0,16},{8,24},{16,0},{24,8},{1,17},{9,25},{17,1},{25,9},{2,18},{10... | collective-permute-start | bytes 393224 | tf_op jit(solution)/shard_map/ppermute | solution.py:921
  131.0 6.8 %collective-permute-start.8 = (bf16[64,1024]{1,0:T(8,128)(2,1)S(1)}, bf16[64,1024]{1,0:T(8,128)(2,1)S(1)}, u32[]{:S(2)}, u32[]{:S(2)}) collective-permute-start(bf16[64,1024]{1,0:T(8,128)(2,1)S(1)} %copy-done.44), channel_id=1, source_target_pairs={{0,24},{8,16},{16,8},{24,0},{1,25},{9,17},{17,9},{25,1},{2,26},{10... | collective-permute-start | bytes 393224 | tf_op jit(solution)/shard_map/ppermute | solution.py:921
  136.0 25.5 %collective-permute-start.9 = (bf16[64,1024]{1,0:T(8,128)(2,1)S(1)}, bf16[64,1024]{1,0:T(8,128)(2,1)S(1)}, u32[]{:S(2)}, u32[]{:S(2)}) collective-permute-start(bf16[64,1024]{1,0:T(8,128)(2,1)S(1)} %copy-done.42), channel_id=1, source_target_pairs={{0,8},{8,0},{16,24},{24,16},{1,9},{9,1},{17,25},{25,17},{2,10},{10... | collective-permute-start | bytes 393224 | tf_op jit(solution)/shard_map/ppermute | solution.py:921
  136.4 25.5 %collective-permute-start.10 = (bf16[64,1024]{1,0:T(8,128)(2,1)S(1)}, bf16[64,1024]{1,0:T(8,128)(2,1)S(1)}, u32[]{:S(2)}, u32[]{:S(2)}) collective-permute-start(bf16[64,1024]{1,0:T(8,128)(2,1)S(1)} %copy-done.40), channel_id=1, source_target_pairs={{0,16},{8,24},{16,0},{24,8},{1,17},{9,25},{17,1},{25,9},{2,18},{10... | collective-permute-start | bytes 393224 | tf_op jit(solution)/shard_map/ppermute | solution.py:921
  137.8 25.6 %collective-permute-start.11 = (bf16[64,1024]{1,0:T(8,128)(2,1)S(1)}, bf16[64,1024]{1,0:T(8,128)(2,1)S(1)}, u32[]{:S(2)}, u32[]{:S(2)}) collective-permute-start(bf16[64,1024]{1,0:T(8,128)(2,1)S(1)} %copy-done.38), channel_id=1, source_target_pairs={{0,24},{8,16},{16,8},{24,0},{1,25},{9,17},{17,9},{25,1},{2,26},{10... | collective-permute-start | bytes 393224 | tf_op jit(solution)/shard_map/ppermute | solution.py:921
  160.8 2.5 collective-permute-start.13
  161.6 8.3 %copy-start.39 = (bf16[64,1024]{1,0:T(8,128)(2,1)}, bf16[64,1024]{1,0:T(8,128)(2,1)S(1)}, u32[]{:S(2)}) copy-start(bf16[64,1024]{1,0:T(8,128)(2,1)S(1)} %collective-permute-done.9.refs_5_) | copy-start | bytes 393220
  161.6 5.3 %collective-permute-start.14 = (bf16[64,1024]{1,0:T(8,128)(2,1)}, bf16[64,1024]{1,0:T(8,128)(2,1)S(1)}, u32[]{:S(2)}, u32[]{:S(2)}) collective-permute-start(bf16[64,1024]{1,0:T(8,128)(2,1)} %get-tuple-element.157), channel_id=1, source_target_pairs={{0,16},{8,24},{16,0},{24,8},{1,17},{9,25},{17,1},{25,9},{2,18},{10... | collective-permute-start | bytes 393224 | tf_op jit(solution)/shard_map/ppermute | solution.py:921
  161.9 7.9 %collective-permute-start.15 = (bf16[64,1024]{1,0:T(8,128)(2,1)}, bf16[64,1024]{1,0:T(8,128)(2,1)S(1)}, u32[]{:S(2)}, u32[]{:S(2)}) collective-permute-start(bf16[64,1024]{1,0:T(8,128)(2,1)} %get-tuple-element.158), channel_id=1, source_target_pairs={{0,24},{8,16},{16,8},{24,0},{1,25},{9,17},{17,9},{25,1},{2,26},{10... | collective-permute-start | bytes 393224 | tf_op jit(solution)/shard_map/ppermute | solution.py:921
  199.1 13.5 %collective-permute-start.16 = (bf16[192,1024]{1,0:T(8,128)(2,1)}, bf16[192,1024]{1,0:T(8,128)(2,1)S(1)}, u32[]{:S(2)}, u32[]{:S(2)}) collective-permute-start(bf16[192,1024]{1,0:T(8,128)(2,1)} %get-tuple-element.170), channel_id=1, source_target_pairs={{0,8},{8,0},{16,24},{24,16},{1,9},{9,1},{17,25},{25,17},{2,10},{10... | collective-permute-start | bytes 1179656 | tf_op jit(solution)/shard_map/ppermute | solution.py:921
  199.4 13.3 %collective-permute-start.17 = (bf16[192,1024]{1,0:T(8,128)(2,1)}, bf16[192,1024]{1,0:T(8,128)(2,1)S(1)}, u32[]{:S(2)}, u32[]{:S(2)}) collective-permute-start(bf16[192,1024]{1,0:T(8,128)(2,1)} %get-tuple-element.171), channel_id=1, source_target_pairs={{0,16},{8,24},{16,0},{24,8},{1,17},{9,25},{17,1},{25,9},{2,18},{10... | collective-permute-start | bytes 1179656 | tf_op jit(solution)/shard_map/ppermute | solution.py:921
  199.6 19.3 %collective-permute-start.18 = (bf16[192,1024]{1,0:T(8,128)(2,1)}, bf16[192,1024]{1,0:T(8,128)(2,1)S(1)}, u32[]{:S(2)}, u32[]{:S(2)}) collective-permute-start(bf16[192,1024]{1,0:T(8,128)(2,1)} %get-tuple-element.172), channel_id=1, source_target_pairs={{0,24},{8,16},{16,8},{24,0},{1,25},{9,17},{17,9},{25,1},{2,26},{10... | collective-permute-start | bytes 1179656 | tf_op jit(solution)/shard_map/ppermute | solution.py:921
  225.1 58.9 %all-to-all-start.1 = ((bf16[8,144,768]{2,1,0:T(8,128)(2,1)}), bf16[8,144,768]{2,1,0:T(8,128)(2,1)S(1)}, u32[]{:S(2)}, u32[]{:S(2)}) async-start(bf16[8,144,768]{2,1,0:T(8,128)(2,1)} %bitcast.27), calls=%async_computation.1 | async-start | bytes 3538944 | tf_op jit(solution)/shard_map/all_to_all | solution.py:988
  230.5 41.3 %collective-permute-start.19 = (bf16[768,768]{1,0:T(8,128)(2,1)}, bf16[768,768]{1,0:T(8,128)(2,1)S(1)}, u32[]{:S(2)}, u32[]{:S(2)}) collective-permute-start(bf16[768,768]{1,0:T(8,128)(2,1)} %get-tuple-element.184), channel_id=1, source_target_pairs={{0,8},{8,0},{16,24},{24,16},{1,9},{9,1},{17,25},{25,17},{2,10},{10... | collective-permute-start | bytes 3538952 | tf_op jit(solution)/shard_map/ppermute | solution.py:921
  230.7 41.1 %collective-permute-start.20 = (bf16[768,768]{1,0:T(8,128)(2,1)}, bf16[768,768]{1,0:T(8,128)(2,1)S(1)}, u32[]{:S(2)}, u32[]{:S(2)}) collective-permute-start(bf16[768,768]{1,0:T(8,128)(2,1)} %get-tuple-element.185), channel_id=1, source_target_pairs={{0,16},{8,24},{16,0},{24,8},{1,17},{9,25},{17,1},{25,9},{2,18},{10... | collective-permute-start | bytes 3538952 | tf_op jit(solution)/shard_map/ppermute | solution.py:921
  230.8 53.2 %collective-permute-start.21 = (bf16[768,768]{1,0:T(8,128)(2,1)}, bf16[768,768]{1,0:T(8,128)(2,1)}, u32[]{:S(2)}, u32[]{:S(2)}) collective-permute-start(bf16[768,768]{1,0:T(8,128)(2,1)} %get-tuple-element.186), channel_id=1, source_target_pairs={{0,24},{8,16},{16,8},{24,0},{1,25},{9,17},{17,9},{25,1},{2,26},{10... | collective-permute-start | bytes 3538952 | tf_op jit(solution)/shard_map/ppermute | solution.py:921
  271.8 12.2 %copy-start.23 = (bf16[768,768]{1,0:T(8,128)(2,1)}, bf16[768,768]{1,0:T(8,128)(2,1)S(1)}, u32[]{:S(2)}) copy-start(bf16[768,768]{1,0:T(8,128)(2,1)S(1)} %collective-permute-done.19.refs_1_) | copy-start | bytes 3538948
  289.4 47.5 %all-to-all-start.2 = ((bf16[8,96,768]{2,1,0:T(8,128)(2,1)}), bf16[8,96,768]{2,1,0:T(8,128)(2,1)S(1)}, u32[]{:S(2)}, u32[]{:S(2)}) async-start(bf16[8,96,768]{2,1,0:T(8,128)(2,1)} %bitcast.30), calls=%async_computation.2 | async-start | bytes 2359296 | tf_op jit(solution)/shard_map/all_to_all | solution.py:988
  295.6 41.3 %collective-permute-start.22 = (bf16[192,1024]{1,0:T(8,128)(2,1)S(1)}, bf16[192,1024]{1,0:T(8,128)(2,1)S(1)}, u32[]{:S(2)}, u32[]{:S(2)}) collective-permute-start(bf16[192,1024]{1,0:T(8,128)(2,1)S(1)} %copy-done.28), channel_id=1, source_target_pairs={{0,8},{8,0},{16,24},{24,16},{1,9},{9,1},{17,25},{25,17},{2,10},{10... | collective-permute-start | bytes 1179656 | tf_op jit(solution)/shard_map/ppermute | solution.py:921
  296.2 40.7 %collective-permute-start.23 = (bf16[192,1024]{1,0:T(8,128)(2,1)S(1)}, bf16[192,1024]{1,0:T(8,128)(2,1)S(1)}, u32[]{:S(2)}, u32[]{:S(2)}) collective-permute-start(bf16[192,1024]{1,0:T(8,128)(2,1)S(1)} %copy-done.29), channel_id=1, source_target_pairs={{0,16},{8,24},{16,0},{24,8},{1,17},{9,25},{17,1},{25,9},{2,18},{10... | collective-permute-start | bytes 1179656 | tf_op jit(solution)/shard_map/ppermute | solution.py:921
  296.3 40.6 %collective-permute-start.24 = (bf16[192,1024]{1,0:T(8,128)(2,1)S(1)}, bf16[192,1024]{1,0:T(8,128)(2,1)S(1)}, u32[]{:S(2)}, u32[]{:S(2)}) collective-permute-start(bf16[192,1024]{1,0:T(8,128)(2,1)S(1)} %copy-done.30), channel_id=1, source_target_pairs={{0,24},{8,16},{16,8},{24,0},{1,25},{9,17},{17,9},{25,1},{2,26},{10... | collective-permute-start | bytes 1179656 | tf_op jit(solution)/shard_map/ppermute | solution.py:921
  341.3 49.5 %collective-permute-start.29 = (bf16[240,768]{1,0:T(8,128)(2,1)}, bf16[240,768]{1,0:T(8,128)(2,1)S(1)}, u32[]{:S(2)}, u32[]{:S(2)}) collective-permute-start(bf16[240,768]{1,0:T(8,128)(2,1)} %get-tuple-element.208.refs_13_.refs_10_), channel_id=1, source_target_pairs={{0,24},{8,16},{16,8},{24,0},{1,25},{9,17},{17,9},{25,1},{2,26},{10... | collective-permute-start | bytes 1105928 | tf_op jit(solution)/shard_map/ppermute | solution.py:921
  341.4 49.4 %collective-permute-start.28 = (bf16[240,768]{1,0:T(8,128)(2,1)}, bf16[240,768]{1,0:T(8,128)(2,1)S(1)}, u32[]{:S(2)}, u32[]{:S(2)}) collective-permute-start(bf16[240,768]{1,0:T(8,128)(2,1)} %get-tuple-element.208.refs_13_.refs_10_), channel_id=1, source_target_pairs={{0,16},{8,24},{16,0},{24,8},{1,17},{9,25},{17,1},{25,9},{2,18},{10... | collective-permute-start | bytes 1105928 | tf_op jit(solution)/shard_map/ppermute | solution.py:921
  342.8 48.1 %all-to-all-start.3 = ((bf16[8,96,512]{2,1,0:T(8,128)(2,1)}), bf16[8,96,512]{2,1,0:T(8,128)(2,1)S(1)}, u32[]{:S(2)}, u32[]{:S(2)}) async-start(bf16[8,96,512]{2,1,0:T(8,128)(2,1)} %bitcast.25), calls=%async_computation.3 | async-start | bytes 1572864 | tf_op jit(solution)/shard_map/all_to_all | solution.py:988
  348.9 41.9 %collective-permute-start.25 = (bf16[192,1024]{1,0:T(8,128)(2,1)}, bf16[192,1024]{1,0:T(8,128)(2,1)S(1)}, u32[]{:S(2)}, u32[]{:S(2)}) collective-permute-start(bf16[192,1024]{1,0:T(8,128)(2,1)} %get-tuple-element.205), channel_id=1, source_target_pairs={{0,8},{8,0},{16,24},{24,16},{1,9},{9,1},{17,25},{25,17},{2,10},{10... | collective-permute-start | bytes 1179656 | tf_op jit(solution)/shard_map/ppermute | solution.py:921
  349.9 40.9 %collective-permute-start.26 = (bf16[192,1024]{1,0:T(8,128)(2,1)}, bf16[192,1024]{1,0:T(8,128)(2,1)S(1)}, u32[]{:S(2)}, u32[]{:S(2)}) collective-permute-start(bf16[192,1024]{1,0:T(8,128)(2,1)} %get-tuple-element.206), channel_id=1, source_target_pairs={{0,16},{8,24},{16,0},{24,8},{1,17},{9,25},{17,1},{25,9},{2,18},{10... | collective-permute-start | bytes 1179656 | tf_op jit(solution)/shard_map/ppermute | solution.py:921
  350.0 40.9 %collective-permute-start.27 = (bf16[192,1024]{1,0:T(8,128)(2,1)}, bf16[192,1024]{1,0:T(8,128)(2,1)S(1)}, u32[]{:S(2)}, u32[]{:S(2)}) collective-permute-start(bf16[192,1024]{1,0:T(8,128)(2,1)} %get-tuple-element.207), channel_id=1, source_target_pairs={{0,24},{8,16},{16,8},{24,0},{1,25},{9,17},{17,9},{25,1},{2,26},{10... | collective-permute-start | bytes 1179656 | tf_op jit(solution)/shard_map/ppermute | solution.py:921
  392.3 25.9 %all-to-all-start.4 = ((bf16[8,96,256]{2,1,0:T(8,128)(2,1)}), bf16[8,96,256]{2,1,0:T(8,128)(2,1)S(1)}, u32[]{:S(2)}, u32[]{:S(2)}) async-start(bf16[8,96,256]{2,1,0:T(8,128)(2,1)} %bitcast.26), calls=%async_computation.4 | async-start | bytes 786432 | tf_op jit(solution)/shard_map/all_to_all | solution.py:988
  398.2 12.0 %collective-permute-start.30 = (bf16[192,1024]{1,0:T(8,128)(2,1)}, bf16[192,1024]{1,0:T(8,128)(2,1)S(1)}, u32[]{:S(2)}, u32[]{:S(2)}) collective-permute-start(bf16[192,1024]{1,0:T(8,128)(2,1)} %get-tuple-element.222), channel_id=1, source_target_pairs={{0,8},{8,0},{16,24},{24,16},{1,9},{9,1},{17,25},{25,17},{2,10},{10... | collective-permute-start | bytes 1179656 | tf_op jit(solution)/shard_map/ppermute | solution.py:921
  398.7 11.5 %collective-permute-start.31 = (bf16[192,1024]{1,0:T(8,128)(2,1)}, bf16[192,1024]{1,0:T(8,128)(2,1)S(1)}, u32[]{:S(2)}, u32[]{:S(2)}) collective-permute-start(bf16[192,1024]{1,0:T(8,128)(2,1)} %get-tuple-element.223), channel_id=1, source_target_pairs={{0,16},{8,24},{16,0},{24,8},{1,17},{9,25},{17,1},{25,9},{2,18},{10... | collective-permute-start | bytes 1179656 | tf_op jit(solution)/shard_map/ppermute | solution.py:921
  398.8 19.4 %collective-permute-start.32 = (bf16[192,1024]{1,0:T(8,128)(2,1)}, bf16[192,1024]{1,0:T(8,128)(2,1)S(1)}, u32[]{:S(2)}, u32[]{:S(2)}) collective-permute-start(bf16[192,1024]{1,0:T(8,128)(2,1)} %get-tuple-element.224), channel_id=1, source_target_pairs={{0,24},{8,16},{16,8},{24,0},{1,25},{9,17},{17,9},{25,1},{2,26},{10... | collective-permute-start | bytes 1179656 | tf_op jit(solution)/shard_map/ppermute | solution.py:921
  400.4 23.5 %collective-permute-start.36 = (bf16[240,768]{1,0:T(8,128)(2,1)}, bf16[240,768]{1,0:T(8,128)(2,1)S(1)}, u32[]{:S(2)}, u32[]{:S(2)}) collective-permute-start(bf16[240,768]{1,0:T(8,128)(2,1)} %get-tuple-element.227.refs_3_), channel_id=1, source_target_pairs={{0,8},{8,0},{16,24},{24,16},{1,9},{9,1},{17,25},{25,17},{2,10},{10... | collective-permute-start | bytes 1105928 | tf_op jit(solution)/shard_map/ppermute | solution.py:921
  421.8 13.4 %collective-permute-start.35 = (bf16[96,768]{1,0:T(8,128)(2,1)}, bf16[96,768]{1,0:T(8,128)(2,1)S(1)}, u32[]{:S(2)}, u32[]{:S(2)}) collective-permute-start(bf16[96,768]{1,0:T(8,128)(2,1)} %beside.1.refs_3_), channel_id=1, source_target_pairs={{0,24},{8,16},{16,8},{24,0},{1,25},{9,17},{17,9},{25,1},{2,26},{10... | collective-permute-start | bytes 442376 | tf_op jit(solution)/shard_map/ppermute | solution.py:921
  422.0 13.3 %collective-permute-start.34 = (bf16[96,768]{1,0:T(8,128)(2,1)}, bf16[96,768]{1,0:T(8,128)(2,1)S(1)}, u32[]{:S(2)}, u32[]{:S(2)}) collective-permute-start(bf16[96,768]{1,0:T(8,128)(2,1)} %beside.1.refs_3_), channel_id=1, source_target_pairs={{0,16},{8,24},{16,0},{24,8},{1,17},{9,25},{17,1},{25,9},{2,18},{10... | collective-permute-start | bytes 442376 | tf_op jit(solution)/shard_map/ppermute | solution.py:921
  423.3 11.9 %collective-permute-start.33 = (bf16[96,768]{1,0:T(8,128)(2,1)}, bf16[96,768]{1,0:T(8,128)(2,1)S(1)}, u32[]{:S(2)}, u32[]{:S(2)}) collective-permute-start(bf16[96,768]{1,0:T(8,128)(2,1)} %beside.1.refs_3_), channel_id=1, source_target_pairs={{0,8},{8,0},{16,24},{24,16},{1,9},{9,1},{17,25},{25,17},{2,10},{10... | collective-permute-start | bytes 442376 | tf_op jit(solution)/shard_map/ppermute | solution.py:921
  (45 other events, 112.9 us)
Sparse Core Ops, SparseCore 0:
  42.4 64.4 all-gather.1

commit v2 on v1

--- a/solution.py
+++ b/solution.py
@@ -685,8 +685,8 @@
     )(cosine, sine)
 
 
-def wide_kernel(place_ref, second_ref, dgu_ref, mixed_ref, branch_ref, *refs):
-    outs, held_ref = refs[:-1], refs[-1]
+def grads_kernel(place_ref, second_ref, dgu_ref, mixed_ref, branch_ref, inner_ref, dy_ref, *refs):
+    outs, tall_ref, held_ref = refs[:-2], refs[-2], refs[-1]
     i = pl.program_id(0)
     group = i ^ place_ref[0]
     end = pl.num_programs(0) - 1
@@ -699,6 +699,10 @@
     def _():
         held_ref[...] = dg(mixed_ref[...], branch_ref[...], NN).astype(bf)
 
+    @pl.when(i < end)
+    def _():
+        tall_ref[...] = dg(inner_ref[...], dy_ref[...], TN).astype(bf)
+
     for j in range(len(outs)):
 
         @pl.when(i == j)
@@ -706,12 +710,14 @@
             outs[j][...] = held_ref[...]
 
 
-def wide_grads(place, second, d_gate_up, mixed_t, branch):
+def weight_grads(place, second, d_gate_up, mixed_t, branch, inner, dy):
     rows = second.shape[0]
+    ff = inner.shape[1]
     steps = d_gate_up.shape[1] // D
     whole = lambda i, p: (0, 0)
-    return pl.pallas_call(
-        wide_kernel,
+    part = lambda i, p: (0, jnp.minimum(i, steps - 1))
+    outs = pl.pallas_call(
+        grads_kernel,
         grid_spec=pltpu.PrefetchScalarGridSpec(
             num_scalar_prefetch=1,
             grid=(steps + 1,),
@@ -720,57 +726,34 @@
                 pl.BlockSpec((rows, D), lambda i, p: (0, jnp.minimum(i ^ p[0], steps - 1))),
                 pl.BlockSpec((D, rows), whole),
                 pl.BlockSpec((rows, D), whole),
+                pl.BlockSpec((rows, ff // steps), part),
+                pl.BlockSpec((rows, D), whole),
             ],
-            out_specs=(pl.BlockSpec((D, D), whole),) * (steps + 1),
+            out_specs=(pl.BlockSpec((D, D), whole),) * (steps + 1)
+            + (pl.BlockSpec((ff // steps, D), lambda i, p: (jnp.minimum(i, steps - 1), 0)),),
             scratch_shapes=[pltpu.VMEM((D, D), bf)],
         ),
-        out_shape=(jax.ShapeDtypeStruct((D, D), bf),) * (steps + 1),
+        out_shape=(jax.ShapeDtypeStruct((D, D), bf),) * (steps + 1)
+        + (jax.ShapeDtypeStruct((ff, D), bf),),
         compiler_params=pltpu.CompilerParams(vmem_limit_bytes=58 * 2**20),
         cost_estimate=pl.CostEstimate(
-            flops=2 * rows * D * D * (steps + 1), bytes_accessed=16 * 2**20, transcendentals=0
+            flops=2 * rows * D * (D * (steps + 1) + ff), bytes_accessed=20 * 2**20, transcendentals=0
         ),
-        name="wide_grads",
-    )(place, second, d_gate_up, mixed_t, branch)
-
-
-def tall_grads(inner, dy, wide, after):
-    rows, ff = inner.shape
-    step = ff // 3
-    many = len(wide)
-
-    def kernel(inner_ref, dy_ref, *refs):
-        refs[many + len(after)][...] = dg(inner_ref[...], dy_ref[...], TN).astype(bf)
-
-    anywhere = pl.BlockSpec(memory_space=pl.ANY)
-    outs = pl.pallas_call(
-        kernel,
-        grid=(3,),
-        in_specs=[
-            pl.BlockSpec((rows, step), lambda i: (0, i)),
-            pl.BlockSpec((rows, D), lambda i: (0, 0)),
-        ]
-        + [anywhere] * (many + len(after)),
-        out_specs=(pl.BlockSpec((step, D), lambda i: (i, 0)),) + (anywhere,) * many,
-        out_shape=(jax.ShapeDtypeStruct((ff, D), bf),)
-        + tuple(jax.ShapeDtypeStruct(w.shape, bf) for w in wide),
-        input_output_aliases={2 + n: 1 + n for n in range(many)},
-        compiler_params=pltpu.CompilerParams(vmem_limit_bytes=58 * 2**20),
-        cost_estimate=pl.CostEstimate(
-            flops=2 * rows * D * ff, bytes_accessed=6 * 2**20, transcendentals=0
-        ),
-        name="tall_grads",
-    )(inner, dy, *wide, *after)
-    return outs[0], list(outs[1:])
-
-
-def ordered(kernel, arrays, after, carry, out_shape, in_specs, out_specs, name, grid=()):
+        name="weight_grads",
+    )(place, second, d_gate_up, mixed_t, branch, inner, dy)
+    return list(outs[:-1]), outs[-1]
+
+
+def ordered(
+    kernel, arrays, after, carry, out_shape, in_specs, out_specs, name, grid=(), scratch=()
+):
     first = len(arrays) + len(after)
     own = len(out_shape)
     anywhere = pl.BlockSpec(memory_space=pl.ANY)
 
     def call(*refs):
         outs = refs[first + len(carry) :]
-        kernel(*refs[: len(arrays)], *outs[:own])
+        kernel(*refs[: len(arrays)], *outs[:own], *outs[own + len(carry) :])
 
     outs = pl.pallas_call(
         call,
@@ -778,6 +761,7 @@
         out_shape=tuple(out_shape) + tuple(jax.ShapeDtypeStruct(a.shape, a.dtype) for a in carry),
         in_specs=list(in_specs) + [anywhere] * (len(after) + len(carry)),
         out_specs=tuple(out_specs) + (anywhere,) * len(carry),
+        scratch_shapes=list(scratch),
         input_output_aliases={first + n: own + n for n in range(len(carry))},
         compiler_params=pltpu.CompilerParams(vmem_limit_bytes=58 * 2**20),
         name=name,
@@ -886,24 +870,15 @@
     dgain_ref[...] = row_of(total / column(gain_ref))
 
 
-def finish(kernel, groups, info, w, gain, parts, shapes, name, after=()):
+def finish(kernel, groups, info, w, gain, parts, shapes, name, after=(), carry=()):
     vmem = pl.BlockSpec(memory_space=pltpu.VMEM)
-    first = 3 + groups
-
-    def call(*refs):
-        kernel(*refs[:first], *refs[first + len(after) :])
-
-    return pl.pallas_call(
-        call,
-        out_shape=tuple(jax.ShapeDtypeStruct(shape, f32) for shape in shapes),
-        in_specs=[pl.BlockSpec(memory_space=pltpu.SMEM)]
-        + [vmem] * (2 + groups)
-        + [pl.BlockSpec(memory_space=pl.ANY)] * len(after),
-        out_specs=(vmem,) * len(shapes),
-        scratch_shapes=[pltpu.VMEM((groups,) + parts[0].shape, bf)],
-        compiler_params=pltpu.CompilerParams(vmem_limit_bytes=58 * 2**20),
-        name=name,
-    )(info, w, gain, *parts, *after)
+    return ordered(
+        kernel, [info, w, gain, *parts], list(after), list(carry),
+        [jax.ShapeDtypeStruct(shape, f32) for shape in shapes],
+        [pl.BlockSpec(memory_space=pltpu.SMEM)] + [vmem] * (2 + groups),
+        [vmem] * len(shapes), name,
+        scratch=[pltpu.VMEM((groups,) + parts[0].shape, bf)],
+    )
 
 
 def body(
@@ -960,22 +935,29 @@
 
     own = hold(own, [normed])
     own_near, own_across = swap(own, 1), swap(own, 2)
-    own_diagonal = swap(own_across, 1)
-    peers = [own, own_near, own_across, own_diagonal]
 
     kept = []
     chunks = []
-    orders = [[], [own_near, own_across], [own_diagonal]]
     for h in range(heads):
         before = [kept[-1][2]] if kept else []
-        if h == 2:
-            before += chunks[1:groups]
-        saved, mixed = attend(h, k, qt, vt, groups, orders[h] + before)
+        if h == 1:
+            before += [own_near, own_across]
+        saved, mixed = attend(h, k, qt, vt, groups, before)
         kept.append(saved)
+        if h > 0:
+            early = [chunks[n] for n in range((h - 1) * groups, h * groups) if n % groups]
+            extra = [mine] if h == heads - 2 else [own_across]
+            _, carried = ordered(
+                lambda: None, [], [saved[2]] + early, mixed[1:] + extra, [], [], [], "hold"
+            )
+            mixed = mixed[:1] + carried[:-1]
+            if h == heads - 2:
+                mine = carried[-1]
+                other = swap(mine, 1)
+            else:
+                own_across = carried[-1]
+                own_diagonal = swap(own_across, 1)
         chunks += exchange(mixed)
-        if h == heads - 2:
-            mine = hold(mine, [saved[2]])
-            other = swap(mine, 1)
 
     dy = out_grad[0]
     d_mixed, (result, d_hidden, mixed_t, second, d_gate_up, inner, branch) = middle(
@@ -990,9 +972,12 @@
     def from_peers(array):
         return [array] + [swap(array, j) for j in range(1, groups)]
 
-    wide_own, *wide_rest = wide_grads(place, second, d_gate_up, mixed_t, branch)
-    tall_grad, wide_rest = tall_grads(inner, dy, wide_rest, d_mixed[1:])
-    wide_all = exchange([wide_own] + wide_rest)
+    wide, tall_grad = weight_grads(place, second, d_gate_up, mixed_t, branch, inner, dy)
+    _, carried = ordered(
+        lambda: None, [], d_mixed[1:], wide[1:] + [tall_grad], [], [], [], "hold"
+    )
+    tall_grad = carried[-1]
+    wide_all = exchange(wide[:1] + carried[:-1])
     tall_parts = to_owner(tall_grad)
 
     def back(h, grad_place, after):
@@ -1000,7 +985,8 @@
             h, v, kt, qt, d_mixed, kept[h], cos_t, sin_t, normed, groups, grad_place, after
         )
 
-    sent_0, qkv_first = back(0, (512, 0, None), [tall_grad])
+    peers = [own, own_near, own_across, own_diagonal]
+    sent_0, qkv_first = back(0, (512, 0, None), [tall_grad, own_diagonal])
     wide_sum, others = add_up(wide_all, [qkv_first, tall_parts], sent_0[1:])
     wide_parts = to_owner(wide_sum)
     received_0 = exchange(sent_0[:1] + others)
@@ -1019,19 +1005,19 @@
     qkv_second, both = carried[-2:]
     received_2 = exchange(sent_2[:1] + carried[:-2])
     both_peers = [both, swap(both, 1)] + both_far
-    qkv_second_parts = to_owner(qkv_second)
-
-    base = last(
-        groups, heads, (0, 1), x0, d_hidden, peers, received_0 + received_1, [qkv_second]
-    )
-    in_weight_grad, proj_weight_grad, ffn_gain_grad, out_weight_grad = finish(
+    (in_weight_grad, proj_weight_grad, ffn_gain_grad, out_weight_grad), carried = finish(
         functools.partial(finish_wide_kernel, groups),
         groups, place, in_weight, ffn_row, both_peers,
         ((shard, 2 * ff), (shard, D), (1, shard), (tall, D)), "finish_wide",
+        carry=[qkv_second],
+    )
+    qkv_second_parts = to_owner(carried[0])
+    base = last(
+        groups, heads, (0, 1), x0, d_hidden, peers, received_0 + received_1, [carried[0]]
     )
     qkv_peers = from_peers(beside(qkv_parts, qkv_second_parts, [base] + received_2[1:]))
     tokens_grad = last(groups, heads, (2,), x0, base, peers, received_2, [])
-    qkv_weight_grad, attn_gain_grad = finish(
+    (qkv_weight_grad, attn_gain_grad), _ = finish(
         functools.partial(finish_qkv_kernel, groups, heads),
         groups, place, qkv_weight, attn_row, qkv_peers,
         ((shard, 3 * D), (1, shard)), "finish_qkv", [tokens_grad],

time: 450 us -> 438 us (0.973)
  waiting for transfers between devices: 59 us -> 49.4 us
    ppermute x37, waiting for transfers between devices: 44.6 us -> 35.1 us  [swap(): return lax.ppermute(array, axis, [(i, i ^ j) for i in range(size)])]
    pallas_call x4 -> x1, Pallas kernels: 22.1 us -> 14.7 us  [weight_grads(): pl.pallas_call(grads_kernel, grid_spec=pltpu.PrefetchScalarGridSpec(num_s...]
    pallas_call x3 -> x8, Pallas kernels: 7.16 us -> 12.4 us  [ordered(): pl.pallas_call(call, grid=grid, out_shape=tuple(out_shape) + tuple((jax.S...]
    unnamed x100 -> x86, local copies, waits for them, and re-layouts: 16.6 us -> 18.6 us
  transfers between devices with their start and end apart: 43 -> 43, of which waited for: 9 -> 8; matrix products, arithmetic and copies ran while one was open for 1% -> 1% of each run, Pallas kernels for 55% -> 63%
where the time goes in v2:
time: 438 us; the launch traced here: 434 us
  Pallas kernels  290 us (66%)
  starting transfers between devices  58 us (13%)
  waiting for transfers between devices  49.4 us (11%)
  local copies, waits for them, and re-layouts  18.6 us (4%)
  between operations  15.5 us (4%)
    pallas_call x3, Pallas kernels, attend_back(): pl.pallas_call(functools.partial(attend_back_kernel, kc, groups), grid=(g...  117 us
    pallas_call x3, Pallas kernels, attend(): pl.pallas_call(functools.partial(attend_kernel, kc, groups, len(after)),...  62.6 us
    ppermute x37, waiting for transfers between devices, swap(): return lax.ppermute(array, axis, [(i, i ^ j) for i in range(size)])  35.1 us
    pallas_call x1, Pallas kernels, middle(): pl.pallas_call(functools.partial(middle_kernel, groups, heads, ff, shards...  28.6 us
    ppermute x37, starting transfers between devices, swap(): return lax.ppermute(array, axis, [(i, i ^ j) for i in range(size)])  28.5 us
    pallas_call x4, Pallas kernels, qkv_call(): pl.pallas_call(functools.partial(qkv_kernel, heads), grid=(steps,), out_s...  25 us
    all_to_all x4, starting transfers between devices, to_owner(): lax.all_to_all(parts, 'fsdp', split_axis=0, concat_axis=0, tiled=True)  23.1 us
    unnamed x86, local copies, waits for them, and re-layouts  18.6 us
  transfers between devices with their start and end apart: 43, of which 8 were waited for; matrix products, arithmetic and copies ran while one was open for 1% of the time, Pallas kernels for 63%

profile of v2, /device:TPU:1, one launch (start us, length us, event | category | flops | bytes accessed | tf_op | source)
XLA Modules:
  0.0 434.1 jit_solution(5580607861316332835)
XLA Ops:
  7.2 2.2 own_columns.1
  9.3 6.4 %all-to-all-start = ((bf16[8,96,640]{2,1,0:T(8,128)(2,1)}), bf16[8,96,640]{2,1,0:T(8,128)(2,1)S(1)}, u32[]{:S(2)}, u32[]{:S(2)}) async-start(bf16[8,96,640]{2,1,0:T(8,128)(2,1)} %own_columns.1), calls=%async_computation | async-start | bytes 1966080 | tf_op jit(solution)/shard_map/all_to_all | solution.py:911
  15.7 1.3 collective-permute-start
  17.1 2.8 multiply_sine_fusion
  19.9 4.7 %tables.1 = (f32[4096,128]{1,0:T(8,128)}, f32[4096,128]{1,0:T(8,128)}, f32[64,4096]{1,0:T(8,128)}, f32[64,4096]{1,0:T(8,128)}) custom-call(f32[32,4096]{1,0:T(8,128)} %get-tuple-element.253.cos_ref, f32[32,4096]{1,0:T(8,128)} %get-tuple-element.252.sin_ref), custom_call_target="tpu_custom_call" | custom-call | tf_op jit(solution)/shard_map/tables/pallas_call | solution.py:676
  24.6 14.3 %all-to-all-done = bf16[8,96,640]{2,1,0:T(8,128)(2,1)S(1)} async-done(((bf16[8,96,640]{2,1,0:T(8,128)(2,1)}), bf16[8,96,640]{2,1,0:T(8,128)(2,1)S(1)}, u32[]{:S(2)}, u32[]{:S(2)}) %all-to-all-start) | async-done | bytes 983072 | tf_op jit(solution)/shard_map/all_to_all | solution.py:911
  39.9 2.4 own_half.1
  42.3 2.0 collective-permute-start.2
  44.3 6.7 %collective-permute-done.x_ref = bf16[1024,768]{1,0:T(8,128)(2,1)} collective-permute-done((bf16[1024,768]{1,0:T(8,128)(2,1)}, bf16[1024,768]{1,0:T(8,128)(2,1)}, u32[]{:S(2)}, u32[]{:S(2)}) %collective-permute-start) | collective-permute-done | bytes 1572896 | tf_op jit(solution)/shard_map/ppermute | solution.py:896
  51.1 1.9 collective-permute-start.1
  55.0 6.3 %qkv.4 = (bf16[4096,768]{1,0:T(8,128)(2,1)}, bf16[3,4096,128]{2,1,0:T(8,128)(2,1)}, bf16[3,4096,128]{2,1,0:T(8,128)(2,1)}, bf16[3,128,4096]{2,1,0:T(8,128)(2,1)}...) custom-call(s32[2]{0:T(128)S(1)} %get-tuple-element.255.info_ref, ...), custom_call_target="tpu_custom_call" | custom-call | flops 2013265920 | bytes 8388608 | tf_op jit(solution)/shard_map/qkv/pallas_call | solution.py:107
  61.3 6.4 %qkv.5 = (bf16[4096,768]{1,0:T(8,128)(2,1)}, bf16[3,4096,128]{2,1,0:T(8,128)(2,1)}, bf16[3,4096,128]{2,1,0:T(8,128)(2,1)}, bf16[3,128,4096]{2,1,0:T(8,128)(2,1)}...) custom-call(s32[2]{0:T(128)S(1)} %get-tuple-element.254.info_ref, ...), custom_call_target="tpu_custom_call", output_to_operand_aliasing={{0}: (5, {}), {1}: (6, {}), {2}: (7, {}), {3}: (8, {}), {4}... | custom-call | flops 2013265920 | bytes 8388608 | tf_op jit(solution)/shard_map/qkv/pallas_call | solution.py:107
  67.7 6.1 %qkv.6 = (bf16[4096,768]{1,0:T(8,128)(2,1)}, bf16[3,4096,128]{2,1,0:T(8,128)(2,1)}, bf16[3,4096,128]{2,1,0:T(8,128)(2,1)}, bf16[3,128,4096]{2,1,0:T(8,128)(2,1)}...) custom-call(s32[2]{0:T(128)S(1)} %pad_add_fusion.1.info_ref, ...), custom_call_target="tpu_custom_call", output_to_operand_aliasing={{0}: (5, {}), {1}: (6, {}), {2}: (7, {}), {3}: (8, {}), {4}... | custom-call | flops 2013265920 | bytes 8388608 | tf_op jit(solution)/shard_map/qkv/pallas_call | solution.py:107
  73.8 6.2 %qkv.7 = (bf16[4096,768]{1,0:T(8,128)(2,1)}, bf16[3,4096,128]{2,1,0:T(8,128)(2,1)}, bf16[3,4096,128]{2,1,0:T(8,128)(2,1)}, bf16[3,128,4096]{2,1,0:T(8,128)(2,1)}...) custom-call(s32[2]{0:T(128)S(1)} %pad_add_fusion.info_ref, ...), custom_call_target="tpu_custom_call", output_to_operand_aliasing={{0}: (5, {}), {1}: (6, {}), {2}: (7, {}), {3}: (8, {}), {4}... | custom-call | flops 2013265920 | bytes 8388608 | tf_op jit(solution)/shard_map/qkv/pallas_call | solution.py:107
  80.0 1.3 copy-done.2
  83.0 20.5 %attend.3 = (bf16[4,4096,512]{2,1,0:T(8,128)(2,1)}, bf16[4,4096,512]{2,1,0:T(8,128)(2,1)}, f32[64,2048]{1,0:T(8,128)}, f32[64,2048]{1,0:T(8,128)}, f32[4,1,512]{...) custom-call(bf16[3,4096,128]{2,1,0:T(8,128)(2,1)} %get-tuple-element, ...), custom_call_target="tpu_custom_call" | custom-call | flops 17179869184 | bytes 33554432 | tf_op jit(solution)/shard_map/attend/pallas_call | solution.py:197
  104.6 1.4 collective-permute-start.7
  107.3 21.0 %attend.4 = (bf16[4,4096,512]{2,1,0:T(8,128)(2,1)}, bf16[4,4096,512]{2,1,0:T(8,128)(2,1)}, f32[64,2048]{1,0:T(8,128)}, f32[64,2048]{1,0:T(8,128)}, f32[4,1,512]{...) custom-call(bf16[3,4096,128]{2,1,0:T(8,128)(2,1)} %get-tuple-element, ...), custom_call_target="tpu_custom_call" | custom-call | flops 17179869184 | bytes 33554432 | tf_op jit(solution)/shard_map/attend/pallas_call | solution.py:197
  131.2 21.1 %attend.5 = (bf16[4,4096,512]{2,1,0:T(8,128)(2,1)}, bf16[4,4096,512]{2,1,0:T(8,128)(2,1)}, f32[64,2048]{1,0:T(8,128)}, f32[64,2048]{1,0:T(8,128)}, f32[4,1,512]{...) custom-call(bf16[3,4096,128]{2,1,0:T(8,128)(2,1)} %get-tuple-element, ...), custom_call_target="tpu_custom_call" | custom-call | flops 17179869184 | bytes 33554432 | tf_op jit(solution)/shard_map/attend/pallas_call | solution.py:197
  155.5 3.5 collective-permute-done.13.refs_10_
  159.0 2.9 collective-permute-done.14.refs_11_
  162.5 28.6 %middle.1 = (bf16[192,1024]{1,0:T(8,128)(2,1)}, bf16[192,1024]{1,0:T(8,128)(2,1)}, bf16[192,1024]{1,0:T(8,128)(2,1)}, bf16[192,1024]{1,0:T(8,128)(2,1)}, bf16[10...) custom-call(s32[1]{0:T(128)} %bitcast.info_ref.place_ref.refs_0_, ...), custom_call_target="tpu_custom_call" | custom-call | flops 15099494400 | bytes 31457280 | tf_op jit(solution)/shard_map/middle/pallas_call | solution.py:514
  191.8 1.6 collective-permute-start.17
  193.4 14.7 %weight_grads.1 = (bf16[768,768]{1,0:T(8,128)(2,1)}, bf16[768,768]{1,0:T(8,128)(2,1)}, bf16[768,768]{1,0:T(8,128)(2,1)}, bf16[768,768]{1,0:T(8,128)(2,1)}, bf16[1152,768]{1,0:T(8,128)(2,1)}) custom-call(s32[1]{0:T(128)} %bitcast.info_ref.place_ref.refs_0_, bf16[1024,768]{1,0:T(8,128)(2,1)} %get-tuple-element.191.second_ref, ...), custom_call_target="tpu_custom_call" | custom-call | flops 6643777536 | bytes 20971520 | tf_op jit(solution)/shard_map/weight_grads/pallas_call | solution.py:719
  208.1 2.9 collective-permute-done.17.refs_2_.refs_12_
  211.7 5.4 %all-to-all-start.1 = ((bf16[8,144,768]{2,1,0:T(8,128)(2,1)}), bf16[8,144,768]{2,1,0:T(8,128)(2,1)S(1)}, u32[]{:S(2)}, u32[]{:S(2)}) async-start(bf16[8,144,768]{2,1,0:T(8,128)(2,1)} %bitcast.26), calls=%async_computation.1 | async-start | bytes 3538944 | tf_op jit(solution)/shard_map/all_to_all | solution.py:970
  217.5 1.8 collective-permute-start.21
  220.2 39.2 %attend_back.3 = (bf16[192,1024]{1,0:T(8,128)(2,1)}, bf16[192,1024]{1,0:T(8,128)(2,1)}, bf16[192,1024]{1,0:T(8,128)(2,1)}, bf16[192,1024]{1,0:T(8,128)(2,1)}, bf16[768,512]{1,0:T(8,128)(2,1)}) custom-call(bf16[3,4096,128]{2,1,0:T(8,128)(2,1)} %get-tuple-element.179.v_ref, bf16[3,64,4096]{2,1,0:T(8,128)(2,1)} %copy-done.3, ...), custom_call_target="tpu_custom_call" | custom-call | flops 25769803776 | bytes 33554432 | tf_op jit(solution)/shard_map/attend_back/pallas_call | solution.py:313
  261.5 9.3 %collective-permute-done.21.refs_3_ = bf16[768,768]{1,0:T(8,128)(2,1)} collective-permute-done((bf16[768,768]{1,0:T(8,128)(2,1)}, bf16[768,768]{1,0:T(8,128)(2,1)}, u32[]{:S(2)}, u32[]{:S(2)}) %collective-permute-start.21) | collective-permute-done | bytes 1179680 | tf_op jit(solution)/shard_map/ppermute | solution.py:896
  272.0 4.2 add_up.1
  276.3 2.0 collective-permute-start.24
  278.4 6.0 %all-to-all-start.2 = ((bf16[8,96,768]{2,1,0:T(8,128)(2,1)}), bf16[8,96,768]{2,1,0:T(8,128)(2,1)S(1)}, u32[]{:S(2)}, u32[]{:S(2)}) async-start(bf16[8,96,768]{2,1,0:T(8,128)(2,1)} %bitcast.28), calls=%async_computation.2 | async-start | bytes 2359296 | tf_op jit(solution)/shard_map/all_to_all | solution.py:970
  284.3 39.0 %attend_back.4 = (bf16[192,1024]{1,0:T(8,128)(2,1)}, bf16[192,1024]{1,0:T(8,128)(2,1)}, bf16[192,1024]{1,0:T(8,128)(2,1)}, bf16[192,1024]{1,0:T(8,128)(2,1)}, bf16[768,512]{1,0:T(8,128)(2,1)}) custom-call(bf16[3,4096,128]{2,1,0:T(8,128)(2,1)} %get-tuple-element.179.v_ref, bf16[3,64,4096]{2,1,0:T(8,128)(2,1)} %copy-done.3, ...), custom_call_target="tpu_custom_call", output_to_operand_aliasing={{4}: (16, {})} | custom-call | flops 25769803776 | bytes 33554432 | tf_op jit(solution)/shard_map/attend_back/pallas_call | solution.py:313
  324.8 3.0 owned.1
  327.8 1.9 collective-permute-start.29
  329.8 2.0 collective-permute-start.27
  331.8 6.2 %all-to-all-start.3 = ((bf16[8,96,512]{2,1,0:T(8,128)(2,1)}), bf16[8,96,512]{2,1,0:T(8,128)(2,1)S(1)}, u32[]{:S(2)}, u32[]{:S(2)}) async-start(bf16[8,96,512]{2,1,0:T(8,128)(2,1)} %bitcast.25), calls=%async_computation.3 | async-start | bytes 1572864 | tf_op jit(solution)/shard_map/all_to_all | solution.py:970
  338.0 39.3 %attend_back.5 = (bf16[192,1024]{1,0:T(8,128)(2,1)}, bf16[192,1024]{1,0:T(8,128)(2,1)}, bf16[192,1024]{1,0:T(8,128)(2,1)}, bf16[192,1024]{1,0:T(8,128)(2,1)}, bf16[768,256]{1,0:T(8,128)(2,1)}) custom-call(bf16[3,4096,128]{2,1,0:T(8,128)(2,1)} %get-tuple-element.179.v_ref, bf16[3,64,4096]{2,1,0:T(8,128)(2,1)} %copy-done.3, ...), custom_call_target="tpu_custom_call" | custom-call | flops 25769803776 | bytes 33554432 | tf_op jit(solution)/shard_map/attend_back/pallas_call | solution.py:313
  378.8 1.9 collective-permute-done.30.refs_4_
  381.4 2.8 finish_wide.1
  384.3 5.6 %all-to-all-start.4 = ((bf16[8,96,256]{2,1,0:T(8,128)(2,1)}), bf16[8,96,256]{2,1,0:T(8,128)(2,1)S(1)}, u32[]{:S(2)}, u32[]{:S(2)}) async-start(bf16[8,96,256]{2,1,0:T(8,128)(2,1)} %bitcast.27), calls=%async_computation.4 | async-start | bytes 786432 | tf_op jit(solution)/shard_map/all_to_all | solution.py:970
  391.0 1.3 collective-permute-start.33
  392.3 9.6 %last.2.base_ref.refs_0_ = f32[1024,768]{1,0:T(8,128)} custom-call(bf16[1024,768]{1,0:T(8,128)(2,1)} %bitcast.1.x_ref, f32[1024,768]{1,0:T(8,128)} %get-tuple-element.178.base_ref, bf16[768,640]{1,0:T(8,128)(2,1)} %hold.4.gain_ref.refs_8_.refs_12_.refs_16_.refs_20_.refs_4_, bf16[192,1024]{1,0:T(8,128)(2,1)} %get-tuple-element.202.refs_0_, ...), custom_call_target="tpu_custom_call" | custom-call | flops 2415919104 | bytes 12582912 | tf_op jit(solution)/shard_map/last/pallas_call | solution.py:602
  401.9 7.9 %collective-permute-done.33.refs_3_ = bf16[192,1024]{1,0:T(8,128)(2,1)S(1)} collective-permute-done((bf16[192,1024]{1,0:T(8,128)(2,1)S(1)}, bf16[192,1024]{1,0:T(8,128)(2,1)S(1)}, u32[]{:S(2)}, u32[]{:S(2)}) %collective-permute-start.33) | collective-permute-done | bytes 393248 | tf_op jit(solution)/shard_map/ppermute | solution.py:896
  411.3 2.1 beside.1.refs_3_
  414.0 1.5 collective-permute-start.36
  415.5 7.7 %last.3.refs_7_ = f32[1024,768]{1,0:T(8,128)} custom-call(bf16[1024,768]{1,0:T(8,128)(2,1)} %bitcast.1.x_ref, f32[1024,768]{1,0:T(8,128)} %last.2.base_ref.refs_0_, bf16[768,640]{1,0:T(8,128)(2,1)} %hold.4.gain_ref.refs_8_.refs_12_.refs_16_.refs_20_.refs_4_, bf16[192,1024]{1,0:T(8,128)(2,1)} %get-tuple-element.242.refs_0_, bf16[192,1024]{1,0:T(8,128)(2,1)} %copy-done.17, ...), custom_call_target="tpu_custom_call" | custom-call | flops 1207959552 | bytes 12582912 | tf_op jit(solution)/shard_map/last/pallas_call | solution.py:602
  424.6 2.4 finish_qkv.1
  (161 shorter events, 27.5 us)
Async XLA Ops:
  9.3 29.6 %all-to-all-start = ((bf16[8,96,640]{2,1,0:T(8,128)(2,1)}), bf16[8,96,640]{2,1,0:T(8,128)(2,1)S(1)}, u32[]{:S(2)}, u32[]{:S(2)}) async-start(bf16[8,96,640]{2,1,0:T(8,128)(2,1)} %own_columns.1), calls=%async_computation | async-start | bytes 1966080 | tf_op jit(solution)/shard_map/all_to_all | solution.py:911
  15.7 112.7 %all-gather.2.cloned.1.call-start = ((), (), s32[]{:S(2)}) async-start(), calls=%async_computation.5 | async-start | bytes 3981312 | tf_op jit(solution)/shard_map/all_gather | solution.py:902
  15.7 35.3 %collective-permute-start = (bf16[1024,768]{1,0:T(8,128)(2,1)}, bf16[1024,768]{1,0:T(8,128)(2,1)}, u32[]{:S(2)}, u32[]{:S(2)}) collective-permute-start(bf16[1024,768]{1,0:T(8,128)(2,1)} %bitcast.1.x_ref), channel_id=1, source_target_pairs={{0,16},{8,24},{16,0},{24,8},{1,17},{9,25},{17,1},{25,9},{2,18},{10... | collective-permute-start | bytes 4718600 | tf_op jit(solution)/shard_map/ppermute | solution.py:896
  42.3 25.3 %collective-permute-start.2 = (bf16[1024,768]{1,0:T(8,128)(2,1)}, bf16[1024,768]{1,0:T(8,128)(2,1)S(1)}, u32[]{:S(2)}, u32[]{:S(2)}) collective-permute-start(bf16[1024,768]{1,0:T(8,128)(2,1)} %bitcast.1.x_ref), channel_id=1, source_target_pairs={{0,8},{8,0},{16,24},{24,16},{1,9},{9,1},{17,25},{25,17},{2,10},{10... | collective-permute-start | bytes 4718600 | tf_op jit(solution)/shard_map/ppermute | solution.py:896
  51.1 22.7 %collective-permute-start.1 = (bf16[1024,768]{1,0:T(8,128)(2,1)}, bf16[1024,768]{1,0:T(8,128)(2,1)S(1)}, u32[]{:S(2)}, u32[]{:S(2)}) collective-permute-start(bf16[1024,768]{1,0:T(8,128)(2,1)} %collective-permute-done.x_ref), channel_id=1, source_target_pairs={{0,8},{8,0},{16,24},{24,16},{1,9},{9,1},{17,25},{25,17},{2,10},{10... | collective-permute-start | bytes 4718600 | tf_op jit(solution)/shard_map/ppermute | solution.py:896
  81.7 24.3 %collective-permute-start.3 = (bf16[768,640]{1,0:T(8,128)(2,1)}, bf16[768,640]{1,0:T(8,128)(2,1)S(1)}, u32[]{:S(2)}, u32[]{:S(2)}) collective-permute-start(bf16[768,640]{1,0:T(8,128)(2,1)} %hold.4.gain_ref.refs_8_.refs_12_.refs_16_.refs_20_.refs_4_), channel_id=1, source_target_pairs={{0,8},{8,0},{16,24},{24,16},{1,9},{9,1},{17,25},{25,17},{2,10},{10... | collective-permute-start | bytes 2949128 | tf_op jit(solution)/shard_map/ppermute | solution.py:896
  81.7 24.3 %collective-permute-start.4 = (bf16[768,640]{1,0:T(8,128)(2,1)}, bf16[768,640]{1,0:T(8,128)(2,1)S(1)}, u32[]{:S(2)}, u32[]{:S(2)}) collective-permute-start(bf16[768,640]{1,0:T(8,128)(2,1)} %hold.4.gain_ref.refs_8_.refs_12_.refs_16_.refs_20_.refs_4_), channel_id=1, source_target_pairs={{0,16},{8,24},{16,0},{24,8},{1,17},{9,25},{17,1},{25,9},{2,18},{10... | collective-permute-start | bytes 2949128 | tf_op jit(solution)/shard_map/ppermute | solution.py:896
  103.5 24.9 %collective-permute-start.5 = (bf16[64,1024]{1,0:T(8,128)(2,1)}, bf16[64,1024]{1,0:T(8,128)(2,1)S(1)}, u32[]{:S(2)}, u32[]{:S(2)}) collective-permute-start(bf16[64,1024]{1,0:T(8,128)(2,1)} %get-tuple-element.156), channel_id=1, source_target_pairs={{0,8},{8,0},{16,24},{24,16},{1,9},{9,1},{17,25},{25,17},{2,10},{10... | collective-permute-start | bytes 393224 | tf_op jit(solution)/shard_map/ppermute | solution.py:896
  104.3 24.0 %collective-permute-start.6 = (bf16[64,1024]{1,0:T(8,128)(2,1)}, bf16[64,1024]{1,0:T(8,128)(2,1)S(1)}, u32[]{:S(2)}, u32[]{:S(2)}) collective-permute-start(bf16[64,1024]{1,0:T(8,128)(2,1)} %get-tuple-element.157), channel_id=1, source_target_pairs={{0,16},{8,24},{16,0},{24,8},{1,17},{9,25},{17,1},{25,9},{2,18},{10... | collective-permute-start | bytes 393224 | tf_op jit(solution)/shard_map/ppermute | solution.py:896
  104.6 23.8 %collective-permute-start.7 = (bf16[64,1024]{1,0:T(8,128)(2,1)}, bf16[64,1024]{1,0:T(8,128)(2,1)S(1)}, u32[]{:S(2)}, u32[]{:S(2)}) collective-permute-start(bf16[64,1024]{1,0:T(8,128)(2,1)} %get-tuple-element.158), channel_id=1, source_target_pairs={{0,24},{8,16},{16,8},{24,0},{1,25},{9,17},{17,9},{25,1},{2,26},{10... | collective-permute-start | bytes 393224 | tf_op jit(solution)/shard_map/ppermute | solution.py:896
  129.1 32.8 %collective-permute-start.8 = (bf16[768,2304]{1,0:T(8,128)(2,1)}, bf16[768,2304]{1,0:T(8,128)(2,1)}, u32[]{:S(2)}, u32[]{:S(2)}) collective-permute-start(bf16[768,2304]{1,0:T(8,128)(2,1)} %get-tuple-element.163.mine_ref), channel_id=1, source_target_pairs={{0,8},{8,0},{16,24},{24,16},{1,9},{9,1},{17,25},{25,17},{2,10},{10... | collective-permute-start | bytes 10616840 | tf_op jit(solution)/shard_map/ppermute | solution.py:896
  129.3 23.1 %collective-permute-start.10 = (bf16[64,1024]{1,0:T(8,128)(2,1)}, bf16[64,1024]{1,0:T(8,128)(2,1)S(1)}, u32[]{:S(2)}, u32[]{:S(2)}) collective-permute-start(bf16[64,1024]{1,0:T(8,128)(2,1)} %get-tuple-element.167), channel_id=1, source_target_pairs={{0,16},{8,24},{16,0},{24,8},{1,17},{9,25},{17,1},{25,9},{2,18},{10... | collective-permute-start | bytes 393224 | tf_op jit(solution)/shard_map/ppermute | solution.py:896
  130.1 22.3 %collective-permute-start.11 = (bf16[64,1024]{1,0:T(8,128)(2,1)}, bf16[64,1024]{1,0:T(8,128)(2,1)S(1)}, u32[]{:S(2)}, u32[]{:S(2)}) collective-permute-start(bf16[64,1024]{1,0:T(8,128)(2,1)} %get-tuple-element.168), channel_id=1, source_target_pairs={{0,24},{8,16},{16,8},{24,0},{1,25},{9,17},{17,9},{25,1},{2,26},{10... | collective-permute-start | bytes 393224 | tf_op jit(solution)/shard_map/ppermute | solution.py:896
  131.2 21.2 %collective-permute-start.9 = (bf16[64,1024]{1,0:T(8,128)(2,1)}, bf16[64,1024]{1,0:T(8,128)(2,1)S(1)}, u32[]{:S(2)}, u32[]{:S(2)}) collective-permute-start(bf16[64,1024]{1,0:T(8,128)(2,1)} %get-tuple-element.166), channel_id=1, source_target_pairs={{0,8},{8,0},{16,24},{24,16},{1,9},{9,1},{17,25},{25,17},{2,10},{10... | collective-permute-start | bytes 393224 | tf_op jit(solution)/shard_map/ppermute | solution.py:896
  153.1 2.4 collective-permute-start.12
  153.6 5.3 %collective-permute-start.13 = (bf16[64,1024]{1,0:T(8,128)(2,1)}, bf16[64,1024]{1,0:T(8,128)(2,1)S(1)}, u32[]{:S(2)}, u32[]{:S(2)}) collective-permute-start(bf16[64,1024]{1,0:T(8,128)(2,1)} %get-tuple-element.175), channel_id=1, source_target_pairs={{0,16},{8,24},{16,0},{24,8},{1,17},{9,25},{17,1},{25,9},{2,18},{10... | collective-permute-start | bytes 393224 | tf_op jit(solution)/shard_map/ppermute | solution.py:896
  154.1 7.8 %collective-permute-start.14 = (bf16[64,1024]{1,0:T(8,128)(2,1)}, bf16[64,1024]{1,0:T(8,128)(2,1)S(1)}, u32[]{:S(2)}, u32[]{:S(2)}) collective-permute-start(bf16[64,1024]{1,0:T(8,128)(2,1)} %get-tuple-element.176), channel_id=1, source_target_pairs={{0,24},{8,16},{16,8},{24,0},{1,25},{9,17},{17,9},{25,1},{2,26},{10... | collective-permute-start | bytes 393224 | tf_op jit(solution)/shard_map/ppermute | solution.py:896
  155.3 64.0 %collective-permute-start.18 = (bf16[768,640]{1,0:T(8,128)(2,1)}, bf16[768,640]{1,0:T(8,128)(2,1)S(1)}, u32[]{:S(2)}, u32[]{:S(2)}) collective-permute-start(bf16[768,640]{1,0:T(8,128)(2,1)} %get-tuple-element.201.refs_10_.refs_14_.refs_18_.refs_22_.refs_6_), channel_id=1, source_target_pairs={{0,8},{8,0},{16,24},{24,16},{1,9},{9,1},{17,25},{25,17},{2,10},{10... | collective-permute-start | bytes 2949128 | tf_op jit(solution)/shard_map/ppermute | solution.py:896
  191.1 16.9 %collective-permute-start.15 = (bf16[192,1024]{1,0:T(8,128)(2,1)}, bf16[192,1024]{1,0:T(8,128)(2,1)S(1)}, u32[]{:S(2)}, u32[]{:S(2)}) collective-permute-start(bf16[192,1024]{1,0:T(8,128)(2,1)} %get-tuple-element.188), channel_id=1, source_target_pairs={{0,8},{8,0},{16,24},{24,16},{1,9},{9,1},{17,25},{25,17},{2,10},{10... | collective-permute-start | bytes 1179656 | tf_op jit(solution)/shard_map/ppermute | solution.py:896
  191.5 16.6 %collective-permute-start.16 = (bf16[192,1024]{1,0:T(8,128)(2,1)}, bf16[192,1024]{1,0:T(8,128)(2,1)S(1)}, u32[]{:S(2)}, u32[]{:S(2)}) collective-permute-start(bf16[192,1024]{1,0:T(8,128)(2,1)} %get-tuple-element.189), channel_id=1, source_target_pairs={{0,16},{8,24},{16,0},{24,8},{1,17},{9,25},{17,1},{25,9},{2,18},{10... | collective-permute-start | bytes 1179656 | tf_op jit(solution)/shard_map/ppermute | solution.py:896
  191.8 19.2 %collective-permute-start.17 = (bf16[192,1024]{1,0:T(8,128)(2,1)}, bf16[192,1024]{1,0:T(8,128)(2,1)S(1)}, u32[]{:S(2)}, u32[]{:S(2)}) collective-permute-start(bf16[192,1024]{1,0:T(8,128)(2,1)} %get-tuple-element.190), channel_id=1, source_target_pairs={{0,24},{8,16},{16,8},{24,0},{1,25},{9,17},{17,9},{25,1},{2,26},{10... | collective-permute-start | bytes 1179656 | tf_op jit(solution)/shard_map/ppermute | solution.py:896
  211.7 59.0 %all-to-all-start.1 = ((bf16[8,144,768]{2,1,0:T(8,128)(2,1)}), bf16[8,144,768]{2,1,0:T(8,128)(2,1)S(1)}, u32[]{:S(2)}, u32[]{:S(2)}) async-start(bf16[8,144,768]{2,1,0:T(8,128)(2,1)} %bitcast.26), calls=%async_computation.1 | async-start | bytes 3538944 | tf_op jit(solution)/shard_map/all_to_all | solution.py:970
  217.1 42.3 %collective-permute-start.19 = (bf16[768,768]{1,0:T(8,128)(2,1)}, bf16[768,768]{1,0:T(8,128)(2,1)S(1)}, u32[]{:S(2)}, u32[]{:S(2)}) collective-permute-start(bf16[768,768]{1,0:T(8,128)(2,1)} %get-tuple-element.204), channel_id=1, source_target_pairs={{0,8},{8,0},{16,24},{24,16},{1,9},{9,1},{17,25},{25,17},{2,10},{10... | collective-permute-start | bytes 3538952 | tf_op jit(solution)/shard_map/ppermute | solution.py:896
  217.5 42.0 %collective-permute-start.20 = (bf16[768,768]{1,0:T(8,128)(2,1)}, bf16[768,768]{1,0:T(8,128)(2,1)S(1)}, u32[]{:S(2)}, u32[]{:S(2)}) collective-permute-start(bf16[768,768]{1,0:T(8,128)(2,1)} %get-tuple-element.205), channel_id=1, source_target_pairs={{0,16},{8,24},{16,0},{24,8},{1,17},{9,25},{17,1},{25,9},{2,18},{10... | collective-permute-start | bytes 3538952 | tf_op jit(solution)/shard_map/ppermute | solution.py:896
  217.5 53.3 %collective-permute-start.21 = (bf16[768,768]{1,0:T(8,128)(2,1)}, bf16[768,768]{1,0:T(8,128)(2,1)}, u32[]{:S(2)}, u32[]{:S(2)}) collective-permute-start(bf16[768,768]{1,0:T(8,128)(2,1)} %get-tuple-element.206), channel_id=1, source_target_pairs={{0,24},{8,16},{16,8},{24,0},{1,25},{9,17},{17,9},{25,1},{2,26},{10... | collective-permute-start | bytes 3538952 | tf_op jit(solution)/shard_map/ppermute | solution.py:896
  276.2 47.1 %collective-permute-start.22 = (bf16[192,1024]{1,0:T(8,128)(2,1)}, bf16[192,1024]{1,0:T(8,128)(2,1)S(1)}, u32[]{:S(2)}, u32[]{:S(2)}) collective-permute-start(bf16[192,1024]{1,0:T(8,128)(2,1)} %get-tuple-element.211), channel_id=1, source_target_pairs={{0,8},{8,0},{16,24},{24,16},{1,9},{9,1},{17,25},{25,17},{2,10},{10... | collective-permute-start | bytes 1179656 | tf_op jit(solution)/shard_map/ppermute | solution.py:896
  276.3 47.1 %collective-permute-start.23 = (bf16[192,1024]{1,0:T(8,128)(2,1)}, bf16[192,1024]{1,0:T(8,128)(2,1)S(1)}, u32[]{:S(2)}, u32[]{:S(2)}) collective-permute-start(bf16[192,1024]{1,0:T(8,128)(2,1)} %get-tuple-element.212), channel_id=1, source_target_pairs={{0,16},{8,24},{16,0},{24,8},{1,17},{9,25},{17,1},{25,9},{2,18},{10... | collective-permute-start | bytes 1179656 | tf_op jit(solution)/shard_map/ppermute | solution.py:896
  276.3 47.1 %collective-permute-start.24 = (bf16[192,1024]{1,0:T(8,128)(2,1)}, bf16[192,1024]{1,0:T(8,128)(2,1)S(1)}, u32[]{:S(2)}, u32[]{:S(2)}) collective-permute-start(bf16[192,1024]{1,0:T(8,128)(2,1)} %get-tuple-element.213), channel_id=1, source_target_pairs={{0,24},{8,16},{16,8},{24,0},{1,25},{9,17},{17,9},{25,1},{2,26},{10... | collective-permute-start | bytes 1179656 | tf_op jit(solution)/shard_map/ppermute | solution.py:896
  278.4 45.1 %all-to-all-start.2 = ((bf16[8,96,768]{2,1,0:T(8,128)(2,1)}), bf16[8,96,768]{2,1,0:T(8,128)(2,1)S(1)}, u32[]{:S(2)}, u32[]{:S(2)}) async-start(bf16[8,96,768]{2,1,0:T(8,128)(2,1)} %bitcast.28), calls=%async_computation.2 | async-start | bytes 2359296 | tf_op jit(solution)/shard_map/all_to_all | solution.py:970
  327.8 49.5 %collective-permute-start.28 = (bf16[240,768]{1,0:T(8,128)(2,1)}, bf16[240,768]{1,0:T(8,128)(2,1)S(1)}, u32[]{:S(2)}, u32[]{:S(2)}) collective-permute-start(bf16[240,768]{1,0:T(8,128)(2,1)} %get-tuple-element.228.refs_13_.refs_10_), channel_id=1, source_target_pairs={{0,16},{8,24},{16,0},{24,8},{1,17},{9,25},{17,1},{25,9},{2,18},{10... | collective-permute-start | bytes 1105928 | tf_op jit(solution)/shard_map/ppermute | solution.py:896
  327.8 49.5 %collective-permute-start.29 = (bf16[240,768]{1,0:T(8,128)(2,1)}, bf16[240,768]{1,0:T(8,128)(2,1)S(1)}, u32[]{:S(2)}, u32[]{:S(2)}) collective-permute-start(bf16[240,768]{1,0:T(8,128)(2,1)} %get-tuple-element.228.refs_13_.refs_10_), channel_id=1, source_target_pairs={{0,24},{8,16},{16,8},{24,0},{1,25},{9,17},{17,9},{25,1},{2,26},{10... | collective-permute-start | bytes 1105928 | tf_op jit(solution)/shard_map/ppermute | solution.py:896
  329.7 47.6 %collective-permute-start.25 = (bf16[192,1024]{1,0:T(8,128)(2,1)}, bf16[192,1024]{1,0:T(8,128)(2,1)S(1)}, u32[]{:S(2)}, u32[]{:S(2)}) collective-permute-start(bf16[192,1024]{1,0:T(8,128)(2,1)} %get-tuple-element.225), channel_id=1, source_target_pairs={{0,8},{8,0},{16,24},{24,16},{1,9},{9,1},{17,25},{25,17},{2,10},{10... | collective-permute-start | bytes 1179656 | tf_op jit(solution)/shard_map/ppermute | solution.py:896
  329.7 47.6 %collective-permute-start.26 = (bf16[192,1024]{1,0:T(8,128)(2,1)}, bf16[192,1024]{1,0:T(8,128)(2,1)S(1)}, u32[]{:S(2)}, u32[]{:S(2)}) collective-permute-start(bf16[192,1024]{1,0:T(8,128)(2,1)} %get-tuple-element.226), channel_id=1, source_target_pairs={{0,16},{8,24},{16,0},{24,8},{1,17},{9,25},{17,1},{25,9},{2,18},{10... | collective-permute-start | bytes 1179656 | tf_op jit(solution)/shard_map/ppermute | solution.py:896
  329.8 47.5 %collective-permute-start.27 = (bf16[192,1024]{1,0:T(8,128)(2,1)}, bf16[192,1024]{1,0:T(8,128)(2,1)S(1)}, u32[]{:S(2)}, u32[]{:S(2)}) collective-permute-start(bf16[192,1024]{1,0:T(8,128)(2,1)} %get-tuple-element.227), channel_id=1, source_target_pairs={{0,24},{8,16},{16,8},{24,0},{1,25},{9,17},{17,9},{25,1},{2,26},{10... | collective-permute-start | bytes 1179656 | tf_op jit(solution)/shard_map/ppermute | solution.py:896
  331.8 45.5 %all-to-all-start.3 = ((bf16[8,96,512]{2,1,0:T(8,128)(2,1)}), bf16[8,96,512]{2,1,0:T(8,128)(2,1)S(1)}, u32[]{:S(2)}, u32[]{:S(2)}) async-start(bf16[8,96,512]{2,1,0:T(8,128)(2,1)} %bitcast.25), calls=%async_computation.3 | async-start | bytes 1572864 | tf_op jit(solution)/shard_map/all_to_all | solution.py:970
  378.8 11.1 %copy-start.27 = (bf16[192,1024]{1,0:T(8,128)(2,1)S(1)}, bf16[192,1024]{1,0:T(8,128)(2,1)}, u32[]{:S(2)}) copy-start(bf16[192,1024]{1,0:T(8,128)(2,1)} %get-tuple-element.243) | copy-start | bytes 1179652
  378.8 11.8 %copy-start.28 = (bf16[192,1024]{1,0:T(8,128)(2,1)S(1)}, bf16[192,1024]{1,0:T(8,128)(2,1)}, u32[]{:S(2)}) copy-start(bf16[192,1024]{1,0:T(8,128)(2,1)} %get-tuple-element.244) | copy-start | bytes 1179652
  378.8 12.2 %copy-start.29 = (bf16[192,1024]{1,0:T(8,128)(2,1)S(1)}, bf16[192,1024]{1,0:T(8,128)(2,1)}, u32[]{:S(2)}) copy-start(bf16[192,1024]{1,0:T(8,128)(2,1)} %get-tuple-element.245) | copy-start | bytes 1179652
  378.8 1.9 collective-permute-start.30
  384.3 25.6 %all-to-all-start.4 = ((bf16[8,96,256]{2,1,0:T(8,128)(2,1)}), bf16[8,96,256]{2,1,0:T(8,128)(2,1)S(1)}, u32[]{:S(2)}, u32[]{:S(2)}) async-start(bf16[8,96,256]{2,1,0:T(8,128)(2,1)} %bitcast.27), calls=%async_computation.4 | async-start | bytes 786432 | tf_op jit(solution)/shard_map/all_to_all | solution.py:970
  389.9 12.0 %collective-permute-start.31 = (bf16[192,1024]{1,0:T(8,128)(2,1)S(1)}, bf16[192,1024]{1,0:T(8,128)(2,1)S(1)}, u32[]{:S(2)}, u32[]{:S(2)}) collective-permute-start(bf16[192,1024]{1,0:T(8,128)(2,1)S(1)} %copy-done.27), channel_id=1, source_target_pairs={{0,8},{8,0},{16,24},{24,16},{1,9},{9,1},{17,25},{25,17},{2,10},{10... | collective-permute-start | bytes 1179656 | tf_op jit(solution)/shard_map/ppermute | solution.py:896
  390.6 11.4 %collective-permute-start.32 = (bf16[192,1024]{1,0:T(8,128)(2,1)S(1)}, bf16[192,1024]{1,0:T(8,128)(2,1)S(1)}, u32[]{:S(2)}, u32[]{:S(2)}) collective-permute-start(bf16[192,1024]{1,0:T(8,128)(2,1)S(1)} %copy-done.28), channel_id=1, source_target_pairs={{0,16},{8,24},{16,0},{24,8},{1,17},{9,25},{17,1},{25,9},{2,18},{10... | collective-permute-start | bytes 1179656 | tf_op jit(solution)/shard_map/ppermute | solution.py:896
  391.0 18.9 %collective-permute-start.33 = (bf16[192,1024]{1,0:T(8,128)(2,1)S(1)}, bf16[192,1024]{1,0:T(8,128)(2,1)S(1)}, u32[]{:S(2)}, u32[]{:S(2)}) collective-permute-start(bf16[192,1024]{1,0:T(8,128)(2,1)S(1)} %copy-done.29), channel_id=1, source_target_pairs={{0,24},{8,16},{16,8},{24,0},{1,25},{9,17},{17,9},{25,1},{2,26},{10... | collective-permute-start | bytes 1179656 | tf_op jit(solution)/shard_map/ppermute | solution.py:896
  401.9 7.9 %copy-start.17 = (bf16[192,1024]{1,0:T(8,128)(2,1)}, bf16[192,1024]{1,0:T(8,128)(2,1)S(1)}, u32[]{:S(2)}) copy-start(bf16[192,1024]{1,0:T(8,128)(2,1)S(1)} %collective-permute-done.31.refs_1_) | copy-start | bytes 1179652
  401.9 7.9 %copy-start.18 = (bf16[192,1024]{1,0:T(8,128)(2,1)}, bf16[192,1024]{1,0:T(8,128)(2,1)S(1)}, u32[]{:S(2)}) copy-start(bf16[192,1024]{1,0:T(8,128)(2,1)S(1)} %collective-permute-done.32.refs_2_) | copy-start | bytes 1179652
  413.4 9.9 %collective-permute-start.34 = (bf16[96,768]{1,0:T(8,128)(2,1)}, bf16[96,768]{1,0:T(8,128)(2,1)S(1)}, u32[]{:S(2)}, u32[]{:S(2)}) collective-permute-start(bf16[96,768]{1,0:T(8,128)(2,1)} %beside.1.refs_3_), channel_id=1, source_target_pairs={{0,8},{8,0},{16,24},{24,16},{1,9},{9,1},{17,25},{25,17},{2,10},{10... | collective-permute-start | bytes 442376 | tf_op jit(solution)/shard_map/ppermute | solution.py:896
  413.6 9.7 %collective-permute-start.35 = (bf16[96,768]{1,0:T(8,128)(2,1)}, bf16[96,768]{1,0:T(8,128)(2,1)S(1)}, u32[]{:S(2)}, u32[]{:S(2)}) collective-permute-start(bf16[96,768]{1,0:T(8,128)(2,1)} %beside.1.refs_3_), channel_id=1, source_target_pairs={{0,16},{8,24},{16,0},{24,8},{1,17},{9,25},{17,1},{25,9},{2,18},{10... | collective-permute-start | bytes 442376 | tf_op jit(solution)/shard_map/ppermute | solution.py:896
  414.0 9.3 %collective-permute-start.36 = (bf16[96,768]{1,0:T(8,128)(2,1)}, bf16[96,768]{1,0:T(8,128)(2,1)S(1)}, u32[]{:S(2)}, u32[]{:S(2)}) collective-permute-start(bf16[96,768]{1,0:T(8,128)(2,1)} %beside.1.refs_3_), channel_id=1, source_target_pairs={{0,24},{8,16},{16,8},{24,0},{1,25},{9,17},{17,9},{25,1},{2,26},{10... | collective-permute-start | bytes 442376 | tf_op jit(solution)/shard_map/ppermute | solution.py:896
  (38 other events, 47.0 us)
Sparse Core Ops, SparseCore 0:
  42.4 64.4 all-gather.1

commit v3 on v2

--- a/solution.py
+++ b/solution.py
@@ -16,6 +16,8 @@
 masked_score = -1e30
 LOG2E = 1.4426950408889634
 LN2 = 0.6931471805599453
+
+VMEM = 63 * 2**20
 
 bf = jnp.bfloat16
 f32 = jnp.float32
@@ -80,7 +82,7 @@
 def qkv_call(block, blocks, heads, info, x, cos, sin, w, carried):
     rows = x.shape[0]
     S = rows * blocks
-    rb = min(256, rows)
+    rb = min(512, rows)
     steps = rows // rb
     width = w.shape[1]
     at = lambda i: block * steps + i
@@ -119,7 +121,7 @@
         ),
         scratch_shapes=[pltpu.VMEM((8, D), f32)],
         input_output_aliases=aliases,
-        compiler_params=pltpu.CompilerParams(vmem_limit_bytes=48 * 2**20),
+        compiler_params=pltpu.CompilerParams(vmem_limit_bytes=VMEM),
         cost_estimate=pl.CostEstimate(
             flops=4 * rows * D * width, bytes_accessed=rows * 8192, transcendentals=0
         ),
@@ -222,7 +224,7 @@
             pltpu.VMEM((S, bq), f32),
             pltpu.VMEM((2, 8, bq), f32),
         ],
-        compiler_params=pltpu.CompilerParams(vmem_limit_bytes=58 * 2**20),
+        compiler_params=pltpu.CompilerParams(vmem_limit_bytes=VMEM),
         cost_estimate=pl.CostEstimate(
             flops=16 * HD * S * S, bytes_accessed=2 * S * S, transcendentals=S * S
         ),
@@ -340,7 +342,7 @@
             pltpu.SemaphoreType.DMA,
         ],
         input_output_aliases={} if earlier is None else {12 + groups: groups},
-        compiler_params=pltpu.CompilerParams(vmem_limit_bytes=58 * 2**20),
+        compiler_params=pltpu.CompilerParams(vmem_limit_bytes=VMEM),
         cost_estimate=pl.CostEstimate(
             flops=24 * HD * S * S, bytes_accessed=2 * S * S, transcendentals=0
         ),
@@ -398,6 +400,7 @@
         + [vmem] * 4
         + [pl.BlockSpec(memory_space=pl.ANY)] * len(after),
         out_specs=vmem,
+        compiler_params=pltpu.CompilerParams(vmem_limit_bytes=VMEM),
         name="own_half",
     )(info, in_w, proj_w, gain, out_w, *after)
 
@@ -412,6 +415,7 @@
         in_specs=[pl.BlockSpec(memory_space=pl.ANY)] * (1 + len(after)),
         out_specs=pl.BlockSpec(memory_space=pl.ANY),
         input_output_aliases={0: 0},
+        compiler_params=pltpu.CompilerParams(vmem_limit_bytes=VMEM),
         name="hold",
     )(array, *after)
 
@@ -551,7 +555,7 @@
             pltpu.VMEM(mine.shape, bf),
             pltpu.SemaphoreType.DMA((2,)),
         ],
-        compiler_params=pltpu.CompilerParams(vmem_limit_bytes=58 * 2**20),
+        compiler_params=pltpu.CompilerParams(vmem_limit_bytes=VMEM),
         cost_estimate=pl.CostEstimate(
             flops=rows * D * (14 * ff + 4 * D), bytes_accessed=30 * 2**20, transcendentals=rows * ff
         ),
@@ -618,7 +622,7 @@
             pltpu.VMEM((D, len(chosen) * D), bf),
             pltpu.VMEM((8, D), f32),
         ],
-        compiler_params=pltpu.CompilerParams(vmem_limit_bytes=58 * 2**20),
+        compiler_params=pltpu.CompilerParams(vmem_limit_bytes=VMEM),
         cost_estimate=pl.CostEstimate(
             flops=2 * len(chosen) * rows * D * D, bytes_accessed=12 * 2**20, transcendentals=0
         ),
@@ -657,6 +661,7 @@
             pl.BlockSpec(memory_space=pltpu.VMEM),
         ],
         out_specs=pl.BlockSpec(memory_space=pltpu.VMEM),
+        compiler_params=pltpu.CompilerParams(vmem_limit_bytes=VMEM),
         name="own_columns",
     )(info, w, gain)
 
@@ -681,6 +686,7 @@
         in_specs=[pl.BlockSpec((half, rb), lambda i: (0, i))] * 2,
         out_specs=(pl.BlockSpec((rb, 4 * half), lambda i: (i, 0)),) * 2
         + (pl.BlockSpec((2 * half, rb), lambda i: (0, i)),) * 2,
+        compiler_params=pltpu.CompilerParams(vmem_limit_bytes=VMEM),
         name="tables",
     )(cosine, sine)
 
@@ -735,7 +741,7 @@
         ),
         out_shape=(jax.ShapeDtypeStruct((D, D), bf),) * (steps + 1)
         + (jax.ShapeDtypeStruct((ff, D), bf),),
-        compiler_params=pltpu.CompilerParams(vmem_limit_bytes=58 * 2**20),
+        compiler_params=pltpu.CompilerParams(vmem_limit_bytes=VMEM),
         cost_estimate=pl.CostEstimate(
             flops=2 * rows * D * (D * (steps + 1) + ff), bytes_accessed=20 * 2**20, transcendentals=0
         ),
@@ -763,7 +769,7 @@
         out_specs=tuple(out_specs) + (anywhere,) * len(carry),
         scratch_shapes=list(scratch),
         input_output_aliases={first + n: own + n for n in range(len(carry))},
-        compiler_params=pltpu.CompilerParams(vmem_limit_bytes=58 * 2**20),
+        compiler_params=pltpu.CompilerParams(vmem_limit_bytes=VMEM),
         name=name,
     )(*arrays, *after, *carry)
     return list(outs[:own]), list(outs[own:])
@@ -809,7 +815,7 @@
         out_shape=jax.ShapeDtypeStruct((first.shape[1], first.shape[2] + second.shape[2]), bf),
         in_specs=[vmem, vmem] + [pl.BlockSpec(memory_space=pl.ANY)] * len(after),
         out_specs=vmem,
-        compiler_params=pltpu.CompilerParams(vmem_limit_bytes=58 * 2**20),
+        compiler_params=pltpu.CompilerParams(vmem_limit_bytes=VMEM),
         name="beside",
     )(first, second, *after)
 

time: 438 us -> 436 us (level)
  local copies, waits for them, and re-layouts: 18.6 us -> 8.16 us
    unnamed x86 -> x30, local copies, waits for them, and re-layouts: 18.6 us -> 8.16 us
  transfers between devices with their start and end apart: 43 -> 43, of which waited for: 8 -> 8; matrix products, arithmetic and copies ran while one was open for 1% -> 1% of each run, Pallas kernels for 63% -> 64%
where the time goes in v3:
time: 436 us; the launch traced here: 428 us
  Pallas kernels  289 us (66%)
  starting transfers between devices  58.1 us (13%)
  waiting for transfers between devices  52.4 us (12%)
  between operations  15.4 us (4%)
  local copies, waits for them, and re-layouts  8.16 us (2%)
  other arithmetic  4.58 us (1%)
    pallas_call x3, Pallas kernels, attend_back(): pl.pallas_call(functools.partial(attend_back_kernel, kc, groups), grid=(g...  117 us
    pallas_call x3, Pallas kernels, attend(): pl.pallas_call(functools.partial(attend_kernel, kc, groups, len(after)),...  62.5 us
    ppermute x37, waiting for transfers between devices, swap(): return lax.ppermute(array, axis, [(i, i ^ j) for i in range(size)])  38 us
    ppermute x37, starting transfers between devices, swap(): return lax.ppermute(array, axis, [(i, i ^ j) for i in range(size)])  28.6 us
    pallas_call x1, Pallas kernels, middle(): pl.pallas_call(functools.partial(middle_kernel, groups, heads, ff, shards...  28.6 us
    pallas_call x4, Pallas kernels, qkv_call(): pl.pallas_call(functools.partial(qkv_kernel, heads), grid=(steps,), out_s...  25.4 us
    all_to_all x4, starting transfers between devices, to_owner(): lax.all_to_all(parts, 'fsdp', split_axis=0, concat_axis=0, tiled=True)  23.1 us
    pallas_call x2, Pallas kernels, last(): pl.pallas_call(functools.partial(last_kernel, groups, chosen), grid=(rows...  17.3 us
  transfers between devices with their start and end apart: 43, of which 8 were waited for; matrix products, arithmetic and copies ran while one was open for 1% of the time, Pallas kernels for 64%

profile of v3, /device:TPU:1, one launch (start us, length us, event | category | flops | bytes accessed | tf_op | source)
XLA Modules:
  0.0 428.0 jit_solution(9949777732857081424)
XLA Ops:
  7.2 2.2 own_columns.1
  9.3 6.4 %all-to-all-start = ((bf16[8,96,640]{2,1,0:T(8,128)(2,1)}), bf16[8,96,640]{2,1,0:T(8,128)(2,1)S(1)}, u32[]{:S(2)}, u32[]{:S(2)}) async-start(bf16[8,96,640]{2,1,0:T(8,128)(2,1)} %own_columns.1), calls=%async_computation | async-start | bytes 1966080 | tf_op jit(solution)/shard_map/all_to_all | solution.py:917
  15.7 1.3 collective-permute-start
  17.1 2.8 multiply_sine_fusion
  19.9 4.8 %tables.1 = (f32[4096,128]{1,0:T(8,128)}, f32[4096,128]{1,0:T(8,128)}, f32[64,4096]{1,0:T(8,128)}, f32[64,4096]{1,0:T(8,128)}) custom-call(f32[32,4096]{1,0:T(8,128)} %get-tuple-element.253.cos_ref, f32[32,4096]{1,0:T(8,128)} %get-tuple-element.252.sin_ref), custom_call_target="tpu_custom_call" | custom-call | tf_op jit(solution)/shard_map/tables/pallas_call | solution.py:681
  24.6 14.3 %all-to-all-done = bf16[8,96,640]{2,1,0:T(8,128)(2,1)S(1)} async-done(((bf16[8,96,640]{2,1,0:T(8,128)(2,1)}), bf16[8,96,640]{2,1,0:T(8,128)(2,1)S(1)}, u32[]{:S(2)}, u32[]{:S(2)}) %all-to-all-start) | async-done | bytes 983072 | tf_op jit(solution)/shard_map/all_to_all | solution.py:917
  39.9 2.1 own_half.1
  42.0 2.0 collective-permute-start.2
  44.0 7.0 %collective-permute-done.x_ref = bf16[1024,768]{1,0:T(8,128)(2,1)} collective-permute-done((bf16[1024,768]{1,0:T(8,128)(2,1)}, bf16[1024,768]{1,0:T(8,128)(2,1)}, u32[]{:S(2)}, u32[]{:S(2)}) %collective-permute-start) | collective-permute-done | bytes 1572896 | tf_op jit(solution)/shard_map/ppermute | solution.py:902
  51.1 1.9 collective-permute-start.1
  55.3 6.4 %qkv.4 = (bf16[4096,768]{1,0:T(8,128)(2,1)}, bf16[3,4096,128]{2,1,0:T(8,128)(2,1)}, bf16[3,4096,128]{2,1,0:T(8,128)(2,1)}, bf16[3,128,4096]{2,1,0:T(8,128)(2,1)}...) custom-call(s32[2]{0:T(128)} %get-tuple-element.255.info_ref, bf16[1024,768]{1,0:T(8,128)(2,1)} %collective-permute-done.x_ref, ...), custom_call_target="tpu_custom_call" | custom-call | flops 2013265920 | bytes 8388608 | tf_op jit(solution)/shard_map/qkv/pallas_call | solution.py:109
  61.7 6.4 %qkv.5 = (bf16[4096,768]{1,0:T(8,128)(2,1)}, bf16[3,4096,128]{2,1,0:T(8,128)(2,1)}, bf16[3,4096,128]{2,1,0:T(8,128)(2,1)}, bf16[3,128,4096]{2,1,0:T(8,128)(2,1)}...) custom-call(s32[2]{0:T(128)} %get-tuple-element.254.info_ref, ...), custom_call_target="tpu_custom_call", output_to_operand_aliasing={{0}: (5, {}), {1}: (6, {}), {2}: (7, {}), {3}: (8, {}), {4}... | custom-call | flops 2013265920 | bytes 8388608 | tf_op jit(solution)/shard_map/qkv/pallas_call | solution.py:109
  68.1 6.3 %qkv.6 = (bf16[4096,768]{1,0:T(8,128)(2,1)}, bf16[3,4096,128]{2,1,0:T(8,128)(2,1)}, bf16[3,4096,128]{2,1,0:T(8,128)(2,1)}, bf16[3,128,4096]{2,1,0:T(8,128)(2,1)}...) custom-call(s32[2]{0:T(128)} %pad_add_fusion.1.info_ref, ...), custom_call_target="tpu_custom_call", output_to_operand_aliasing={{0}: (5, {}), {1}: (6, {}), {2}: (7, {}), {3}: (8, {}), {4}... | custom-call | flops 2013265920 | bytes 8388608 | tf_op jit(solution)/shard_map/qkv/pallas_call | solution.py:109
  74.4 6.4 %qkv.7 = (bf16[4096,768]{1,0:T(8,128)(2,1)}, bf16[3,4096,128]{2,1,0:T(8,128)(2,1)}, bf16[3,4096,128]{2,1,0:T(8,128)(2,1)}, bf16[3,128,4096]{2,1,0:T(8,128)(2,1)}...) custom-call(s32[2]{0:T(128)} %pad_add_fusion.info_ref, ...), custom_call_target="tpu_custom_call", output_to_operand_aliasing={{0}: (5, {}), {1}: (6, {}), {2}: (7, {}), {3}: (8, {}), {4}... | custom-call | flops 2013265920 | bytes 8388608 | tf_op jit(solution)/shard_map/qkv/pallas_call | solution.py:109
  80.9 1.3 collective-permute-start.4
  82.2 21.0 %attend.3 = (bf16[4,4096,512]{2,1,0:T(8,128)(2,1)}, bf16[4,4096,512]{2,1,0:T(8,128)(2,1)}, f32[64,2048]{1,0:T(8,128)}, f32[64,2048]{1,0:T(8,128)}, f32[4,1,512]{...) custom-call(bf16[3,4096,128]{2,1,0:T(8,128)(2,1)} %get-tuple-element, ...), custom_call_target="tpu_custom_call" | custom-call | flops 17179869184 | bytes 33554432 | tf_op jit(solution)/shard_map/attend/pallas_call | solution.py:199
  104.2 1.5 collective-permute-start.7
  106.7 20.7 %attend.4 = (bf16[4,4096,512]{2,1,0:T(8,128)(2,1)}, bf16[4,4096,512]{2,1,0:T(8,128)(2,1)}, f32[64,2048]{1,0:T(8,128)}, f32[64,2048]{1,0:T(8,128)}, f32[4,1,512]{...) custom-call(bf16[3,4096,128]{2,1,0:T(8,128)(2,1)} %get-tuple-element, ...), custom_call_target="tpu_custom_call" | custom-call | flops 17179869184 | bytes 33554432 | tf_op jit(solution)/shard_map/attend/pallas_call | solution.py:199
  129.7 20.7 %attend.5 = (bf16[4,4096,512]{2,1,0:T(8,128)(2,1)}, bf16[4,4096,512]{2,1,0:T(8,128)(2,1)}, f32[64,2048]{1,0:T(8,128)}, f32[64,2048]{1,0:T(8,128)}, f32[4,1,512]{...) custom-call(bf16[3,4096,128]{2,1,0:T(8,128)(2,1)} %get-tuple-element, ...), custom_call_target="tpu_custom_call" | custom-call | flops 17179869184 | bytes 33554432 | tf_op jit(solution)/shard_map/attend/pallas_call | solution.py:199
  153.5 3.6 collective-permute-done.13.refs_10_
  157.1 2.9 collective-permute-done.14.refs_11_
  160.0 28.6 %middle.1 = (bf16[192,1024]{1,0:T(8,128)(2,1)}, bf16[192,1024]{1,0:T(8,128)(2,1)}, bf16[192,1024]{1,0:T(8,128)(2,1)}, bf16[192,1024]{1,0:T(8,128)(2,1)}, bf16[10...) custom-call(s32[1]{0:T(128)} %bitcast.info_ref.place_ref.refs_0_, ...), custom_call_target="tpu_custom_call" | custom-call | flops 15099494400 | bytes 31457280 | tf_op jit(solution)/shard_map/middle/pallas_call | solution.py:518
  189.2 1.6 collective-permute-start.17
  190.8 14.9 %weight_grads.1 = (bf16[768,768]{1,0:T(8,128)(2,1)}, bf16[768,768]{1,0:T(8,128)(2,1)}, bf16[768,768]{1,0:T(8,128)(2,1)}, bf16[768,768]{1,0:T(8,128)(2,1)}, bf16[1152,768]{1,0:T(8,128)(2,1)}) custom-call(s32[1]{0:T(128)} %bitcast.info_ref.place_ref.refs_0_, bf16[1024,768]{1,0:T(8,128)(2,1)} %get-tuple-element.191.second_ref, ...), custom_call_target="tpu_custom_call" | custom-call | flops 6643777536 | bytes 20971520 | tf_op jit(solution)/shard_map/weight_grads/pallas_call | solution.py:725
  205.7 2.8 collective-permute-done.17.refs_2_.refs_12_
  208.6 5.3 %all-to-all-start.1 = ((bf16[8,144,768]{2,1,0:T(8,128)(2,1)}), bf16[8,144,768]{2,1,0:T(8,128)(2,1)}, u32[]{:S(2)}, u32[]{:S(2)}) async-start(bf16[8,144,768]{2,1,0:T(8,128)(2,1)} %bitcast.32), calls=%async_computation.1 | async-start | bytes 3538944 | tf_op jit(solution)/shard_map/all_to_all | solution.py:976
  214.3 1.7 collective-permute-start.21
  217.0 39.0 %attend_back.3 = (bf16[192,1024]{1,0:T(8,128)(2,1)}, bf16[192,1024]{1,0:T(8,128)(2,1)}, bf16[192,1024]{1,0:T(8,128)(2,1)}, bf16[192,1024]{1,0:T(8,128)(2,1)}, bf16[768,512]{1,0:T(8,128)(2,1)}) custom-call(bf16[3,4096,128]{2,1,0:T(8,128)(2,1)} %get-tuple-element.179.v_ref, bf16[3,64,4096]{2,1,0:T(8,128)(2,1)} %get-tuple-element.180.kt_ref, ...), custom_call_target="tpu_custom_call" | custom-call | flops 25769803776 | bytes 33554432 | tf_op jit(solution)/shard_map/attend_back/pallas_call | solution.py:315
  256.0 11.5 %collective-permute-done.21.refs_3_ = bf16[768,768]{1,0:T(8,128)(2,1)} collective-permute-done((bf16[768,768]{1,0:T(8,128)(2,1)}, bf16[768,768]{1,0:T(8,128)(2,1)}, u32[]{:S(2)}, u32[]{:S(2)}) %collective-permute-start.21) | collective-permute-done | bytes 1179680 | tf_op jit(solution)/shard_map/ppermute | solution.py:902
  267.5 4.2 add_up.1
  271.8 2.0 collective-permute-start.24
  273.9 6.2 %all-to-all-start.2 = ((bf16[8,96,768]{2,1,0:T(8,128)(2,1)}), bf16[8,96,768]{2,1,0:T(8,128)(2,1)}, u32[]{:S(2)}, u32[]{:S(2)}) async-start(bf16[8,96,768]{2,1,0:T(8,128)(2,1)} %bitcast.34), calls=%async_computation.2 | async-start | bytes 2359296 | tf_op jit(solution)/shard_map/all_to_all | solution.py:976
  280.1 39.0 %attend_back.4 = (bf16[192,1024]{1,0:T(8,128)(2,1)}, bf16[192,1024]{1,0:T(8,128)(2,1)}, bf16[192,1024]{1,0:T(8,128)(2,1)}, bf16[192,1024]{1,0:T(8,128)(2,1)}, bf16[768,512]{1,0:T(8,128)(2,1)}) custom-call(bf16[3,4096,128]{2,1,0:T(8,128)(2,1)} %get-tuple-element.179.v_ref, ...), custom_call_target="tpu_custom_call", output_to_operand_aliasing={{4}: (16, {})} | custom-call | flops 25769803776 | bytes 33554432 | tf_op jit(solution)/shard_map/attend_back/pallas_call | solution.py:315
  320.0 3.0 owned.1
  323.0 1.8 collective-permute-start.29
  325.0 2.0 collective-permute-start.27
  327.0 5.9 %all-to-all-start.3 = ((bf16[8,96,512]{2,1,0:T(8,128)(2,1)}), bf16[8,96,512]{2,1,0:T(8,128)(2,1)S(1)}, u32[]{:S(2)}, u32[]{:S(2)}) async-start(bf16[8,96,512]{2,1,0:T(8,128)(2,1)} %bitcast.31), calls=%async_computation.3 | async-start | bytes 1572864 | tf_op jit(solution)/shard_map/all_to_all | solution.py:976
  332.9 39.2 %attend_back.5 = (bf16[192,1024]{1,0:T(8,128)(2,1)}, bf16[192,1024]{1,0:T(8,128)(2,1)}, bf16[192,1024]{1,0:T(8,128)(2,1)}, bf16[192,1024]{1,0:T(8,128)(2,1)}, bf16[768,256]{1,0:T(8,128)(2,1)}) custom-call(bf16[3,4096,128]{2,1,0:T(8,128)(2,1)} %get-tuple-element.179.v_ref, bf16[3,64,4096]{2,1,0:T(8,128)(2,1)} %get-tuple-element.180.kt_ref, ...), custom_call_target="tpu_custom_call" | custom-call | flops 25769803776 | bytes 33554432 | tf_op jit(solution)/shard_map/attend_back/pallas_call | solution.py:315
  373.1 1.9 collective-permute-done.30.refs_4_
  375.8 2.8 finish_wide.1
  378.6 5.7 %all-to-all-start.4 = ((bf16[8,96,256]{2,1,0:T(8,128)(2,1)}), bf16[8,96,256]{2,1,0:T(8,128)(2,1)S(1)}, u32[]{:S(2)}, u32[]{:S(2)}) async-start(bf16[8,96,256]{2,1,0:T(8,128)(2,1)} %bitcast.33), calls=%async_computation.4 | async-start | bytes 786432 | tf_op jit(solution)/shard_map/all_to_all | solution.py:976
  385.3 1.3 collective-permute-start.33
  386.6 9.6 %last.2.base_ref.refs_0_ = f32[1024,768]{1,0:T(8,128)} custom-call(bf16[1024,768]{1,0:T(8,128)(2,1)} %bitcast.28, f32[1024,768]{1,0:T(8,128)} %get-tuple-element.178.base_ref, bf16[768,640]{1,0:T(8,128)(2,1)} %hold.4.gain_ref.refs_8_.refs_12_.refs_16_.refs_20_.refs_4_, bf16[192,1024]{1,0:T(8,128)(2,1)} %get-tuple-element.202.refs_0_, ...), custom_call_target="tpu_custom_call" | custom-call | flops 2415919104 | bytes 12582912 | tf_op jit(solution)/shard_map/last/pallas_call | solution.py:606
  396.3 8.2 %collective-permute-done.33.refs_3_ = bf16[192,1024]{1,0:T(8,128)(2,1)} collective-permute-done((bf16[192,1024]{1,0:T(8,128)(2,1)}, bf16[192,1024]{1,0:T(8,128)(2,1)}, u32[]{:S(2)}, u32[]{:S(2)}) %collective-permute-start.33) | collective-permute-done | bytes 393248 | tf_op jit(solution)/shard_map/ppermute | solution.py:902
  405.3 2.1 beside.1.refs_3_
  407.9 1.5 collective-permute-start.36
  409.5 7.7 %last.3.refs_7_ = f32[1024,768]{1,0:T(8,128)} custom-call(bf16[1024,768]{1,0:T(8,128)(2,1)} %bitcast.29, f32[1024,768]{1,0:T(8,128)} %last.2.base_ref.refs_0_, bf16[768,640]{1,0:T(8,128)(2,1)} %hold.4.gain_ref.refs_8_.refs_12_.refs_16_.refs_20_.refs_4_, bf16[192,1024]{1,0:T(8,128)(2,1)} %get-tuple-element.242.refs_0_, bf16[192,1024]{1,0:T(8,128)(2,1)} %copy-done.7, ...), custom_call_target="tpu_custom_call" | custom-call | flops 1207959552 | bytes 12582912 | tf_op jit(solution)/shard_map/last/pallas_call | solution.py:606
  418.6 2.4 finish_qkv.1
  (105 shorter events, 18.8 us)
Async XLA Ops:
  9.3 29.6 %all-to-all-start = ((bf16[8,96,640]{2,1,0:T(8,128)(2,1)}), bf16[8,96,640]{2,1,0:T(8,128)(2,1)S(1)}, u32[]{:S(2)}, u32[]{:S(2)}) async-start(bf16[8,96,640]{2,1,0:T(8,128)(2,1)} %own_columns.1), calls=%async_computation | async-start | bytes 1966080 | tf_op jit(solution)/shard_map/all_to_all | solution.py:917
  15.7 111.8 %all-gather.2.cloned.1.call-start = ((), (), s32[]{:S(2)}) async-start(), calls=%async_computation.5 | async-start | bytes 3981312 | tf_op jit(solution)/shard_map/all_gather | solution.py:908
  15.7 35.3 %collective-permute-start = (bf16[1024,768]{1,0:T(8,128)(2,1)}, bf16[1024,768]{1,0:T(8,128)(2,1)}, u32[]{:S(2)}, u32[]{:S(2)}) collective-permute-start(bf16[1024,768]{1,0:T(8,128)(2,1)} %bitcast.24), channel_id=1, source_target_pairs={{0,16},{8,24},{16,0},{24,8},{1,17},{9,25},{17,1},{25,9},{2,18},{10... | collective-permute-start | bytes 4718600 | tf_op jit(solution)/shard_map/ppermute | solution.py:902
  38.9 1.0 copy-start
  42.0 26.0 %collective-permute-start.2 = (bf16[1024,768]{1,0:T(8,128)(2,1)}, bf16[1024,768]{1,0:T(8,128)(2,1)}, u32[]{:S(2)}, u32[]{:S(2)}) collective-permute-start(bf16[1024,768]{1,0:T(8,128)(2,1)} %bitcast.25), channel_id=1, source_target_pairs={{0,8},{8,0},{16,24},{24,16},{1,9},{9,1},{17,25},{25,17},{2,10},{10... | collective-permute-start | bytes 4718600 | tf_op jit(solution)/shard_map/ppermute | solution.py:902
  51.1 23.3 %collective-permute-start.1 = (bf16[1024,768]{1,0:T(8,128)(2,1)}, bf16[1024,768]{1,0:T(8,128)(2,1)}, u32[]{:S(2)}, u32[]{:S(2)}) collective-permute-start(bf16[1024,768]{1,0:T(8,128)(2,1)} %collective-permute-done.x_ref), channel_id=1, source_target_pairs={{0,8},{8,0},{16,24},{24,16},{1,9},{9,1},{17,25},{25,17},{2,10},{10... | collective-permute-start | bytes 4718600 | tf_op jit(solution)/shard_map/ppermute | solution.py:902
  80.8 24.9 %collective-permute-start.3 = (bf16[768,640]{1,0:T(8,128)(2,1)}, bf16[768,640]{1,0:T(8,128)(2,1)}, u32[]{:S(2)}, u32[]{:S(2)}) collective-permute-start(bf16[768,640]{1,0:T(8,128)(2,1)} %hold.4.gain_ref.refs_8_.refs_12_.refs_16_.refs_20_.refs_4_), channel_id=1, source_target_pairs={{0,8},{8,0},{16,24},{24,16},{1,9},{9,1},{17,25},{25,17},{2,10},{10... | collective-permute-start | bytes 2949128 | tf_op jit(solution)/shard_map/ppermute | solution.py:902
  80.9 24.8 %collective-permute-start.4 = (bf16[768,640]{1,0:T(8,128)(2,1)}, bf16[768,640]{1,0:T(8,128)(2,1)S(1)}, u32[]{:S(2)}, u32[]{:S(2)}) collective-permute-start(bf16[768,640]{1,0:T(8,128)(2,1)} %hold.4.gain_ref.refs_8_.refs_12_.refs_16_.refs_20_.refs_4_), channel_id=1, source_target_pairs={{0,16},{8,24},{16,0},{24,8},{1,17},{9,25},{17,1},{25,9},{2,18},{10... | collective-permute-start | bytes 2949128 | tf_op jit(solution)/shard_map/ppermute | solution.py:902
  103.2 24.2 %collective-permute-start.5 = (bf16[64,1024]{1,0:T(8,128)(2,1)}, bf16[64,1024]{1,0:T(8,128)(2,1)}, u32[]{:S(2)}, u32[]{:S(2)}) collective-permute-start(bf16[64,1024]{1,0:T(8,128)(2,1)} %get-tuple-element.156), channel_id=1, source_target_pairs={{0,8},{8,0},{16,24},{24,16},{1,9},{9,1},{17,25},{25,17},{2,10},{10... | collective-permute-start | bytes 393224 | tf_op jit(solution)/shard_map/ppermute | solution.py:902
  104.0 23.4 %collective-permute-start.6 = (bf16[64,1024]{1,0:T(8,128)(2,1)}, bf16[64,1024]{1,0:T(8,128)(2,1)}, u32[]{:S(2)}, u32[]{:S(2)}) collective-permute-start(bf16[64,1024]{1,0:T(8,128)(2,1)} %get-tuple-element.157), channel_id=1, source_target_pairs={{0,16},{8,24},{16,0},{24,8},{1,17},{9,25},{17,1},{25,9},{2,18},{10... | collective-permute-start | bytes 393224 | tf_op jit(solution)/shard_map/ppermute | solution.py:902
  104.2 23.2 %collective-permute-start.7 = (bf16[64,1024]{1,0:T(8,128)(2,1)}, bf16[64,1024]{1,0:T(8,128)(2,1)}, u32[]{:S(2)}, u32[]{:S(2)}) collective-permute-start(bf16[64,1024]{1,0:T(8,128)(2,1)} %get-tuple-element.158), channel_id=1, source_target_pairs={{0,24},{8,16},{16,8},{24,0},{1,25},{9,17},{17,9},{25,1},{2,26},{10... | collective-permute-start | bytes 393224 | tf_op jit(solution)/shard_map/ppermute | solution.py:902
  105.7 1.0 copy-start.1
  127.5 32.5 %collective-permute-start.8 = (bf16[768,2304]{1,0:T(8,128)(2,1)}, bf16[768,2304]{1,0:T(8,128)(2,1)}, u32[]{:S(2)}, u32[]{:S(2)}) collective-permute-start(bf16[768,2304]{1,0:T(8,128)(2,1)} %get-tuple-element.163.mine_ref), channel_id=1, source_target_pairs={{0,8},{8,0},{16,24},{24,16},{1,9},{9,1},{17,25},{25,17},{2,10},{10... | collective-permute-start | bytes 10616840 | tf_op jit(solution)/shard_map/ppermute | solution.py:902
  127.7 22.7 %collective-permute-start.10 = (bf16[64,1024]{1,0:T(8,128)(2,1)}, bf16[64,1024]{1,0:T(8,128)(2,1)S(1)}, u32[]{:S(2)}, u32[]{:S(2)}) collective-permute-start(bf16[64,1024]{1,0:T(8,128)(2,1)} %get-tuple-element.167), channel_id=1, source_target_pairs={{0,16},{8,24},{16,0},{24,8},{1,17},{9,25},{17,1},{25,9},{2,18},{10... | collective-permute-start | bytes 393224 | tf_op jit(solution)/shard_map/ppermute | solution.py:902
  128.4 22.0 %collective-permute-start.11 = (bf16[64,1024]{1,0:T(8,128)(2,1)}, bf16[64,1024]{1,0:T(8,128)(2,1)S(1)}, u32[]{:S(2)}, u32[]{:S(2)}) collective-permute-start(bf16[64,1024]{1,0:T(8,128)(2,1)} %get-tuple-element.168), channel_id=1, source_target_pairs={{0,24},{8,16},{16,8},{24,0},{1,25},{9,17},{17,9},{25,1},{2,26},{10... | collective-permute-start | bytes 393224 | tf_op jit(solution)/shard_map/ppermute | solution.py:902
  129.7 20.8 %collective-permute-start.9 = (bf16[64,1024]{1,0:T(8,128)(2,1)}, bf16[64,1024]{1,0:T(8,128)(2,1)S(1)}, u32[]{:S(2)}, u32[]{:S(2)}) collective-permute-start(bf16[64,1024]{1,0:T(8,128)(2,1)} %get-tuple-element.166), channel_id=1, source_target_pairs={{0,8},{8,0},{16,24},{24,16},{1,9},{9,1},{17,25},{25,17},{2,10},{10... | collective-permute-start | bytes 393224 | tf_op jit(solution)/shard_map/ppermute | solution.py:902
  151.1 2.4 collective-permute-start.12
  151.7 5.4 %collective-permute-start.13 = (bf16[64,1024]{1,0:T(8,128)(2,1)}, bf16[64,1024]{1,0:T(8,128)(2,1)}, u32[]{:S(2)}, u32[]{:S(2)}) collective-permute-start(bf16[64,1024]{1,0:T(8,128)(2,1)} %get-tuple-element.175), channel_id=1, source_target_pairs={{0,16},{8,24},{16,0},{24,8},{1,17},{9,25},{17,1},{25,9},{2,18},{10... | collective-permute-start | bytes 393224 | tf_op jit(solution)/shard_map/ppermute | solution.py:902
  152.1 7.9 %collective-permute-start.14 = (bf16[64,1024]{1,0:T(8,128)(2,1)}, bf16[64,1024]{1,0:T(8,128)(2,1)}, u32[]{:S(2)}, u32[]{:S(2)}) collective-permute-start(bf16[64,1024]{1,0:T(8,128)(2,1)} %get-tuple-element.176), channel_id=1, source_target_pairs={{0,24},{8,16},{16,8},{24,0},{1,25},{9,17},{17,9},{25,1},{2,26},{10... | collective-permute-start | bytes 393224 | tf_op jit(solution)/shard_map/ppermute | solution.py:902
  153.3 62.7 %collective-permute-start.18 = (bf16[768,640]{1,0:T(8,128)(2,1)}, bf16[768,640]{1,0:T(8,128)(2,1)S(1)}, u32[]{:S(2)}, u32[]{:S(2)}) collective-permute-start(bf16[768,640]{1,0:T(8,128)(2,1)} %get-tuple-element.201.refs_10_.refs_14_.refs_18_.refs_22_.refs_6_), channel_id=1, source_target_pairs={{0,8},{8,0},{16,24},{24,16},{1,9},{9,1},{17,25},{25,17},{2,10},{10... | collective-permute-start | bytes 2949128 | tf_op jit(solution)/shard_map/ppermute | solution.py:902
  188.6 17.1 %collective-permute-start.15 = (bf16[192,1024]{1,0:T(8,128)(2,1)}, bf16[192,1024]{1,0:T(8,128)(2,1)}, u32[]{:S(2)}, u32[]{:S(2)}) collective-permute-start(bf16[192,1024]{1,0:T(8,128)(2,1)} %get-tuple-element.188), channel_id=1, source_target_pairs={{0,8},{8,0},{16,24},{24,16},{1,9},{9,1},{17,25},{25,17},{2,10},{10... | collective-permute-start | bytes 1179656 | tf_op jit(solution)/shard_map/ppermute | solution.py:902
  189.0 16.7 %collective-permute-start.16 = (bf16[192,1024]{1,0:T(8,128)(2,1)}, bf16[192,1024]{1,0:T(8,128)(2,1)}, u32[]{:S(2)}, u32[]{:S(2)}) collective-permute-start(bf16[192,1024]{1,0:T(8,128)(2,1)} %get-tuple-element.189), channel_id=1, source_target_pairs={{0,16},{8,24},{16,0},{24,8},{1,17},{9,25},{17,1},{25,9},{2,18},{10... | collective-permute-start | bytes 1179656 | tf_op jit(solution)/shard_map/ppermute | solution.py:902
  189.2 19.3 %collective-permute-start.17 = (bf16[192,1024]{1,0:T(8,128)(2,1)}, bf16[192,1024]{1,0:T(8,128)(2,1)}, u32[]{:S(2)}, u32[]{:S(2)}) collective-permute-start(bf16[192,1024]{1,0:T(8,128)(2,1)} %get-tuple-element.190), channel_id=1, source_target_pairs={{0,24},{8,16},{16,8},{24,0},{1,25},{9,17},{17,9},{25,1},{2,26},{10... | collective-permute-start | bytes 1179656 | tf_op jit(solution)/shard_map/ppermute | solution.py:902
  208.6 58.9 %all-to-all-start.1 = ((bf16[8,144,768]{2,1,0:T(8,128)(2,1)}), bf16[8,144,768]{2,1,0:T(8,128)(2,1)}, u32[]{:S(2)}, u32[]{:S(2)}) async-start(bf16[8,144,768]{2,1,0:T(8,128)(2,1)} %bitcast.32), calls=%async_computation.1 | async-start | bytes 3538944 | tf_op jit(solution)/shard_map/all_to_all | solution.py:976
  213.9 42.1 %collective-permute-start.19 = (bf16[768,768]{1,0:T(8,128)(2,1)}, bf16[768,768]{1,0:T(8,128)(2,1)}, u32[]{:S(2)}, u32[]{:S(2)}) collective-permute-start(bf16[768,768]{1,0:T(8,128)(2,1)} %get-tuple-element.204), channel_id=1, source_target_pairs={{0,8},{8,0},{16,24},{24,16},{1,9},{9,1},{17,25},{25,17},{2,10},{10... | collective-permute-start | bytes 3538952 | tf_op jit(solution)/shard_map/ppermute | solution.py:902
  214.2 41.8 %collective-permute-start.20 = (bf16[768,768]{1,0:T(8,128)(2,1)}, bf16[768,768]{1,0:T(8,128)(2,1)}, u32[]{:S(2)}, u32[]{:S(2)}) collective-permute-start(bf16[768,768]{1,0:T(8,128)(2,1)} %get-tuple-element.205), channel_id=1, source_target_pairs={{0,16},{8,24},{16,0},{24,8},{1,17},{9,25},{17,1},{25,9},{2,18},{10... | collective-permute-start | bytes 3538952 | tf_op jit(solution)/shard_map/ppermute | solution.py:902
  214.3 53.2 %collective-permute-start.21 = (bf16[768,768]{1,0:T(8,128)(2,1)}, bf16[768,768]{1,0:T(8,128)(2,1)}, u32[]{:S(2)}, u32[]{:S(2)}) collective-permute-start(bf16[768,768]{1,0:T(8,128)(2,1)} %get-tuple-element.206), channel_id=1, source_target_pairs={{0,24},{8,16},{16,8},{24,0},{1,25},{9,17},{17,9},{25,1},{2,26},{10... | collective-permute-start | bytes 3538952 | tf_op jit(solution)/shard_map/ppermute | solution.py:902
  216.0 1.0 copy-start.2
  271.7 47.4 %collective-permute-start.22 = (bf16[192,1024]{1,0:T(8,128)(2,1)}, bf16[192,1024]{1,0:T(8,128)(2,1)S(1)}, u32[]{:S(2)}, u32[]{:S(2)}) collective-permute-start(bf16[192,1024]{1,0:T(8,128)(2,1)} %get-tuple-element.211), channel_id=1, source_target_pairs={{0,8},{8,0},{16,24},{24,16},{1,9},{9,1},{17,25},{25,17},{2,10},{10... | collective-permute-start | bytes 1179656 | tf_op jit(solution)/shard_map/ppermute | solution.py:902
  271.8 47.3 %collective-permute-start.23 = (bf16[192,1024]{1,0:T(8,128)(2,1)}, bf16[192,1024]{1,0:T(8,128)(2,1)S(1)}, u32[]{:S(2)}, u32[]{:S(2)}) collective-permute-start(bf16[192,1024]{1,0:T(8,128)(2,1)} %get-tuple-element.212), channel_id=1, source_target_pairs={{0,16},{8,24},{16,0},{24,8},{1,17},{9,25},{17,1},{25,9},{2,18},{10... | collective-permute-start | bytes 1179656 | tf_op jit(solution)/shard_map/ppermute | solution.py:902
  271.8 47.3 %collective-permute-start.24 = (bf16[192,1024]{1,0:T(8,128)(2,1)}, bf16[192,1024]{1,0:T(8,128)(2,1)}, u32[]{:S(2)}, u32[]{:S(2)}) collective-permute-start(bf16[192,1024]{1,0:T(8,128)(2,1)} %get-tuple-element.213), channel_id=1, source_target_pairs={{0,24},{8,16},{16,8},{24,0},{1,25},{9,17},{17,9},{25,1},{2,26},{10... | collective-permute-start | bytes 1179656 | tf_op jit(solution)/shard_map/ppermute | solution.py:902
  273.9 45.3 %all-to-all-start.2 = ((bf16[8,96,768]{2,1,0:T(8,128)(2,1)}), bf16[8,96,768]{2,1,0:T(8,128)(2,1)}, u32[]{:S(2)}, u32[]{:S(2)}) async-start(bf16[8,96,768]{2,1,0:T(8,128)(2,1)} %bitcast.34), calls=%async_computation.2 | async-start | bytes 2359296 | tf_op jit(solution)/shard_map/all_to_all | solution.py:976
  322.9 49.2 %collective-permute-start.28 = (bf16[240,768]{1,0:T(8,128)(2,1)}, bf16[240,768]{1,0:T(8,128)(2,1)}, u32[]{:S(2)}, u32[]{:S(2)}) collective-permute-start(bf16[240,768]{1,0:T(8,128)(2,1)} %get-tuple-element.228.refs_13_.refs_10_), channel_id=1, source_target_pairs={{0,16},{8,24},{16,0},{24,8},{1,17},{9,25},{17,1},{25,9},{2,18},{10... | collective-permute-start | bytes 1105928 | tf_op jit(solution)/shard_map/ppermute | solution.py:902
  323.0 49.1 %collective-permute-start.29 = (bf16[240,768]{1,0:T(8,128)(2,1)}, bf16[240,768]{1,0:T(8,128)(2,1)}, u32[]{:S(2)}, u32[]{:S(2)}) collective-permute-start(bf16[240,768]{1,0:T(8,128)(2,1)} %get-tuple-element.228.refs_13_.refs_10_), channel_id=1, source_target_pairs={{0,24},{8,16},{16,8},{24,0},{1,25},{9,17},{17,9},{25,1},{2,26},{10... | collective-permute-start | bytes 1105928 | tf_op jit(solution)/shard_map/ppermute | solution.py:902
  324.9 47.3 %collective-permute-start.25 = (bf16[192,1024]{1,0:T(8,128)(2,1)}, bf16[192,1024]{1,0:T(8,128)(2,1)}, u32[]{:S(2)}, u32[]{:S(2)}) collective-permute-start(bf16[192,1024]{1,0:T(8,128)(2,1)} %get-tuple-element.225), channel_id=1, source_target_pairs={{0,8},{8,0},{16,24},{24,16},{1,9},{9,1},{17,25},{25,17},{2,10},{10... | collective-permute-start | bytes 1179656 | tf_op jit(solution)/shard_map/ppermute | solution.py:902
  324.9 47.3 %collective-permute-start.26 = (bf16[192,1024]{1,0:T(8,128)(2,1)}, bf16[192,1024]{1,0:T(8,128)(2,1)}, u32[]{:S(2)}, u32[]{:S(2)}) collective-permute-start(bf16[192,1024]{1,0:T(8,128)(2,1)} %get-tuple-element.226), channel_id=1, source_target_pairs={{0,16},{8,24},{16,0},{24,8},{1,17},{9,25},{17,1},{25,9},{2,18},{10... | collective-permute-start | bytes 1179656 | tf_op jit(solution)/shard_map/ppermute | solution.py:902
  325.0 47.2 %collective-permute-start.27 = (bf16[192,1024]{1,0:T(8,128)(2,1)}, bf16[192,1024]{1,0:T(8,128)(2,1)}, u32[]{:S(2)}, u32[]{:S(2)}) collective-permute-start(bf16[192,1024]{1,0:T(8,128)(2,1)} %get-tuple-element.227), channel_id=1, source_target_pairs={{0,24},{8,16},{16,8},{24,0},{1,25},{9,17},{17,9},{25,1},{2,26},{10... | collective-permute-start | bytes 1179656 | tf_op jit(solution)/shard_map/ppermute | solution.py:902
  327.0 45.2 %all-to-all-start.3 = ((bf16[8,96,512]{2,1,0:T(8,128)(2,1)}), bf16[8,96,512]{2,1,0:T(8,128)(2,1)S(1)}, u32[]{:S(2)}, u32[]{:S(2)}) async-start(bf16[8,96,512]{2,1,0:T(8,128)(2,1)} %bitcast.31), calls=%async_computation.3 | async-start | bytes 1572864 | tf_op jit(solution)/shard_map/all_to_all | solution.py:976
  372.2 0.9 copy-start.3
  373.1 1.9 collective-permute-start.30
  378.6 25.9 %all-to-all-start.4 = ((bf16[8,96,256]{2,1,0:T(8,128)(2,1)}), bf16[8,96,256]{2,1,0:T(8,128)(2,1)S(1)}, u32[]{:S(2)}, u32[]{:S(2)}) async-start(bf16[8,96,256]{2,1,0:T(8,128)(2,1)} %bitcast.33), calls=%async_computation.4 | async-start | bytes 786432 | tf_op jit(solution)/shard_map/all_to_all | solution.py:976
  384.3 11.9 %collective-permute-start.31 = (bf16[192,1024]{1,0:T(8,128)(2,1)}, bf16[192,1024]{1,0:T(8,128)(2,1)S(1)}, u32[]{:S(2)}, u32[]{:S(2)}) collective-permute-start(bf16[192,1024]{1,0:T(8,128)(2,1)} %get-tuple-element.243), channel_id=1, source_target_pairs={{0,8},{8,0},{16,24},{24,16},{1,9},{9,1},{17,25},{25,17},{2,10},{10... | collective-permute-start | bytes 1179656 | tf_op jit(solution)/shard_map/ppermute | solution.py:902
  384.9 11.3 %collective-permute-start.32 = (bf16[192,1024]{1,0:T(8,128)(2,1)}, bf16[192,1024]{1,0:T(8,128)(2,1)}, u32[]{:S(2)}, u32[]{:S(2)}) collective-permute-start(bf16[192,1024]{1,0:T(8,128)(2,1)} %get-tuple-element.244), channel_id=1, source_target_pairs={{0,16},{8,24},{16,0},{24,8},{1,17},{9,25},{17,1},{25,9},{2,18},{10... | collective-permute-start | bytes 1179656 | tf_op jit(solution)/shard_map/ppermute | solution.py:902
  385.3 19.2 %collective-permute-start.33 = (bf16[192,1024]{1,0:T(8,128)(2,1)}, bf16[192,1024]{1,0:T(8,128)(2,1)}, u32[]{:S(2)}, u32[]{:S(2)}) collective-permute-start(bf16[192,1024]{1,0:T(8,128)(2,1)} %get-tuple-element.245), channel_id=1, source_target_pairs={{0,24},{8,16},{16,8},{24,0},{1,25},{9,17},{17,9},{25,1},{2,26},{10... | collective-permute-start | bytes 1179656 | tf_op jit(solution)/shard_map/ppermute | solution.py:902
  396.2 8.3 %copy-start.7 = (bf16[192,1024]{1,0:T(8,128)(2,1)}, bf16[192,1024]{1,0:T(8,128)(2,1)S(1)}, u32[]{:S(2)}) copy-start(bf16[192,1024]{1,0:T(8,128)(2,1)S(1)} %collective-permute-done.31.refs_1_) | copy-start | bytes 1179652
  407.3 9.9 %collective-permute-start.34 = (bf16[96,768]{1,0:T(8,128)(2,1)}, bf16[96,768]{1,0:T(8,128)(2,1)S(1)}, u32[]{:S(2)}, u32[]{:S(2)}) collective-permute-start(bf16[96,768]{1,0:T(8,128)(2,1)} %beside.1.refs_3_), channel_id=1, source_target_pairs={{0,8},{8,0},{16,24},{24,16},{1,9},{9,1},{17,25},{25,17},{2,10},{10... | collective-permute-start | bytes 442376 | tf_op jit(solution)/shard_map/ppermute | solution.py:902
  407.5 9.6 %collective-permute-start.35 = (bf16[96,768]{1,0:T(8,128)(2,1)}, bf16[96,768]{1,0:T(8,128)(2,1)S(1)}, u32[]{:S(2)}, u32[]{:S(2)}) collective-permute-start(bf16[96,768]{1,0:T(8,128)(2,1)} %beside.1.refs_3_), channel_id=1, source_target_pairs={{0,16},{8,24},{16,0},{24,8},{1,17},{9,25},{17,1},{25,9},{2,18},{10... | collective-permute-start | bytes 442376 | tf_op jit(solution)/shard_map/ppermute | solution.py:902
  407.9 9.3 %collective-permute-start.36 = (bf16[96,768]{1,0:T(8,128)(2,1)}, bf16[96,768]{1,0:T(8,128)(2,1)S(1)}, u32[]{:S(2)}, u32[]{:S(2)}) collective-permute-start(bf16[96,768]{1,0:T(8,128)(2,1)} %beside.1.refs_3_), channel_id=1, source_target_pairs={{0,24},{8,16},{16,8},{24,0},{1,25},{9,17},{17,9},{25,1},{2,26},{10... | collective-permute-start | bytes 442376 | tf_op jit(solution)/shard_map/ppermute | solution.py:902
  (10 other events, 7.1 us)
Sparse Core Ops, SparseCore 0:
  42.1 64.4 all-gather.1

commit v4 on v3

--- a/solution.py
+++ b/solution.py
@@ -18,6 +18,7 @@
 LN2 = 0.6931471805599453
 
 VMEM = 63 * 2**20
+SMALL = pl.CostEstimate(flops=1024, bytes_accessed=1024, transcendentals=0)
 
 bf = jnp.bfloat16
 f32 = jnp.float32
@@ -122,9 +123,7 @@
         scratch_shapes=[pltpu.VMEM((8, D), f32)],
         input_output_aliases=aliases,
         compiler_params=pltpu.CompilerParams(vmem_limit_bytes=VMEM),
-        cost_estimate=pl.CostEstimate(
-            flops=4 * rows * D * width, bytes_accessed=rows * 8192, transcendentals=0
-        ),
+        cost_estimate=SMALL,
         name="qkv",
     )(info, x, cos, sin, w, *(carried or ()))
 
@@ -225,9 +224,7 @@
             pltpu.VMEM((2, 8, bq), f32),
         ],
         compiler_params=pltpu.CompilerParams(vmem_limit_bytes=VMEM),
-        cost_estimate=pl.CostEstimate(
-            flops=16 * HD * S * S, bytes_accessed=2 * S * S, transcendentals=S * S
-        ),
+        cost_estimate=SMALL,
         name="attend",
     )(k, qt, qt, vt, *after)
     return outs[:6], list(outs[6:])
@@ -343,9 +340,7 @@
         ],
         input_output_aliases={} if earlier is None else {12 + groups: groups},
         compiler_params=pltpu.CompilerParams(vmem_limit_bytes=VMEM),
-        cost_estimate=pl.CostEstimate(
-            flops=24 * HD * S * S, bytes_accessed=2 * S * S, transcendentals=0
-        ),
+        cost_estimate=SMALL,
         name="attend_back",
     )(v, kt, qt, oa, ob, la, lb, pa, pb, cos, sin, normed, *do, *extra)
     return list(outs[:groups]), outs[groups]
@@ -401,6 +396,7 @@
         + [pl.BlockSpec(memory_space=pl.ANY)] * len(after),
         out_specs=vmem,
         compiler_params=pltpu.CompilerParams(vmem_limit_bytes=VMEM),
+        cost_estimate=SMALL,
         name="own_half",
     )(info, in_w, proj_w, gain, out_w, *after)
 
@@ -416,6 +412,7 @@
         out_specs=pl.BlockSpec(memory_space=pl.ANY),
         input_output_aliases={0: 0},
         compiler_params=pltpu.CompilerParams(vmem_limit_bytes=VMEM),
+        cost_estimate=SMALL,
         name="hold",
     )(array, *after)
 
@@ -556,9 +553,7 @@
             pltpu.SemaphoreType.DMA((2,)),
         ],
         compiler_params=pltpu.CompilerParams(vmem_limit_bytes=VMEM),
-        cost_estimate=pl.CostEstimate(
-            flops=rows * D * (14 * ff + 4 * D), bytes_accessed=30 * 2**20, transcendentals=rows * ff
-        ),
+        cost_estimate=SMALL,
         name="middle",
     )(info, x, dy, mine, other, *out_w, *chunks)
     return list(outs[:groups]), outs[groups:]
@@ -623,9 +618,7 @@
             pltpu.VMEM((8, D), f32),
         ],
         compiler_params=pltpu.CompilerParams(vmem_limit_bytes=VMEM),
-        cost_estimate=pl.CostEstimate(
-            flops=2 * len(chosen) * rows * D * D, bytes_accessed=12 * 2**20, transcendentals=0
-        ),
+        cost_estimate=SMALL,
         name="last",
     )(x, base, peers[0], *chunks, *(list(peers) * (2 * len(chosen))), *after)
 
@@ -662,6 +655,7 @@
         ],
         out_specs=pl.BlockSpec(memory_space=pltpu.VMEM),
         compiler_params=pltpu.CompilerParams(vmem_limit_bytes=VMEM),
+        cost_estimate=SMALL,
         name="own_columns",
     )(info, w, gain)
 
@@ -687,6 +681,7 @@
         out_specs=(pl.BlockSpec((rb, 4 * half), lambda i: (i, 0)),) * 2
         + (pl.BlockSpec((2 * half, rb), lambda i: (0, i)),) * 2,
         compiler_params=pltpu.CompilerParams(vmem_limit_bytes=VMEM),
+        cost_estimate=SMALL,
         name="tables",
     )(cosine, sine)
 
@@ -742,9 +737,7 @@
         out_shape=(jax.ShapeDtypeStruct((D, D), bf),) * (steps + 1)
         + (jax.ShapeDtypeStruct((ff, D), bf),),
         compiler_params=pltpu.CompilerParams(vmem_limit_bytes=VMEM),
-        cost_estimate=pl.CostEstimate(
-            flops=2 * rows * D * (D * (steps + 1) + ff), bytes_accessed=20 * 2**20, transcendentals=0
-        ),
+        cost_estimate=SMALL,
         name="weight_grads",
     )(place, second, d_gate_up, mixed_t, branch, inner, dy)
     return list(outs[:-1]), outs[-1]
@@ -770,6 +763,7 @@
         scratch_shapes=list(scratch),
         input_output_aliases={first + n: own + n for n in range(len(carry))},
         compiler_params=pltpu.CompilerParams(vmem_limit_bytes=VMEM),
+        cost_estimate=SMALL,
         name=name,
     )(*arrays, *after, *carry)
     return list(outs[:own]), list(outs[own:])
@@ -816,6 +810,7 @@
         in_specs=[vmem, vmem] + [pl.BlockSpec(memory_space=pl.ANY)] * len(after),
         out_specs=vmem,
         compiler_params=pltpu.CompilerParams(vmem_limit_bytes=VMEM),
+        cost_estimate=SMALL,
         name="beside",
     )(first, second, *after)
 

time: 436 us -> 463 us (1.062)
  waiting for transfers between devices: 52.4 us -> 77.5 us
    ppermute x37, waiting for transfers between devices: 38 us -> 61.9 us  [swap(): return lax.ppermute(array, axis, [(i, i ^ j) for i in range(size)])]
  transfers between devices with their start and end apart: 43 -> 43, of which waited for: 8 -> 9; matrix products, arithmetic and copies ran while one was open for 1% -> 1% of each run, Pallas kernels for 64% -> 53%
where the time goes in v4:
time: 463 us; the launch traced here: 455 us
  Pallas kernels  289 us (62%)
  waiting for transfers between devices  77.5 us (17%)
  starting transfers between devices  59.4 us (13%)
  between operations  15.4 us (3%)
  local copies, waits for them, and re-layouts  8.85 us (2%)
    pallas_call x3, Pallas kernels, attend_back(): pl.pallas_call(functools.partial(attend_back_kernel, kc, groups), grid=(g...  117 us
    pallas_call x3, Pallas kernels, attend(): pl.pallas_call(functools.partial(attend_kernel, kc, groups, len(after)),...  62.3 us
    ppermute x37, waiting for transfers between devices, swap(): return lax.ppermute(array, axis, [(i, i ^ j) for i in range(size)])  61.9 us
    ppermute x37, starting transfers between devices, swap(): return lax.ppermute(array, axis, [(i, i ^ j) for i in range(size)])  29.8 us
    pallas_call x1, Pallas kernels, middle(): pl.pallas_call(functools.partial(middle_kernel, groups, heads, ff, shards...  28.6 us
    pallas_call x4, Pallas kernels, qkv_call(): pl.pallas_call(functools.partial(qkv_kernel, heads), grid=(steps,), out_s...  25.4 us
    all_to_all x4, starting transfers between devices, to_owner(): lax.all_to_all(parts, 'fsdp', split_axis=0, concat_axis=0, tiled=True)  23.2 us
    pallas_call x2, Pallas kernels, last(): pl.pallas_call(functools.partial(last_kernel, groups, chosen), grid=(rows...  17.3 us
  transfers between devices with their start and end apart: 43, of which 9 were waited for; matrix products, arithmetic and copies ran while one was open for 1% of the time, Pallas kernels for 53%

profile of v4, /device:TPU:1, one launch (start us, length us, event | category | flops | bytes accessed | tf_op | source)
XLA Modules:
  0.0 454.6 jit_solution(17035234424064639724)
XLA Ops:
  7.2 2.2 own_columns.1
  9.3 6.4 %all-to-all-start = ((bf16[8,96,640]{2,1,0:T(8,128)(2,1)}), bf16[8,96,640]{2,1,0:T(8,128)(2,1)S(1)}, u32[]{:S(2)}, u32[]{:S(2)}) async-start(bf16[8,96,640]{2,1,0:T(8,128)(2,1)} %own_columns.1), calls=%async_computation | async-start | bytes 1966080 | tf_op jit(solution)/shard_map/all_to_all | solution.py:912
  15.8 2.8 multiply_sine_fusion
  18.6 4.7 %tables.1 = (f32[4096,128]{1,0:T(8,128)}, f32[4096,128]{1,0:T(8,128)}, f32[64,4096]{1,0:T(8,128)}, f32[64,4096]{1,0:T(8,128)}) custom-call(f32[32,4096]{1,0:T(8,128)} %get-tuple-element.253.cos_ref, f32[32,4096]{1,0:T(8,128)} %get-tuple-element.252.sin_ref), custom_call_target="tpu_custom_call" | custom-call | flops 1024 | bytes 1024 | tf_op jit(solution)/shard_map/tables/pallas_call | solution.py:675
  23.3 15.6 %all-to-all-done = bf16[8,96,640]{2,1,0:T(8,128)(2,1)S(1)} async-done(((bf16[8,96,640]{2,1,0:T(8,128)(2,1)}), bf16[8,96,640]{2,1,0:T(8,128)(2,1)S(1)}, u32[]{:S(2)}, u32[]{:S(2)}) %all-to-all-start) | async-done | bytes 983072 | tf_op jit(solution)/shard_map/all_to_all | solution.py:912
  39.9 2.1 own_half.1
  42.1 1.3 collective-permute-start
  43.3 2.2 collective-permute-start.2
  45.6 30.8 %collective-permute-done.x_ref = bf16[1024,768]{1,0:T(8,128)(2,1)} collective-permute-done((bf16[1024,768]{1,0:T(8,128)(2,1)}, bf16[1024,768]{1,0:T(8,128)(2,1)}, u32[]{:S(2)}, u32[]{:S(2)}) %collective-permute-start) | collective-permute-done | bytes 1572896 | tf_op jit(solution)/shard_map/ppermute | solution.py:897
  76.4 2.9 collective-permute-start.1
  81.7 6.4 %qkv.4 = (bf16[4096,768]{1,0:T(8,128)(2,1)}, bf16[3,4096,128]{2,1,0:T(8,128)(2,1)}, bf16[3,4096,128]{2,1,0:T(8,128)(2,1)}, bf16[3,128,4096]{2,1,0:T(8,128)(2,1)}...) custom-call(s32[2]{0:T(128)} %get-tuple-element.255.info_ref, bf16[1024,768]{1,0:T(8,128)(2,1)} %collective-permute-done.x_ref, ...), custom_call_target="tpu_custom_call" | custom-call | flops 1024 | bytes 1024 | tf_op jit(solution)/shard_map/qkv/pallas_call | solution.py:110
  88.0 6.3 %qkv.5 = (bf16[4096,768]{1,0:T(8,128)(2,1)}, bf16[3,4096,128]{2,1,0:T(8,128)(2,1)}, bf16[3,4096,128]{2,1,0:T(8,128)(2,1)}, bf16[3,128,4096]{2,1,0:T(8,128)(2,1)}...) custom-call(s32[2]{0:T(128)} %get-tuple-element.254.info_ref, ...), custom_call_target="tpu_custom_call", output_to_operand_aliasing={{0}: (5, {}), {1}: (6, {}), {2}: (7, {}), {3}: (8, {}), {4}... | custom-call | flops 1024 | bytes 1024 | tf_op jit(solution)/shard_map/qkv/pallas_call | solution.py:110
  94.3 6.4 %qkv.6 = (bf16[4096,768]{1,0:T(8,128)(2,1)}, bf16[3,4096,128]{2,1,0:T(8,128)(2,1)}, bf16[3,4096,128]{2,1,0:T(8,128)(2,1)}, bf16[3,128,4096]{2,1,0:T(8,128)(2,1)}...) custom-call(s32[2]{0:T(128)} %pad_add_fusion.1.info_ref, ...), custom_call_target="tpu_custom_call", output_to_operand_aliasing={{0}: (5, {}), {1}: (6, {}), {2}: (7, {}), {3}: (8, {}), {4}... | custom-call | flops 1024 | bytes 1024 | tf_op jit(solution)/shard_map/qkv/pallas_call | solution.py:110
  100.8 6.3 %qkv.7 = (bf16[4096,768]{1,0:T(8,128)(2,1)}, bf16[3,4096,128]{2,1,0:T(8,128)(2,1)}, bf16[3,4096,128]{2,1,0:T(8,128)(2,1)}, bf16[3,128,4096]{2,1,0:T(8,128)(2,1)}...) custom-call(s32[2]{0:T(128)} %pad_add_fusion.info_ref, ...), custom_call_target="tpu_custom_call", output_to_operand_aliasing={{0}: (5, {}), {1}: (6, {}), {2}: (7, {}), {3}: (8, {}), {4}... | custom-call | flops 1024 | bytes 1024 | tf_op jit(solution)/shard_map/qkv/pallas_call | solution.py:110
  107.2 1.3 collective-permute-start.4
  108.5 20.7 %attend.3 = (bf16[4,4096,512]{2,1,0:T(8,128)(2,1)}, bf16[4,4096,512]{2,1,0:T(8,128)(2,1)}, f32[64,2048]{1,0:T(8,128)}, f32[64,2048]{1,0:T(8,128)}, f32[4,1,512]{...) custom-call(bf16[3,4096,128]{2,1,0:T(8,128)(2,1)} %get-tuple-element, ...), custom_call_target="tpu_custom_call" | custom-call | flops 1024 | bytes 1024 | tf_op jit(solution)/shard_map/attend/pallas_call | solution.py:198
  130.2 1.5 collective-permute-start.7
  132.7 20.7 %attend.4 = (bf16[4,4096,512]{2,1,0:T(8,128)(2,1)}, bf16[4,4096,512]{2,1,0:T(8,128)(2,1)}, f32[64,2048]{1,0:T(8,128)}, f32[64,2048]{1,0:T(8,128)}, f32[4,1,512]{...) custom-call(bf16[3,4096,128]{2,1,0:T(8,128)(2,1)} %get-tuple-element, ...), custom_call_target="tpu_custom_call" | custom-call | flops 1024 | bytes 1024 | tf_op jit(solution)/shard_map/attend/pallas_call | solution.py:198
  155.6 20.9 %attend.5 = (bf16[4,4096,512]{2,1,0:T(8,128)(2,1)}, bf16[4,4096,512]{2,1,0:T(8,128)(2,1)}, f32[64,2048]{1,0:T(8,128)}, f32[64,2048]{1,0:T(8,128)}, f32[4,1,512]{...) custom-call(bf16[3,4096,128]{2,1,0:T(8,128)(2,1)} %get-tuple-element, ...), custom_call_target="tpu_custom_call" | custom-call | flops 1024 | bytes 1024 | tf_op jit(solution)/shard_map/attend/pallas_call | solution.py:198
  179.5 3.7 collective-permute-done.13.refs_10_
  183.2 2.9 collective-permute-done.14.refs_11_
  186.8 28.6 %middle.1 = (bf16[192,1024]{1,0:T(8,128)(2,1)}, bf16[192,1024]{1,0:T(8,128)(2,1)}, bf16[192,1024]{1,0:T(8,128)(2,1)}, bf16[192,1024]{1,0:T(8,128)(2,1)}, bf16[10...) custom-call(s32[1]{0:T(128)} %bitcast.info_ref.place_ref.refs_0_, ...), custom_call_target="tpu_custom_call" | custom-call | flops 1024 | bytes 1024 | tf_op jit(solution)/shard_map/middle/pallas_call | solution.py:515
  217.6 14.9 %weight_grads.1 = (bf16[768,768]{1,0:T(8,128)(2,1)}, bf16[768,768]{1,0:T(8,128)(2,1)}, bf16[768,768]{1,0:T(8,128)(2,1)}, bf16[768,768]{1,0:T(8,128)(2,1)}, bf16[1152,768]{1,0:T(8,128)(2,1)}) custom-call(s32[1]{0:T(128)} %bitcast.info_ref.place_ref.refs_0_, bf16[1024,768]{1,0:T(8,128)(2,1)} %get-tuple-element.191.second_ref, ...), custom_call_target="tpu_custom_call" | custom-call | flops 1024 | bytes 1024 | tf_op jit(solution)/shard_map/weight_grads/pallas_call | solution.py:720
  232.5 2.8 collective-permute-done.17.refs_2_.refs_12_
  235.3 5.1 %all-to-all-start.1 = ((bf16[8,144,768]{2,1,0:T(8,128)(2,1)}), bf16[8,144,768]{2,1,0:T(8,128)(2,1)}, u32[]{:S(2)}, u32[]{:S(2)}) async-start(bf16[8,144,768]{2,1,0:T(8,128)(2,1)} %bitcast.30), calls=%async_computation.1 | async-start | bytes 3538944 | tf_op jit(solution)/shard_map/all_to_all | solution.py:971
  241.2 1.4 collective-permute-start.21
  242.7 2.5 collective-permute-done.18.refs_14_.refs_11_.refs_15_.refs_19_.refs_23_.refs_7_
  246.1 38.9 %attend_back.3 = (bf16[192,1024]{1,0:T(8,128)(2,1)}, bf16[192,1024]{1,0:T(8,128)(2,1)}, bf16[192,1024]{1,0:T(8,128)(2,1)}, bf16[192,1024]{1,0:T(8,128)(2,1)}, bf16[768,512]{1,0:T(8,128)(2,1)}) custom-call(bf16[3,4096,128]{2,1,0:T(8,128)(2,1)} %get-tuple-element.179.v_ref, bf16[3,64,4096]{2,1,0:T(8,128)(2,1)} %get-tuple-element.180.kt_ref, ...), custom_call_target="tpu_custom_call" | custom-call | flops 1024 | bytes 1024 | tf_op jit(solution)/shard_map/attend_back/pallas_call | solution.py:312
  285.1 9.0 %collective-permute-done.21.refs_3_ = bf16[768,768]{1,0:T(8,128)(2,1)} collective-permute-done((bf16[768,768]{1,0:T(8,128)(2,1)}, bf16[768,768]{1,0:T(8,128)(2,1)}, u32[]{:S(2)}, u32[]{:S(2)}) %collective-permute-start.21) | collective-permute-done | bytes 1179680 | tf_op jit(solution)/shard_map/ppermute | solution.py:897
  294.1 4.2 add_up.1
  298.3 6.0 %all-to-all-start.2 = ((bf16[8,96,768]{2,1,0:T(8,128)(2,1)}), bf16[8,96,768]{2,1,0:T(8,128)(2,1)}, u32[]{:S(2)}, u32[]{:S(2)}) async-start(bf16[8,96,768]{2,1,0:T(8,128)(2,1)} %bitcast.36), calls=%async_computation.2 | async-start | bytes 2359296 | tf_op jit(solution)/shard_map/all_to_all | solution.py:971
  305.3 1.3 collective-permute-start.24
  306.6 38.9 %attend_back.4 = (bf16[192,1024]{1,0:T(8,128)(2,1)}, bf16[192,1024]{1,0:T(8,128)(2,1)}, bf16[192,1024]{1,0:T(8,128)(2,1)}, bf16[192,1024]{1,0:T(8,128)(2,1)}, bf16[768,512]{1,0:T(8,128)(2,1)}) custom-call(bf16[3,4096,128]{2,1,0:T(8,128)(2,1)} %get-tuple-element.179.v_ref, ...), custom_call_target="tpu_custom_call", output_to_operand_aliasing={{4}: (16, {})} | custom-call | flops 1024 | bytes 1024 | tf_op jit(solution)/shard_map/attend_back/pallas_call | solution.py:312
  346.4 2.9 owned.1
  349.4 6.2 %all-to-all-start.3 = ((bf16[8,96,512]{2,1,0:T(8,128)(2,1)}), bf16[8,96,512]{2,1,0:T(8,128)(2,1)S(1)}, u32[]{:S(2)}, u32[]{:S(2)}) async-start(bf16[8,96,512]{2,1,0:T(8,128)(2,1)} %bitcast.32), calls=%async_computation.3 | async-start | bytes 1572864 | tf_op jit(solution)/shard_map/all_to_all | solution.py:971
  356.4 1.4 collective-permute-start.27
  358.1 1.4 collective-permute-start.29
  359.6 39.1 %attend_back.5 = (bf16[192,1024]{1,0:T(8,128)(2,1)}, bf16[192,1024]{1,0:T(8,128)(2,1)}, bf16[192,1024]{1,0:T(8,128)(2,1)}, bf16[192,1024]{1,0:T(8,128)(2,1)}, bf16[768,256]{1,0:T(8,128)(2,1)}) custom-call(bf16[3,4096,128]{2,1,0:T(8,128)(2,1)} %get-tuple-element.179.v_ref, bf16[3,64,4096]{2,1,0:T(8,128)(2,1)} %get-tuple-element.180.kt_ref, ...), custom_call_target="tpu_custom_call" | custom-call | flops 1024 | bytes 1024 | tf_op jit(solution)/shard_map/attend_back/pallas_call | solution.py:312
  399.7 1.8 collective-permute-done.30.refs_4_
  402.3 2.8 finish_wide.1
  405.1 5.9 %all-to-all-start.4 = ((bf16[8,96,256]{2,1,0:T(8,128)(2,1)}), bf16[8,96,256]{2,1,0:T(8,128)(2,1)S(1)}, u32[]{:S(2)}, u32[]{:S(2)}) async-start(bf16[8,96,256]{2,1,0:T(8,128)(2,1)} %bitcast.33), calls=%async_computation.4 | async-start | bytes 786432 | tf_op jit(solution)/shard_map/all_to_all | solution.py:971
  411.9 1.4 collective-permute-start.33
  413.3 9.6 %last.2.base_ref.refs_0_ = f32[1024,768]{1,0:T(8,128)} custom-call(bf16[1024,768]{1,0:T(8,128)(2,1)} %bitcast.28, f32[1024,768]{1,0:T(8,128)} %get-tuple-element.178.base_ref, bf16[768,640]{1,0:T(8,128)(2,1)} %hold.4.gain_ref.refs_8_.refs_12_.refs_16_.refs_20_.refs_4_, bf16[192,1024]{1,0:T(8,128)(2,1)} %get-tuple-element.202.refs_0_, ...), custom_call_target="tpu_custom_call" | custom-call | flops 1024 | bytes 1024 | tf_op jit(solution)/shard_map/last/pallas_call | solution.py:601
  422.9 8.2 %collective-permute-done.33.refs_3_ = bf16[192,1024]{1,0:T(8,128)(2,1)} collective-permute-done((bf16[192,1024]{1,0:T(8,128)(2,1)}, bf16[192,1024]{1,0:T(8,128)(2,1)}, u32[]{:S(2)}, u32[]{:S(2)}) %collective-permute-start.33) | collective-permute-done | bytes 393248 | tf_op jit(solution)/shard_map/ppermute | solution.py:897
  431.9 2.0 beside.1.refs_3_
  434.5 1.6 collective-permute-start.36
  436.1 7.7 %last.3.refs_7_ = f32[1024,768]{1,0:T(8,128)} custom-call(bf16[1024,768]{1,0:T(8,128)(2,1)} %bitcast.29, f32[1024,768]{1,0:T(8,128)} %last.2.base_ref.refs_0_, bf16[768,640]{1,0:T(8,128)(2,1)} %hold.4.gain_ref.refs_8_.refs_12_.refs_16_.refs_20_.refs_4_, bf16[192,1024]{1,0:T(8,128)(2,1)} %get-tuple-element.242.refs_0_, bf16[192,1024]{1,0:T(8,128)(2,1)} %copy-done.10, ...), custom_call_target="tpu_custom_call" | custom-call | flops 1024 | bytes 1024 | tf_op jit(solution)/shard_map/last/pallas_call | solution.py:601
  445.2 2.4 finish_qkv.1
  (117 shorter events, 23.0 us)
Async XLA Ops:
  9.3 29.6 %all-to-all-start = ((bf16[8,96,640]{2,1,0:T(8,128)(2,1)}), bf16[8,96,640]{2,1,0:T(8,128)(2,1)S(1)}, u32[]{:S(2)}, u32[]{:S(2)}) async-start(bf16[8,96,640]{2,1,0:T(8,128)(2,1)} %own_columns.1), calls=%async_computation | async-start | bytes 1966080 | tf_op jit(solution)/shard_map/all_to_all | solution.py:912
  15.7 137.7 %all-gather.2.cloned.1.call-start = ((), (), s32[]{:S(2)}) async-start(), calls=%async_computation.5 | async-start | bytes 3981312 | tf_op jit(solution)/shard_map/all_gather | solution.py:903
  42.1 34.3 %collective-permute-start = (bf16[1024,768]{1,0:T(8,128)(2,1)}, bf16[1024,768]{1,0:T(8,128)(2,1)}, u32[]{:S(2)}, u32[]{:S(2)}) collective-permute-start(bf16[1024,768]{1,0:T(8,128)(2,1)} %bitcast.24), channel_id=1, source_target_pairs={{0,16},{8,24},{16,0},{24,8},{1,17},{9,25},{17,1},{25,9},{2,18},{10... | collective-permute-start | bytes 4718600 | tf_op jit(solution)/shard_map/ppermute | solution.py:897
  43.3 51.0 %collective-permute-start.2 = (bf16[1024,768]{1,0:T(8,128)(2,1)}, bf16[1024,768]{1,0:T(8,128)(2,1)}, u32[]{:S(2)}, u32[]{:S(2)}) collective-permute-start(bf16[1024,768]{1,0:T(8,128)(2,1)} %bitcast.25), channel_id=1, source_target_pairs={{0,8},{8,0},{16,24},{24,16},{1,9},{9,1},{17,25},{25,17},{2,10},{10... | collective-permute-start | bytes 4718600 | tf_op jit(solution)/shard_map/ppermute | solution.py:897
  76.4 24.4 %collective-permute-start.1 = (bf16[1024,768]{1,0:T(8,128)(2,1)}, bf16[1024,768]{1,0:T(8,128)(2,1)}, u32[]{:S(2)}, u32[]{:S(2)}) collective-permute-start(bf16[1024,768]{1,0:T(8,128)(2,1)} %collective-permute-done.x_ref), channel_id=1, source_target_pairs={{0,8},{8,0},{16,24},{24,16},{1,9},{9,1},{17,25},{25,17},{2,10},{10... | collective-permute-start | bytes 4718600 | tf_op jit(solution)/shard_map/ppermute | solution.py:897
  107.1 24.6 %collective-permute-start.3 = (bf16[768,640]{1,0:T(8,128)(2,1)}, bf16[768,640]{1,0:T(8,128)(2,1)}, u32[]{:S(2)}, u32[]{:S(2)}) collective-permute-start(bf16[768,640]{1,0:T(8,128)(2,1)} %hold.4.gain_ref.refs_8_.refs_12_.refs_16_.refs_20_.refs_4_), channel_id=1, source_target_pairs={{0,8},{8,0},{16,24},{24,16},{1,9},{9,1},{17,25},{25,17},{2,10},{10... | collective-permute-start | bytes 2949128 | tf_op jit(solution)/shard_map/ppermute | solution.py:897
  107.2 24.5 %collective-permute-start.4 = (bf16[768,640]{1,0:T(8,128)(2,1)}, bf16[768,640]{1,0:T(8,128)(2,1)S(1)}, u32[]{:S(2)}, u32[]{:S(2)}) collective-permute-start(bf16[768,640]{1,0:T(8,128)(2,1)} %hold.4.gain_ref.refs_8_.refs_12_.refs_16_.refs_20_.refs_4_), channel_id=1, source_target_pairs={{0,16},{8,24},{16,0},{24,8},{1,17},{9,25},{17,1},{25,9},{2,18},{10... | collective-permute-start | bytes 2949128 | tf_op jit(solution)/shard_map/ppermute | solution.py:897
  129.2 24.2 %collective-permute-start.5 = (bf16[64,1024]{1,0:T(8,128)(2,1)}, bf16[64,1024]{1,0:T(8,128)(2,1)}, u32[]{:S(2)}, u32[]{:S(2)}) collective-permute-start(bf16[64,1024]{1,0:T(8,128)(2,1)} %get-tuple-element.156), channel_id=1, source_target_pairs={{0,8},{8,0},{16,24},{24,16},{1,9},{9,1},{17,25},{25,17},{2,10},{10... | collective-permute-start | bytes 393224 | tf_op jit(solution)/shard_map/ppermute | solution.py:897
  130.0 23.4 %collective-permute-start.6 = (bf16[64,1024]{1,0:T(8,128)(2,1)}, bf16[64,1024]{1,0:T(8,128)(2,1)}, u32[]{:S(2)}, u32[]{:S(2)}) collective-permute-start(bf16[64,1024]{1,0:T(8,128)(2,1)} %get-tuple-element.157), channel_id=1, source_target_pairs={{0,16},{8,24},{16,0},{24,8},{1,17},{9,25},{17,1},{25,9},{2,18},{10... | collective-permute-start | bytes 393224 | tf_op jit(solution)/shard_map/ppermute | solution.py:897
  130.2 23.2 %collective-permute-start.7 = (bf16[64,1024]{1,0:T(8,128)(2,1)}, bf16[64,1024]{1,0:T(8,128)(2,1)}, u32[]{:S(2)}, u32[]{:S(2)}) collective-permute-start(bf16[64,1024]{1,0:T(8,128)(2,1)} %get-tuple-element.158), channel_id=1, source_target_pairs={{0,24},{8,16},{16,8},{24,0},{1,25},{9,17},{17,9},{25,1},{2,26},{10... | collective-permute-start | bytes 393224 | tf_op jit(solution)/shard_map/ppermute | solution.py:897
  153.4 32.7 %collective-permute-start.8 = (bf16[768,2304]{1,0:T(8,128)(2,1)}, bf16[768,2304]{1,0:T(8,128)(2,1)}, u32[]{:S(2)}, u32[]{:S(2)}) collective-permute-start(bf16[768,2304]{1,0:T(8,128)(2,1)} %get-tuple-element.163.mine_ref), channel_id=1, source_target_pairs={{0,8},{8,0},{16,24},{24,16},{1,9},{9,1},{17,25},{25,17},{2,10},{10... | collective-permute-start | bytes 10616840 | tf_op jit(solution)/shard_map/ppermute | solution.py:897
  153.7 22.9 %collective-permute-start.10 = (bf16[64,1024]{1,0:T(8,128)(2,1)}, bf16[64,1024]{1,0:T(8,128)(2,1)S(1)}, u32[]{:S(2)}, u32[]{:S(2)}) collective-permute-start(bf16[64,1024]{1,0:T(8,128)(2,1)} %get-tuple-element.167), channel_id=1, source_target_pairs={{0,16},{8,24},{16,0},{24,8},{1,17},{9,25},{17,1},{25,9},{2,18},{10... | collective-permute-start | bytes 393224 | tf_op jit(solution)/shard_map/ppermute | solution.py:897
  154.7 21.9 %collective-permute-start.11 = (bf16[64,1024]{1,0:T(8,128)(2,1)}, bf16[64,1024]{1,0:T(8,128)(2,1)S(1)}, u32[]{:S(2)}, u32[]{:S(2)}) collective-permute-start(bf16[64,1024]{1,0:T(8,128)(2,1)} %get-tuple-element.168), channel_id=1, source_target_pairs={{0,24},{8,16},{16,8},{24,0},{1,25},{9,17},{17,9},{25,1},{2,26},{10... | collective-permute-start | bytes 393224 | tf_op jit(solution)/shard_map/ppermute | solution.py:897
  155.6 21.0 %collective-permute-start.9 = (bf16[64,1024]{1,0:T(8,128)(2,1)}, bf16[64,1024]{1,0:T(8,128)(2,1)S(1)}, u32[]{:S(2)}, u32[]{:S(2)}) collective-permute-start(bf16[64,1024]{1,0:T(8,128)(2,1)} %get-tuple-element.166), channel_id=1, source_target_pairs={{0,8},{8,0},{16,24},{24,16},{1,9},{9,1},{17,25},{25,17},{2,10},{10... | collective-permute-start | bytes 393224 | tf_op jit(solution)/shard_map/ppermute | solution.py:897
  177.3 2.1 collective-permute-start.12
  177.8 5.3 %collective-permute-start.13 = (bf16[64,1024]{1,0:T(8,128)(2,1)}, bf16[64,1024]{1,0:T(8,128)(2,1)S(1)}, u32[]{:S(2)}, u32[]{:S(2)}) collective-permute-start(bf16[64,1024]{1,0:T(8,128)(2,1)} %get-tuple-element.175), channel_id=1, source_target_pairs={{0,16},{8,24},{16,0},{24,8},{1,17},{9,25},{17,1},{25,9},{2,18},{10... | collective-permute-start | bytes 393224 | tf_op jit(solution)/shard_map/ppermute | solution.py:897
  178.6 7.5 %collective-permute-start.14 = (bf16[64,1024]{1,0:T(8,128)(2,1)}, bf16[64,1024]{1,0:T(8,128)(2,1)S(1)}, u32[]{:S(2)}, u32[]{:S(2)}) collective-permute-start(bf16[64,1024]{1,0:T(8,128)(2,1)} %get-tuple-element.176), channel_id=1, source_target_pairs={{0,24},{8,16},{16,8},{24,0},{1,25},{9,17},{17,9},{25,1},{2,26},{10... | collective-permute-start | bytes 393224 | tf_op jit(solution)/shard_map/ppermute | solution.py:897
  179.5 6.6 %copy-start.18 = (bf16[64,1024]{1,0:T(8,128)(2,1)}, bf16[64,1024]{1,0:T(8,128)(2,1)S(1)}, u32[]{:S(2)}) copy-start(bf16[64,1024]{1,0:T(8,128)(2,1)S(1)} %collective-permute-done.12.refs_9_) | copy-start | bytes 393220
  183.2 2.9 copy-start.19
  215.4 17.1 %collective-permute-start.15 = (bf16[192,1024]{1,0:T(8,128)(2,1)}, bf16[192,1024]{1,0:T(8,128)(2,1)S(1)}, u32[]{:S(2)}, u32[]{:S(2)}) collective-permute-start(bf16[192,1024]{1,0:T(8,128)(2,1)} %get-tuple-element.188), channel_id=1, source_target_pairs={{0,8},{8,0},{16,24},{24,16},{1,9},{9,1},{17,25},{25,17},{2,10},{10... | collective-permute-start | bytes 1179656 | tf_op jit(solution)/shard_map/ppermute | solution.py:897
  215.7 16.7 %collective-permute-start.16 = (bf16[192,1024]{1,0:T(8,128)(2,1)}, bf16[192,1024]{1,0:T(8,128)(2,1)S(1)}, u32[]{:S(2)}, u32[]{:S(2)}) collective-permute-start(bf16[192,1024]{1,0:T(8,128)(2,1)} %get-tuple-element.189), channel_id=1, source_target_pairs={{0,16},{8,24},{16,0},{24,8},{1,17},{9,25},{17,1},{25,9},{2,18},{10... | collective-permute-start | bytes 1179656 | tf_op jit(solution)/shard_map/ppermute | solution.py:897
  216.3 19.0 %collective-permute-start.17 = (bf16[192,1024]{1,0:T(8,128)(2,1)}, bf16[192,1024]{1,0:T(8,128)(2,1)}, u32[]{:S(2)}, u32[]{:S(2)}) collective-permute-start(bf16[192,1024]{1,0:T(8,128)(2,1)} %get-tuple-element.190), channel_id=1, source_target_pairs={{0,24},{8,16},{16,8},{24,0},{1,25},{9,17},{17,9},{25,1},{2,26},{10... | collective-permute-start | bytes 1179656 | tf_op jit(solution)/shard_map/ppermute | solution.py:897
  232.4 2.9 copy-start.5
  235.3 7.3 %copy-start.2 = (bf16[768,640]{1,0:T(8,128)(2,1)S(1)}, bf16[768,640]{1,0:T(8,128)(2,1)}, u32[]{:S(2)}) copy-start(bf16[768,640]{1,0:T(8,128)(2,1)} %get-tuple-element.201.refs_10_.refs_14_.refs_18_.refs_22_.refs_6_) | copy-start | bytes 2949124
  235.3 58.8 %all-to-all-start.1 = ((bf16[8,144,768]{2,1,0:T(8,128)(2,1)}), bf16[8,144,768]{2,1,0:T(8,128)(2,1)}, u32[]{:S(2)}, u32[]{:S(2)}) async-start(bf16[8,144,768]{2,1,0:T(8,128)(2,1)} %bitcast.30), calls=%async_computation.1 | async-start | bytes 3538944 | tf_op jit(solution)/shard_map/all_to_all | solution.py:971
  240.4 44.6 %collective-permute-start.19 = (bf16[768,768]{1,0:T(8,128)(2,1)}, bf16[768,768]{1,0:T(8,128)(2,1)}, u32[]{:S(2)}, u32[]{:S(2)}) collective-permute-start(bf16[768,768]{1,0:T(8,128)(2,1)} %get-tuple-element.204), channel_id=1, source_target_pairs={{0,8},{8,0},{16,24},{24,16},{1,9},{9,1},{17,25},{25,17},{2,10},{10... | collective-permute-start | bytes 3538952 | tf_op jit(solution)/shard_map/ppermute | solution.py:897
  240.8 44.3 %collective-permute-start.20 = (bf16[768,768]{1,0:T(8,128)(2,1)}, bf16[768,768]{1,0:T(8,128)(2,1)}, u32[]{:S(2)}, u32[]{:S(2)}) collective-permute-start(bf16[768,768]{1,0:T(8,128)(2,1)} %get-tuple-element.205), channel_id=1, source_target_pairs={{0,16},{8,24},{16,0},{24,8},{1,17},{9,25},{17,1},{25,9},{2,18},{10... | collective-permute-start | bytes 3538952 | tf_op jit(solution)/shard_map/ppermute | solution.py:897
  241.2 52.9 %collective-permute-start.21 = (bf16[768,768]{1,0:T(8,128)(2,1)}, bf16[768,768]{1,0:T(8,128)(2,1)}, u32[]{:S(2)}, u32[]{:S(2)}) collective-permute-start(bf16[768,768]{1,0:T(8,128)(2,1)} %get-tuple-element.206), channel_id=1, source_target_pairs={{0,24},{8,16},{16,8},{24,0},{1,25},{9,17},{17,9},{25,1},{2,26},{10... | collective-permute-start | bytes 3538952 | tf_op jit(solution)/shard_map/ppermute | solution.py:897
  242.6 2.6 collective-permute-start.18
  298.3 47.3 %all-to-all-start.2 = ((bf16[8,96,768]{2,1,0:T(8,128)(2,1)}), bf16[8,96,768]{2,1,0:T(8,128)(2,1)}, u32[]{:S(2)}, u32[]{:S(2)}) async-start(bf16[8,96,768]{2,1,0:T(8,128)(2,1)} %bitcast.36), calls=%async_computation.2 | async-start | bytes 2359296 | tf_op jit(solution)/shard_map/all_to_all | solution.py:971
  304.3 41.3 %collective-permute-start.22 = (bf16[192,1024]{1,0:T(8,128)(2,1)}, bf16[192,1024]{1,0:T(8,128)(2,1)S(1)}, u32[]{:S(2)}, u32[]{:S(2)}) collective-permute-start(bf16[192,1024]{1,0:T(8,128)(2,1)} %get-tuple-element.211), channel_id=1, source_target_pairs={{0,8},{8,0},{16,24},{24,16},{1,9},{9,1},{17,25},{25,17},{2,10},{10... | collective-permute-start | bytes 1179656 | tf_op jit(solution)/shard_map/ppermute | solution.py:897
  304.9 40.7 %collective-permute-start.23 = (bf16[192,1024]{1,0:T(8,128)(2,1)}, bf16[192,1024]{1,0:T(8,128)(2,1)S(1)}, u32[]{:S(2)}, u32[]{:S(2)}) collective-permute-start(bf16[192,1024]{1,0:T(8,128)(2,1)} %get-tuple-element.212), channel_id=1, source_target_pairs={{0,16},{8,24},{16,0},{24,8},{1,17},{9,25},{17,1},{25,9},{2,18},{10... | collective-permute-start | bytes 1179656 | tf_op jit(solution)/shard_map/ppermute | solution.py:897
  305.3 40.3 %collective-permute-start.24 = (bf16[192,1024]{1,0:T(8,128)(2,1)}, bf16[192,1024]{1,0:T(8,128)(2,1)}, u32[]{:S(2)}, u32[]{:S(2)}) collective-permute-start(bf16[192,1024]{1,0:T(8,128)(2,1)} %get-tuple-element.213), channel_id=1, source_target_pairs={{0,24},{8,16},{16,8},{24,0},{1,25},{9,17},{17,9},{25,1},{2,26},{10... | collective-permute-start | bytes 1179656 | tf_op jit(solution)/shard_map/ppermute | solution.py:897
  349.4 49.4 %all-to-all-start.3 = ((bf16[8,96,512]{2,1,0:T(8,128)(2,1)}), bf16[8,96,512]{2,1,0:T(8,128)(2,1)S(1)}, u32[]{:S(2)}, u32[]{:S(2)}) async-start(bf16[8,96,512]{2,1,0:T(8,128)(2,1)} %bitcast.32), calls=%async_computation.3 | async-start | bytes 1572864 | tf_op jit(solution)/shard_map/all_to_all | solution.py:971
  355.6 43.2 %collective-permute-start.25 = (bf16[192,1024]{1,0:T(8,128)(2,1)}, bf16[192,1024]{1,0:T(8,128)(2,1)}, u32[]{:S(2)}, u32[]{:S(2)}) collective-permute-start(bf16[192,1024]{1,0:T(8,128)(2,1)} %get-tuple-element.225), channel_id=1, source_target_pairs={{0,8},{8,0},{16,24},{24,16},{1,9},{9,1},{17,25},{25,17},{2,10},{10... | collective-permute-start | bytes 1179656 | tf_op jit(solution)/shard_map/ppermute | solution.py:897
  356.1 42.7 %collective-permute-start.26 = (bf16[192,1024]{1,0:T(8,128)(2,1)}, bf16[192,1024]{1,0:T(8,128)(2,1)}, u32[]{:S(2)}, u32[]{:S(2)}) collective-permute-start(bf16[192,1024]{1,0:T(8,128)(2,1)} %get-tuple-element.226), channel_id=1, source_target_pairs={{0,16},{8,24},{16,0},{24,8},{1,17},{9,25},{17,1},{25,9},{2,18},{10... | collective-permute-start | bytes 1179656 | tf_op jit(solution)/shard_map/ppermute | solution.py:897
  356.4 42.3 %collective-permute-start.27 = (bf16[192,1024]{1,0:T(8,128)(2,1)}, bf16[192,1024]{1,0:T(8,128)(2,1)}, u32[]{:S(2)}, u32[]{:S(2)}) collective-permute-start(bf16[192,1024]{1,0:T(8,128)(2,1)} %get-tuple-element.227), channel_id=1, source_target_pairs={{0,24},{8,16},{16,8},{24,0},{1,25},{9,17},{17,9},{25,1},{2,26},{10... | collective-permute-start | bytes 1179656 | tf_op jit(solution)/shard_map/ppermute | solution.py:897
  357.8 40.9 %collective-permute-start.28 = (bf16[240,768]{1,0:T(8,128)(2,1)}, bf16[240,768]{1,0:T(8,128)(2,1)}, u32[]{:S(2)}, u32[]{:S(2)}) collective-permute-start(bf16[240,768]{1,0:T(8,128)(2,1)} %get-tuple-element.228.refs_13_.refs_10_), channel_id=1, source_target_pairs={{0,16},{8,24},{16,0},{24,8},{1,17},{9,25},{17,1},{25,9},{2,18},{10... | collective-permute-start | bytes 1105928 | tf_op jit(solution)/shard_map/ppermute | solution.py:897
  358.1 40.6 %collective-permute-start.29 = (bf16[240,768]{1,0:T(8,128)(2,1)}, bf16[240,768]{1,0:T(8,128)(2,1)}, u32[]{:S(2)}, u32[]{:S(2)}) collective-permute-start(bf16[240,768]{1,0:T(8,128)(2,1)} %get-tuple-element.228.refs_13_.refs_10_), channel_id=1, source_target_pairs={{0,24},{8,16},{16,8},{24,0},{1,25},{9,17},{17,9},{25,1},{2,26},{10... | collective-permute-start | bytes 1105928 | tf_op jit(solution)/shard_map/ppermute | solution.py:897
  399.6 1.9 collective-permute-start.30
  405.1 26.0 %all-to-all-start.4 = ((bf16[8,96,256]{2,1,0:T(8,128)(2,1)}), bf16[8,96,256]{2,1,0:T(8,128)(2,1)S(1)}, u32[]{:S(2)}, u32[]{:S(2)}) async-start(bf16[8,96,256]{2,1,0:T(8,128)(2,1)} %bitcast.33), calls=%async_computation.4 | async-start | bytes 786432 | tf_op jit(solution)/shard_map/all_to_all | solution.py:971
  411.1 11.8 %collective-permute-start.31 = (bf16[192,1024]{1,0:T(8,128)(2,1)}, bf16[192,1024]{1,0:T(8,128)(2,1)S(1)}, u32[]{:S(2)}, u32[]{:S(2)}) collective-permute-start(bf16[192,1024]{1,0:T(8,128)(2,1)} %get-tuple-element.243), channel_id=1, source_target_pairs={{0,8},{8,0},{16,24},{24,16},{1,9},{9,1},{17,25},{25,17},{2,10},{10... | collective-permute-start | bytes 1179656 | tf_op jit(solution)/shard_map/ppermute | solution.py:897
  411.6 11.3 %collective-permute-start.32 = (bf16[192,1024]{1,0:T(8,128)(2,1)}, bf16[192,1024]{1,0:T(8,128)(2,1)}, u32[]{:S(2)}, u32[]{:S(2)}) collective-permute-start(bf16[192,1024]{1,0:T(8,128)(2,1)} %get-tuple-element.244), channel_id=1, source_target_pairs={{0,16},{8,24},{16,0},{24,8},{1,17},{9,25},{17,1},{25,9},{2,18},{10... | collective-permute-start | bytes 1179656 | tf_op jit(solution)/shard_map/ppermute | solution.py:897
  411.9 19.2 %collective-permute-start.33 = (bf16[192,1024]{1,0:T(8,128)(2,1)}, bf16[192,1024]{1,0:T(8,128)(2,1)}, u32[]{:S(2)}, u32[]{:S(2)}) collective-permute-start(bf16[192,1024]{1,0:T(8,128)(2,1)} %get-tuple-element.245), channel_id=1, source_target_pairs={{0,24},{8,16},{16,8},{24,0},{1,25},{9,17},{17,9},{25,1},{2,26},{10... | collective-permute-start | bytes 1179656 | tf_op jit(solution)/shard_map/ppermute | solution.py:897
  422.9 8.3 %copy-start.10 = (bf16[192,1024]{1,0:T(8,128)(2,1)}, bf16[192,1024]{1,0:T(8,128)(2,1)S(1)}, u32[]{:S(2)}) copy-start(bf16[192,1024]{1,0:T(8,128)(2,1)S(1)} %collective-permute-done.31.refs_1_) | copy-start | bytes 1179652
  434.0 9.9 %collective-permute-start.34 = (bf16[96,768]{1,0:T(8,128)(2,1)}, bf16[96,768]{1,0:T(8,128)(2,1)S(1)}, u32[]{:S(2)}, u32[]{:S(2)}) collective-permute-start(bf16[96,768]{1,0:T(8,128)(2,1)} %beside.1.refs_3_), channel_id=1, source_target_pairs={{0,8},{8,0},{16,24},{24,16},{1,9},{9,1},{17,25},{25,17},{2,10},{10... | collective-permute-start | bytes 442376 | tf_op jit(solution)/shard_map/ppermute | solution.py:897
  434.2 9.6 %collective-permute-start.35 = (bf16[96,768]{1,0:T(8,128)(2,1)}, bf16[96,768]{1,0:T(8,128)(2,1)S(1)}, u32[]{:S(2)}, u32[]{:S(2)}) collective-permute-start(bf16[96,768]{1,0:T(8,128)(2,1)} %beside.1.refs_3_), channel_id=1, source_target_pairs={{0,16},{8,24},{16,0},{24,8},{1,17},{9,25},{17,1},{25,9},{2,18},{10... | collective-permute-start | bytes 442376 | tf_op jit(solution)/shard_map/ppermute | solution.py:897
  434.5 9.3 %collective-permute-start.36 = (bf16[96,768]{1,0:T(8,128)(2,1)}, bf16[96,768]{1,0:T(8,128)(2,1)S(1)}, u32[]{:S(2)}, u32[]{:S(2)}) collective-permute-start(bf16[96,768]{1,0:T(8,128)(2,1)} %beside.1.refs_3_), channel_id=1, source_target_pairs={{0,24},{8,16},{16,8},{24,0},{1,25},{9,17},{17,9},{25,1},{2,26},{10... | collective-permute-start | bytes 442376 | tf_op jit(solution)/shard_map/ppermute | solution.py:897
  (16 other events, 14.5 us)
Sparse Core Ops, SparseCore 0:
  42.2 64.4 all-gather.1

commit v5 on v3

--- a/solution.py
+++ b/solution.py
@@ -82,7 +82,7 @@
 def qkv_call(block, blocks, heads, info, x, cos, sin, w, carried):
     rows = x.shape[0]
     S = rows * blocks
-    rb = min(512, rows)
+    rb = min(256, rows)
     steps = rows // rb
     width = w.shape[1]
     at = lambda i: block * steps + i
@@ -480,7 +480,7 @@
     dy = dy_ref[...]
     result = hidden
     d_second = jnp.zeros_like(hidden)
-    step = 384
+    step = ff
     for c in range(ff // step):
         a = slice(c * step, (c + 1) * step)
         b = slice(ff + c * step, ff + (c + 1) * step)
@@ -797,27 +797,20 @@
     return -(-n // 16) * 16
 
 
-def beside_kernel(first_ref, second_ref, *refs):
-    out_ref = refs[-1]
-    start = 0
-    for ref in (first_ref, second_ref):
-        total = ref[0].astype(f32)
-        for f in range(1, ref.shape[0]):
-            total = total + ref[f].astype(f32)
-        out_ref[:, start : start + ref.shape[2]] = total.astype(bf)
-        start += ref.shape[2]
-
-
-def beside(first, second, after):
+def sum_kernel(parts_ref, *refs):
+    total = parts_ref[0].astype(f32)
+    for f in range(1, parts_ref.shape[0]):
+        total = total + parts_ref[f].astype(f32)
+    refs[-1][...] = total.astype(bf)
+
+
+def sum_owned(parts, after):
     vmem = pl.BlockSpec(memory_space=pltpu.VMEM)
-    return pl.pallas_call(
-        beside_kernel,
-        out_shape=jax.ShapeDtypeStruct((first.shape[1], first.shape[2] + second.shape[2]), bf),
-        in_specs=[vmem, vmem] + [pl.BlockSpec(memory_space=pl.ANY)] * len(after),
-        out_specs=vmem,
-        compiler_params=pltpu.CompilerParams(vmem_limit_bytes=VMEM),
-        name="beside",
-    )(first, second, *after)
+    (total,), _ = ordered(
+        sum_kernel, [parts], after, [], [jax.ShapeDtypeStruct(parts.shape[1:], bf)],
+        [vmem], [vmem], "sum_owned",
+    )
+    return total
 
 
 def owned_kernel(wide_ref, tall_ref, *refs):
@@ -992,20 +985,19 @@
         )
 
     peers = [own, own_near, own_across, own_diagonal]
-    sent_0, qkv_first = back(0, (512, 0, None), [tall_grad, own_diagonal])
+    sent_0, qkv_first = back(0, (768, 0, None), [tall_grad, own_diagonal])
     wide_sum, others = add_up(wide_all, [qkv_first, tall_parts], sent_0[1:])
     wide_parts = to_owner(wide_sum)
     received_0 = exchange(sent_0[:1] + others)
 
-    sent_1, qkv_first = back(1, (512, 1, qkv_first), [wide_sum])
+    sent_1, qkv_first = back(1, (768, 1, qkv_first), [wide_sum])
     both, carried = owned(wide_parts, tall_parts, received_0[1:], sent_1[1:] + [qkv_first])
     received_1 = exchange(sent_1[:1] + carried[:-1])
     both_far = [swap(both, j) for j in range(2, groups)]
-    qkv_parts = to_owner(carried[-1])
-
-    sent_2, qkv_second = back(2, (256, 0, None), [both])
+
+    sent_2, qkv_second = back(2, (768, 2, carried[-1]), [both])
     _, carried = ordered(
-        lambda: None, [], received_1[1:] + both_far + [qkv_parts],
+        lambda: None, [], received_1[1:] + both_far,
         sent_2[1:] + [qkv_second, both], [], [], [], "pass_on",
     )
     qkv_second, both = carried[-2:]
@@ -1017,11 +1009,11 @@
         ((shard, 2 * ff), (shard, D), (1, shard), (tall, D)), "finish_wide",
         carry=[qkv_second],
     )
-    qkv_second_parts = to_owner(carried[0])
+    qkv_parts = to_owner(carried[0])
     base = last(
         groups, heads, (0, 1), x0, d_hidden, peers, received_0 + received_1, [carried[0]]
     )
-    qkv_peers = from_peers(beside(qkv_parts, qkv_second_parts, [base] + received_2[1:]))
+    qkv_peers = from_peers(sum_owned(qkv_parts, [base] + received_2[1:]))
     tokens_grad = last(groups, heads, (2,), x0, base, peers, received_2, [])
     (qkv_weight_grad, attn_gain_grad), _ = finish(
         functools.partial(finish_qkv_kernel, groups, heads),

time: 436 us -> 436 us (level)
  waiting for transfers between devices: 52.4 us -> 60.4 us
  starting transfers between devices: 58.1 us -> 52.9 us
    all_to_all x4 -> x3, waiting for transfers between devices: 0.01 us -> 7.91 us  [to_owner(): lax.all_to_all(parts, 'fsdp', split_axis=0, concat_axis=0, tiled=True)]
    all_to_all x4 -> x3, starting transfers between devices: 23.1 us -> 17.3 us  [to_owner(): lax.all_to_all(parts, 'fsdp', split_axis=0, concat_axis=0, tiled=True)]
    pallas_call x8 -> x9, Pallas kernels: 12.4 us -> 14.5 us  [ordered(): pl.pallas_call(call, grid=grid, out_shape=tuple(out_shape) + tuple((jax.S...]
  transfers between devices with their start and end apart: 43 -> 42, of which waited for: 8 -> 9; matrix products, arithmetic and copies ran while one was open for 1% -> 1% of each run, Pallas kernels for 64% -> 64%
where the time goes in v5:
time: 436 us; the launch traced here: 432 us
  Pallas kernels  292 us (67%)
  waiting for transfers between devices  60.4 us (14%)
  starting transfers between devices  52.9 us (12%)
  between operations  15.3 us (4%)
  local copies, waits for them, and re-layouts  7.46 us (2%)
  other arithmetic  4.58 us (1%)
    pallas_call x3, Pallas kernels, attend_back(): pl.pallas_call(functools.partial(attend_back_kernel, kc, groups), grid=(g...  118 us
    pallas_call x3, Pallas kernels, attend(): pl.pallas_call(functools.partial(attend_kernel, kc, groups, len(after)),...  62.7 us
    ppermute x37, waiting for transfers between devices, swap(): return lax.ppermute(array, axis, [(i, i ^ j) for i in range(size)])  38.1 us
    ppermute x37, starting transfers between devices, swap(): return lax.ppermute(array, axis, [(i, i ^ j) for i in range(size)])  29.3 us
    pallas_call x1, Pallas kernels, middle(): pl.pallas_call(functools.partial(middle_kernel, groups, heads, ff, shards...  28 us
    pallas_call x4, Pallas kernels, qkv_call(): pl.pallas_call(functools.partial(qkv_kernel, heads), grid=(steps,), out_s...  27.3 us
    pallas_call x2, Pallas kernels, last(): pl.pallas_call(functools.partial(last_kernel, groups, chosen), grid=(rows...  17.4 us
    all_to_all x3, starting transfers between devices, to_owner(): lax.all_to_all(parts, 'fsdp', split_axis=0, concat_axis=0, tiled=True)  17.3 us
  transfers between devices with their start and end apart: 42, of which 9 were waited for; matrix products, arithmetic and copies ran while one was open for 1% of the time, Pallas kernels for 64%

profile of v5, /device:TPU:1, one launch (start us, length us, event | category | flops | bytes accessed | tf_op | source)
XLA Modules:
  0.0 432.3 jit_solution(8925687985190671141)
XLA Ops:
  7.2 2.2 own_columns.1
  9.3 6.4 %all-to-all-start = ((bf16[8,96,640]{2,1,0:T(8,128)(2,1)}), bf16[8,96,640]{2,1,0:T(8,128)(2,1)S(1)}, u32[]{:S(2)}, u32[]{:S(2)}) async-start(bf16[8,96,640]{2,1,0:T(8,128)(2,1)} %own_columns.1), calls=%async_computation | async-start | bytes 1966080 | tf_op jit(solution)/shard_map/all_to_all | solution.py:910
  15.7 1.3 collective-permute-start
  17.1 2.8 multiply_sine_fusion
  19.9 4.7 %tables.1 = (f32[4096,128]{1,0:T(8,128)}, f32[4096,128]{1,0:T(8,128)}, f32[64,4096]{1,0:T(8,128)}, f32[64,4096]{1,0:T(8,128)}) custom-call(f32[32,4096]{1,0:T(8,128)} %get-tuple-element.253.cos_ref, f32[32,4096]{1,0:T(8,128)} %get-tuple-element.252.sin_ref), custom_call_target="tpu_custom_call" | custom-call | tf_op jit(solution)/shard_map/tables/pallas_call | solution.py:681
  24.6 14.4 %all-to-all-done = bf16[8,96,640]{2,1,0:T(8,128)(2,1)S(1)} async-done(((bf16[8,96,640]{2,1,0:T(8,128)(2,1)}), bf16[8,96,640]{2,1,0:T(8,128)(2,1)S(1)}, u32[]{:S(2)}, u32[]{:S(2)}) %all-to-all-start) | async-done | bytes 983072 | tf_op jit(solution)/shard_map/all_to_all | solution.py:910
  39.9 2.4 own_half.1
  42.3 2.0 collective-permute-start.2
  44.3 6.7 %collective-permute-done.x_ref = bf16[1024,768]{1,0:T(8,128)(2,1)} collective-permute-done((bf16[1024,768]{1,0:T(8,128)(2,1)}, bf16[1024,768]{1,0:T(8,128)(2,1)}, u32[]{:S(2)}, u32[]{:S(2)}) %collective-permute-start) | collective-permute-done | bytes 1572896 | tf_op jit(solution)/shard_map/ppermute | solution.py:895
  51.1 1.9 collective-permute-start.1
  55.3 6.8 %qkv.4 = (bf16[4096,768]{1,0:T(8,128)(2,1)}, bf16[3,4096,128]{2,1,0:T(8,128)(2,1)}, bf16[3,4096,128]{2,1,0:T(8,128)(2,1)}, bf16[3,128,4096]{2,1,0:T(8,128)(2,1)}...) custom-call(s32[2]{0:T(128)} %get-tuple-element.255.info_ref, bf16[1024,768]{1,0:T(8,128)(2,1)} %collective-permute-done.x_ref, ...), custom_call_target="tpu_custom_call" | custom-call | flops 2013265920 | bytes 8388608 | tf_op jit(solution)/shard_map/qkv/pallas_call | solution.py:109
  62.2 6.8 %qkv.5 = (bf16[4096,768]{1,0:T(8,128)(2,1)}, bf16[3,4096,128]{2,1,0:T(8,128)(2,1)}, bf16[3,4096,128]{2,1,0:T(8,128)(2,1)}, bf16[3,128,4096]{2,1,0:T(8,128)(2,1)}...) custom-call(s32[2]{0:T(128)} %get-tuple-element.254.info_ref, ...), custom_call_target="tpu_custom_call", output_to_operand_aliasing={{0}: (5, {}), {1}: (6, {}), {2}: (7, {}), {3}: (8, {}), {4}... | custom-call | flops 2013265920 | bytes 8388608 | tf_op jit(solution)/shard_map/qkv/pallas_call | solution.py:109
  69.0 6.8 %qkv.6 = (bf16[4096,768]{1,0:T(8,128)(2,1)}, bf16[3,4096,128]{2,1,0:T(8,128)(2,1)}, bf16[3,4096,128]{2,1,0:T(8,128)(2,1)}, bf16[3,128,4096]{2,1,0:T(8,128)(2,1)}...) custom-call(s32[2]{0:T(128)} %pad_add_fusion.1.info_ref, ...), custom_call_target="tpu_custom_call", output_to_operand_aliasing={{0}: (5, {}), {1}: (6, {}), {2}: (7, {}), {3}: (8, {}), {4}... | custom-call | flops 2013265920 | bytes 8388608 | tf_op jit(solution)/shard_map/qkv/pallas_call | solution.py:109
  75.8 6.8 %qkv.7 = (bf16[4096,768]{1,0:T(8,128)(2,1)}, bf16[3,4096,128]{2,1,0:T(8,128)(2,1)}, bf16[3,4096,128]{2,1,0:T(8,128)(2,1)}, bf16[3,128,4096]{2,1,0:T(8,128)(2,1)}...) custom-call(s32[2]{0:T(128)} %pad_add_fusion.info_ref, ...), custom_call_target="tpu_custom_call", output_to_operand_aliasing={{0}: (5, {}), {1}: (6, {}), {2}: (7, {}), {3}: (8, {}), {4}... | custom-call | flops 2013265920 | bytes 8388608 | tf_op jit(solution)/shard_map/qkv/pallas_call | solution.py:109
  82.8 1.3 collective-permute-start.4
  84.0 20.5 %attend.3 = (bf16[4,4096,512]{2,1,0:T(8,128)(2,1)}, bf16[4,4096,512]{2,1,0:T(8,128)(2,1)}, f32[64,2048]{1,0:T(8,128)}, f32[64,2048]{1,0:T(8,128)}, f32[4,1,512]{...) custom-call(bf16[3,4096,128]{2,1,0:T(8,128)(2,1)} %get-tuple-element, ...), custom_call_target="tpu_custom_call" | custom-call | flops 17179869184 | bytes 33554432 | tf_op jit(solution)/shard_map/attend/pallas_call | solution.py:199
  105.6 1.5 collective-permute-start.7
  108.1 21.1 %attend.4 = (bf16[4,4096,512]{2,1,0:T(8,128)(2,1)}, bf16[4,4096,512]{2,1,0:T(8,128)(2,1)}, f32[64,2048]{1,0:T(8,128)}, f32[64,2048]{1,0:T(8,128)}, f32[4,1,512]{...) custom-call(bf16[3,4096,128]{2,1,0:T(8,128)(2,1)} %get-tuple-element, ...), custom_call_target="tpu_custom_call" | custom-call | flops 17179869184 | bytes 33554432 | tf_op jit(solution)/shard_map/attend/pallas_call | solution.py:199
  129.5 1.2 collective-permute-start.10
  131.4 21.1 %attend.5 = (bf16[4,4096,512]{2,1,0:T(8,128)(2,1)}, bf16[4,4096,512]{2,1,0:T(8,128)(2,1)}, f32[64,2048]{1,0:T(8,128)}, f32[64,2048]{1,0:T(8,128)}, f32[4,1,512]{...) custom-call(bf16[3,4096,128]{2,1,0:T(8,128)(2,1)} %get-tuple-element, ...), custom_call_target="tpu_custom_call" | custom-call | flops 17179869184 | bytes 33554432 | tf_op jit(solution)/shard_map/attend/pallas_call | solution.py:199
  155.7 3.6 collective-permute-done.13.refs_10_
  159.3 2.9 collective-permute-done.14.refs_11_
  162.2 28.0 %middle.1 = (bf16[192,1024]{1,0:T(8,128)(2,1)}, bf16[192,1024]{1,0:T(8,128)(2,1)}, bf16[192,1024]{1,0:T(8,128)(2,1)}, bf16[192,1024]{1,0:T(8,128)(2,1)}, bf16[10...) custom-call(s32[1]{0:T(128)} %bitcast.info_ref.place_ref.refs_0_, ...), custom_call_target="tpu_custom_call" | custom-call | flops 15099494400 | bytes 31457280 | tf_op jit(solution)/shard_map/middle/pallas_call | solution.py:518
  192.4 14.8 %weight_grads.1 = (bf16[768,768]{1,0:T(8,128)(2,1)}, bf16[768,768]{1,0:T(8,128)(2,1)}, bf16[768,768]{1,0:T(8,128)(2,1)}, bf16[768,768]{1,0:T(8,128)(2,1)}, bf16[1152,768]{1,0:T(8,128)(2,1)}) custom-call(s32[1]{0:T(128)} %bitcast.info_ref.place_ref.refs_0_, bf16[1024,768]{1,0:T(8,128)(2,1)} %get-tuple-element.191.second_ref, ...), custom_call_target="tpu_custom_call" | custom-call | flops 6643777536 | bytes 20971520 | tf_op jit(solution)/shard_map/weight_grads/pallas_call | solution.py:725
  207.2 2.9 collective-permute-done.17.refs_2_.refs_12_
  210.1 5.3 %all-to-all-start.1 = ((bf16[8,144,768]{2,1,0:T(8,128)(2,1)}), bf16[8,144,768]{2,1,0:T(8,128)(2,1)}, u32[]{:S(2)}, u32[]{:S(2)}) async-start(bf16[8,144,768]{2,1,0:T(8,128)(2,1)} %bitcast.25), calls=%async_computation.1 | async-start | bytes 3538944 | tf_op jit(solution)/shard_map/all_to_all | solution.py:969
  216.3 1.3 collective-permute-start.21
  218.5 39.0 %attend_back.3 = (bf16[192,1024]{1,0:T(8,128)(2,1)}, bf16[192,1024]{1,0:T(8,128)(2,1)}, bf16[192,1024]{1,0:T(8,128)(2,1)}, bf16[192,1024]{1,0:T(8,128)(2,1)}, bf16[768,768]{1,0:T(8,128)(2,1)}) custom-call(bf16[3,4096,128]{2,1,0:T(8,128)(2,1)} %get-tuple-element.179.v_ref, bf16[3,64,4096]{2,1,0:T(8,128)(2,1)} %get-tuple-element.180.kt_ref, ...), custom_call_target="tpu_custom_call" | custom-call | flops 25769803776 | bytes 33554432 | tf_op jit(solution)/shard_map/attend_back/pallas_call | solution.py:315
  257.5 11.5 %collective-permute-done.21.refs_3_ = bf16[768,768]{1,0:T(8,128)(2,1)} collective-permute-done((bf16[768,768]{1,0:T(8,128)(2,1)}, bf16[768,768]{1,0:T(8,128)(2,1)}, u32[]{:S(2)}, u32[]{:S(2)}) %collective-permute-start.21) | collective-permute-done | bytes 1179680 | tf_op jit(solution)/shard_map/ppermute | solution.py:895
  269.1 4.2 add_up.1
  273.8 1.6 collective-permute-start.24
  275.4 6.0 %all-to-all-start.2 = ((bf16[8,96,768]{2,1,0:T(8,128)(2,1)}), bf16[8,96,768]{2,1,0:T(8,128)(2,1)}, u32[]{:S(2)}, u32[]{:S(2)}) async-start(bf16[8,96,768]{2,1,0:T(8,128)(2,1)} %bitcast.26), calls=%async_computation.2 | async-start | bytes 2359296 | tf_op jit(solution)/shard_map/all_to_all | solution.py:969
  281.4 39.1 %attend_back.4 = (bf16[192,1024]{1,0:T(8,128)(2,1)}, bf16[192,1024]{1,0:T(8,128)(2,1)}, bf16[192,1024]{1,0:T(8,128)(2,1)}, bf16[192,1024]{1,0:T(8,128)(2,1)}, bf16[768,768]{1,0:T(8,128)(2,1)}) custom-call(bf16[3,4096,128]{2,1,0:T(8,128)(2,1)} %get-tuple-element.179.v_ref, ...), custom_call_target="tpu_custom_call", output_to_operand_aliasing={{4}: (16, {})} | custom-call | flops 25769803776 | bytes 33554432 | tf_op jit(solution)/shard_map/attend_back/pallas_call | solution.py:315
  321.5 2.9 owned.1
  325.0 1.3 collective-permute-start.29
  326.8 1.6 collective-permute-start.27
  328.5 39.6 %attend_back.5 = (bf16[192,1024]{1,0:T(8,128)(2,1)}, bf16[192,1024]{1,0:T(8,128)(2,1)}, bf16[192,1024]{1,0:T(8,128)(2,1)}, bf16[192,1024]{1,0:T(8,128)(2,1)}, bf16[768,768]{1,0:T(8,128)(2,1)}) custom-call(bf16[3,4096,128]{2,1,0:T(8,128)(2,1)} %get-tuple-element.179.v_ref, ...), custom_call_target="tpu_custom_call", output_to_operand_aliasing={{4}: (16, {})} | custom-call | flops 25769803776 | bytes 33554432 | tf_op jit(solution)/shard_map/attend_back/pallas_call | solution.py:315
  369.0 1.9 collective-permute-done.30.refs_4_
  371.7 2.8 finish_wide.1
  374.5 5.9 %all-to-all-start.3 = ((bf16[8,96,768]{2,1,0:T(8,128)(2,1)}), bf16[8,96,768]{2,1,0:T(8,128)(2,1)}, u32[]{:S(2)}, u32[]{:S(2)}) async-start(bf16[8,96,768]{2,1,0:T(8,128)(2,1)} %bitcast.23), calls=%async_computation.3 | async-start | bytes 2359296 | tf_op jit(solution)/shard_map/all_to_all | solution.py:969
  381.5 1.2 collective-permute-start.33
  382.7 9.6 %last.2.base_ref.refs_1_ = f32[1024,768]{1,0:T(8,128)} custom-call(bf16[1024,768]{1,0:T(8,128)(2,1)} %bitcast.1.x_ref, f32[1024,768]{1,0:T(8,128)} %get-tuple-element.178.base_ref, bf16[768,640]{1,0:T(8,128)(2,1)} %hold.4.gain_ref.refs_8_.refs_12_.refs_16_.refs_20_.refs_4_, bf16[192,1024]{1,0:T(8,128)(2,1)} %get-tuple-element.202.refs_0_, ...), custom_call_target="tpu_custom_call" | custom-call | flops 2415919104 | bytes 12582912 | tf_op jit(solution)/shard_map/last/pallas_call | solution.py:606
  392.4 8.5 %collective-permute-done.33.refs_3_.refs_4_ = bf16[192,1024]{1,0:T(8,128)(2,1)} collective-permute-done((bf16[192,1024]{1,0:T(8,128)(2,1)}, bf16[192,1024]{1,0:T(8,128)(2,1)}, u32[]{:S(2)}, u32[]{:S(2)}) %collective-permute-start.33) | collective-permute-done | bytes 393248 | tf_op jit(solution)/shard_map/ppermute | solution.py:895
  400.8 7.9 %all-to-all-done.3.refs_0_ = bf16[8,96,768]{2,1,0:T(8,128)(2,1)} async-done(((bf16[8,96,768]{2,1,0:T(8,128)(2,1)}), bf16[8,96,768]{2,1,0:T(8,128)(2,1)}, u32[]{:S(2)}, u32[]{:S(2)}) %all-to-all-start.3) | async-done | bytes 1179680 | tf_op jit(solution)/shard_map/all_to_all | solution.py:969
  408.8 2.1 sum_owned.1.refs_3_
  410.8 1.3 collective-permute-start.34
  413.7 7.7 %last.3.refs_7_ = f32[1024,768]{1,0:T(8,128)} custom-call(bf16[1024,768]{1,0:T(8,128)(2,1)} %bitcast.1.x_ref, f32[1024,768]{1,0:T(8,128)} %last.2.base_ref.refs_1_, bf16[768,640]{1,0:T(8,128)(2,1)} %hold.4.gain_ref.refs_8_.refs_12_.refs_16_.refs_20_.refs_4_, bf16[192,1024]{1,0:T(8,128)(2,1)} %get-tuple-element.242.refs_0_, bf16[192,1024]{1,0:T(8,128)(2,1)} %copy-done.7, ...), custom_call_target="tpu_custom_call" | custom-call | flops 1207959552 | bytes 12582912 | tf_op jit(solution)/shard_map/last/pallas_call | solution.py:606
  422.8 2.4 finish_qkv.1
  (105 shorter events, 21.3 us)
Async XLA Ops:
  9.3 29.6 %all-to-all-start = ((bf16[8,96,640]{2,1,0:T(8,128)(2,1)}), bf16[8,96,640]{2,1,0:T(8,128)(2,1)S(1)}, u32[]{:S(2)}, u32[]{:S(2)}) async-start(bf16[8,96,640]{2,1,0:T(8,128)(2,1)} %own_columns.1), calls=%async_computation | async-start | bytes 1966080 | tf_op jit(solution)/shard_map/all_to_all | solution.py:910
  15.7 113.5 %all-gather.2.cloned.1.call-start = ((), (), s32[]{:S(2)}) async-start(), calls=%async_computation.4 | async-start | bytes 3981312 | tf_op jit(solution)/shard_map/all_gather | solution.py:901
  15.7 35.3 %collective-permute-start = (bf16[1024,768]{1,0:T(8,128)(2,1)}, bf16[1024,768]{1,0:T(8,128)(2,1)}, u32[]{:S(2)}, u32[]{:S(2)}) collective-permute-start(bf16[1024,768]{1,0:T(8,128)(2,1)} %bitcast.1.x_ref), channel_id=1, source_target_pairs={{0,16},{8,24},{16,0},{24,8},{1,17},{9,25},{17,1},{25,9},{2,18},{10... | collective-permute-start | bytes 4718600 | tf_op jit(solution)/shard_map/ppermute | solution.py:895
  38.9 1.0 copy-start
  42.3 26.7 %collective-permute-start.2 = (bf16[1024,768]{1,0:T(8,128)(2,1)}, bf16[1024,768]{1,0:T(8,128)(2,1)}, u32[]{:S(2)}, u32[]{:S(2)}) collective-permute-start(bf16[1024,768]{1,0:T(8,128)(2,1)} %bitcast.1.x_ref), channel_id=1, source_target_pairs={{0,8},{8,0},{16,24},{24,16},{1,9},{9,1},{17,25},{25,17},{2,10},{10... | collective-permute-start | bytes 4718600 | tf_op jit(solution)/shard_map/ppermute | solution.py:895
  51.1 24.8 %collective-permute-start.1 = (bf16[1024,768]{1,0:T(8,128)(2,1)}, bf16[1024,768]{1,0:T(8,128)(2,1)}, u32[]{:S(2)}, u32[]{:S(2)}) collective-permute-start(bf16[1024,768]{1,0:T(8,128)(2,1)} %collective-permute-done.x_ref), channel_id=1, source_target_pairs={{0,8},{8,0},{16,24},{24,16},{1,9},{9,1},{17,25},{25,17},{2,10},{10... | collective-permute-start | bytes 4718600 | tf_op jit(solution)/shard_map/ppermute | solution.py:895
  82.7 24.4 %collective-permute-start.3 = (bf16[768,640]{1,0:T(8,128)(2,1)}, bf16[768,640]{1,0:T(8,128)(2,1)}, u32[]{:S(2)}, u32[]{:S(2)}) collective-permute-start(bf16[768,640]{1,0:T(8,128)(2,1)} %hold.4.gain_ref.refs_8_.refs_12_.refs_16_.refs_20_.refs_4_), channel_id=1, source_target_pairs={{0,8},{8,0},{16,24},{24,16},{1,9},{9,1},{17,25},{25,17},{2,10},{10... | collective-permute-start | bytes 2949128 | tf_op jit(solution)/shard_map/ppermute | solution.py:895
  82.8 24.3 %collective-permute-start.4 = (bf16[768,640]{1,0:T(8,128)(2,1)}, bf16[768,640]{1,0:T(8,128)(2,1)S(1)}, u32[]{:S(2)}, u32[]{:S(2)}) collective-permute-start(bf16[768,640]{1,0:T(8,128)(2,1)} %hold.4.gain_ref.refs_8_.refs_12_.refs_16_.refs_20_.refs_4_), channel_id=1, source_target_pairs={{0,16},{8,24},{16,0},{24,8},{1,17},{9,25},{17,1},{25,9},{2,18},{10... | collective-permute-start | bytes 2949128 | tf_op jit(solution)/shard_map/ppermute | solution.py:895
  104.6 24.6 %collective-permute-start.5 = (bf16[64,1024]{1,0:T(8,128)(2,1)}, bf16[64,1024]{1,0:T(8,128)(2,1)}, u32[]{:S(2)}, u32[]{:S(2)}) collective-permute-start(bf16[64,1024]{1,0:T(8,128)(2,1)} %get-tuple-element.156), channel_id=1, source_target_pairs={{0,8},{8,0},{16,24},{24,16},{1,9},{9,1},{17,25},{25,17},{2,10},{10... | collective-permute-start | bytes 393224 | tf_op jit(solution)/shard_map/ppermute | solution.py:895
  105.3 23.8 %collective-permute-start.6 = (bf16[64,1024]{1,0:T(8,128)(2,1)}, bf16[64,1024]{1,0:T(8,128)(2,1)}, u32[]{:S(2)}, u32[]{:S(2)}) collective-permute-start(bf16[64,1024]{1,0:T(8,128)(2,1)} %get-tuple-element.157), channel_id=1, source_target_pairs={{0,16},{8,24},{16,0},{24,8},{1,17},{9,25},{17,1},{25,9},{2,18},{10... | collective-permute-start | bytes 393224 | tf_op jit(solution)/shard_map/ppermute | solution.py:895
  105.6 23.6 %collective-permute-start.7 = (bf16[64,1024]{1,0:T(8,128)(2,1)}, bf16[64,1024]{1,0:T(8,128)(2,1)}, u32[]{:S(2)}, u32[]{:S(2)}) collective-permute-start(bf16[64,1024]{1,0:T(8,128)(2,1)} %get-tuple-element.158), channel_id=1, source_target_pairs={{0,24},{8,16},{16,8},{24,0},{1,25},{9,17},{17,9},{25,1},{2,26},{10... | collective-permute-start | bytes 393224 | tf_op jit(solution)/shard_map/ppermute | solution.py:895
  107.1 1.0 copy-start.1
  129.2 32.9 %collective-permute-start.8 = (bf16[768,2304]{1,0:T(8,128)(2,1)}, bf16[768,2304]{1,0:T(8,128)(2,1)}, u32[]{:S(2)}, u32[]{:S(2)}) collective-permute-start(bf16[768,2304]{1,0:T(8,128)(2,1)} %get-tuple-element.163.mine_ref), channel_id=1, source_target_pairs={{0,8},{8,0},{16,24},{24,16},{1,9},{9,1},{17,25},{25,17},{2,10},{10... | collective-permute-start | bytes 10616840 | tf_op jit(solution)/shard_map/ppermute | solution.py:895
  129.5 23.1 %collective-permute-start.10 = (bf16[64,1024]{1,0:T(8,128)(2,1)}, bf16[64,1024]{1,0:T(8,128)(2,1)S(1)}, u32[]{:S(2)}, u32[]{:S(2)}) collective-permute-start(bf16[64,1024]{1,0:T(8,128)(2,1)} %get-tuple-element.167), channel_id=1, source_target_pairs={{0,16},{8,24},{16,0},{24,8},{1,17},{9,25},{17,1},{25,9},{2,18},{10... | collective-permute-start | bytes 393224 | tf_op jit(solution)/shard_map/ppermute | solution.py:895
  130.7 21.9 %collective-permute-start.11 = (bf16[64,1024]{1,0:T(8,128)(2,1)}, bf16[64,1024]{1,0:T(8,128)(2,1)S(1)}, u32[]{:S(2)}, u32[]{:S(2)}) collective-permute-start(bf16[64,1024]{1,0:T(8,128)(2,1)} %get-tuple-element.168), channel_id=1, source_target_pairs={{0,24},{8,16},{16,8},{24,0},{1,25},{9,17},{17,9},{25,1},{2,26},{10... | collective-permute-start | bytes 393224 | tf_op jit(solution)/shard_map/ppermute | solution.py:895
  131.4 21.2 %collective-permute-start.9 = (bf16[64,1024]{1,0:T(8,128)(2,1)}, bf16[64,1024]{1,0:T(8,128)(2,1)S(1)}, u32[]{:S(2)}, u32[]{:S(2)}) collective-permute-start(bf16[64,1024]{1,0:T(8,128)(2,1)} %get-tuple-element.166), channel_id=1, source_target_pairs={{0,8},{8,0},{16,24},{24,16},{1,9},{9,1},{17,25},{25,17},{2,10},{10... | collective-permute-start | bytes 393224 | tf_op jit(solution)/shard_map/ppermute | solution.py:895
  153.3 2.4 collective-permute-start.12
  153.8 5.4 %collective-permute-start.13 = (bf16[64,1024]{1,0:T(8,128)(2,1)}, bf16[64,1024]{1,0:T(8,128)(2,1)}, u32[]{:S(2)}, u32[]{:S(2)}) collective-permute-start(bf16[64,1024]{1,0:T(8,128)(2,1)} %get-tuple-element.175), channel_id=1, source_target_pairs={{0,16},{8,24},{16,0},{24,8},{1,17},{9,25},{17,1},{25,9},{2,18},{10... | collective-permute-start | bytes 393224 | tf_op jit(solution)/shard_map/ppermute | solution.py:895
  154.8 7.4 %collective-permute-start.14 = (bf16[64,1024]{1,0:T(8,128)(2,1)}, bf16[64,1024]{1,0:T(8,128)(2,1)}, u32[]{:S(2)}, u32[]{:S(2)}) collective-permute-start(bf16[64,1024]{1,0:T(8,128)(2,1)} %get-tuple-element.176), channel_id=1, source_target_pairs={{0,24},{8,16},{16,8},{24,0},{1,25},{9,17},{17,9},{25,1},{2,26},{10... | collective-permute-start | bytes 393224 | tf_op jit(solution)/shard_map/ppermute | solution.py:895
  155.5 62.1 %collective-permute-start.18 = (bf16[768,640]{1,0:T(8,128)(2,1)}, bf16[768,640]{1,0:T(8,128)(2,1)S(1)}, u32[]{:S(2)}, u32[]{:S(2)}) collective-permute-start(bf16[768,640]{1,0:T(8,128)(2,1)} %get-tuple-element.201.refs_10_.refs_14_.refs_18_.refs_22_.refs_6_), channel_id=1, source_target_pairs={{0,8},{8,0},{16,24},{24,16},{1,9},{9,1},{17,25},{25,17},{2,10},{10... | collective-permute-start | bytes 2949128 | tf_op jit(solution)/shard_map/ppermute | solution.py:895
  190.1 17.0 %collective-permute-start.15 = (bf16[192,1024]{1,0:T(8,128)(2,1)}, bf16[192,1024]{1,0:T(8,128)(2,1)}, u32[]{:S(2)}, u32[]{:S(2)}) collective-permute-start(bf16[192,1024]{1,0:T(8,128)(2,1)} %get-tuple-element.188), channel_id=1, source_target_pairs={{0,8},{8,0},{16,24},{24,16},{1,9},{9,1},{17,25},{25,17},{2,10},{10... | collective-permute-start | bytes 1179656 | tf_op jit(solution)/shard_map/ppermute | solution.py:895
  190.5 16.6 %collective-permute-start.16 = (bf16[192,1024]{1,0:T(8,128)(2,1)}, bf16[192,1024]{1,0:T(8,128)(2,1)}, u32[]{:S(2)}, u32[]{:S(2)}) collective-permute-start(bf16[192,1024]{1,0:T(8,128)(2,1)} %get-tuple-element.189), channel_id=1, source_target_pairs={{0,16},{8,24},{16,0},{24,8},{1,17},{9,25},{17,1},{25,9},{2,18},{10... | collective-permute-start | bytes 1179656 | tf_op jit(solution)/shard_map/ppermute | solution.py:895
  191.3 18.8 %collective-permute-start.17 = (bf16[192,1024]{1,0:T(8,128)(2,1)}, bf16[192,1024]{1,0:T(8,128)(2,1)}, u32[]{:S(2)}, u32[]{:S(2)}) collective-permute-start(bf16[192,1024]{1,0:T(8,128)(2,1)} %get-tuple-element.190), channel_id=1, source_target_pairs={{0,24},{8,16},{16,8},{24,0},{1,25},{9,17},{17,9},{25,1},{2,26},{10... | collective-permute-start | bytes 1179656 | tf_op jit(solution)/shard_map/ppermute | solution.py:895
  210.1 59.0 %all-to-all-start.1 = ((bf16[8,144,768]{2,1,0:T(8,128)(2,1)}), bf16[8,144,768]{2,1,0:T(8,128)(2,1)}, u32[]{:S(2)}, u32[]{:S(2)}) async-start(bf16[8,144,768]{2,1,0:T(8,128)(2,1)} %bitcast.25), calls=%async_computation.1 | async-start | bytes 3538944 | tf_op jit(solution)/shard_map/all_to_all | solution.py:969
  215.4 42.1 %collective-permute-start.19 = (bf16[768,768]{1,0:T(8,128)(2,1)}, bf16[768,768]{1,0:T(8,128)(2,1)}, u32[]{:S(2)}, u32[]{:S(2)}) collective-permute-start(bf16[768,768]{1,0:T(8,128)(2,1)} %get-tuple-element.204), channel_id=1, source_target_pairs={{0,8},{8,0},{16,24},{24,16},{1,9},{9,1},{17,25},{25,17},{2,10},{10... | collective-permute-start | bytes 3538952 | tf_op jit(solution)/shard_map/ppermute | solution.py:895
  215.8 41.8 %collective-permute-start.20 = (bf16[768,768]{1,0:T(8,128)(2,1)}, bf16[768,768]{1,0:T(8,128)(2,1)}, u32[]{:S(2)}, u32[]{:S(2)}) collective-permute-start(bf16[768,768]{1,0:T(8,128)(2,1)} %get-tuple-element.205), channel_id=1, source_target_pairs={{0,16},{8,24},{16,0},{24,8},{1,17},{9,25},{17,1},{25,9},{2,18},{10... | collective-permute-start | bytes 3538952 | tf_op jit(solution)/shard_map/ppermute | solution.py:895
  216.3 52.7 %collective-permute-start.21 = (bf16[768,768]{1,0:T(8,128)(2,1)}, bf16[768,768]{1,0:T(8,128)(2,1)}, u32[]{:S(2)}, u32[]{:S(2)}) collective-permute-start(bf16[768,768]{1,0:T(8,128)(2,1)} %get-tuple-element.206), channel_id=1, source_target_pairs={{0,24},{8,16},{16,8},{24,0},{1,25},{9,17},{17,9},{25,1},{2,26},{10... | collective-permute-start | bytes 3538952 | tf_op jit(solution)/shard_map/ppermute | solution.py:895
  217.6 1.0 copy-start.2
  273.3 47.3 %collective-permute-start.22 = (bf16[192,1024]{1,0:T(8,128)(2,1)}, bf16[192,1024]{1,0:T(8,128)(2,1)S(1)}, u32[]{:S(2)}, u32[]{:S(2)}) collective-permute-start(bf16[192,1024]{1,0:T(8,128)(2,1)} %get-tuple-element.211), channel_id=1, source_target_pairs={{0,8},{8,0},{16,24},{24,16},{1,9},{9,1},{17,25},{25,17},{2,10},{10... | collective-permute-start | bytes 1179656 | tf_op jit(solution)/shard_map/ppermute | solution.py:895
  273.4 47.2 %collective-permute-start.23 = (bf16[192,1024]{1,0:T(8,128)(2,1)}, bf16[192,1024]{1,0:T(8,128)(2,1)S(1)}, u32[]{:S(2)}, u32[]{:S(2)}) collective-permute-start(bf16[192,1024]{1,0:T(8,128)(2,1)} %get-tuple-element.212), channel_id=1, source_target_pairs={{0,16},{8,24},{16,0},{24,8},{1,17},{9,25},{17,1},{25,9},{2,18},{10... | collective-permute-start | bytes 1179656 | tf_op jit(solution)/shard_map/ppermute | solution.py:895
  273.8 46.8 %collective-permute-start.24 = (bf16[192,1024]{1,0:T(8,128)(2,1)}, bf16[192,1024]{1,0:T(8,128)(2,1)}, u32[]{:S(2)}, u32[]{:S(2)}) collective-permute-start(bf16[192,1024]{1,0:T(8,128)(2,1)} %get-tuple-element.213), channel_id=1, source_target_pairs={{0,24},{8,16},{16,8},{24,0},{1,25},{9,17},{17,9},{25,1},{2,26},{10... | collective-permute-start | bytes 1179656 | tf_op jit(solution)/shard_map/ppermute | solution.py:895
  275.4 45.2 %all-to-all-start.2 = ((bf16[8,96,768]{2,1,0:T(8,128)(2,1)}), bf16[8,96,768]{2,1,0:T(8,128)(2,1)}, u32[]{:S(2)}, u32[]{:S(2)}) async-start(bf16[8,96,768]{2,1,0:T(8,128)(2,1)} %bitcast.26), calls=%async_computation.2 | async-start | bytes 2359296 | tf_op jit(solution)/shard_map/all_to_all | solution.py:969
  324.4 43.7 %collective-permute-start.28 = (bf16[240,768]{1,0:T(8,128)(2,1)}, bf16[240,768]{1,0:T(8,128)(2,1)}, u32[]{:S(2)}, u32[]{:S(2)}) collective-permute-start(bf16[240,768]{1,0:T(8,128)(2,1)} %get-tuple-element.228.refs_14_.refs_9_), channel_id=1, source_target_pairs={{0,16},{8,24},{16,0},{24,8},{1,17},{9,25},{17,1},{25,9},{2,18},{10... | collective-permute-start | bytes 1105928 | tf_op jit(solution)/shard_map/ppermute | solution.py:895
  325.0 43.1 %collective-permute-start.29 = (bf16[240,768]{1,0:T(8,128)(2,1)}, bf16[240,768]{1,0:T(8,128)(2,1)}, u32[]{:S(2)}, u32[]{:S(2)}) collective-permute-start(bf16[240,768]{1,0:T(8,128)(2,1)} %get-tuple-element.228.refs_14_.refs_9_), channel_id=1, source_target_pairs={{0,24},{8,16},{16,8},{24,0},{1,25},{9,17},{17,9},{25,1},{2,26},{10... | collective-permute-start | bytes 1105928 | tf_op jit(solution)/shard_map/ppermute | solution.py:895
  326.3 41.8 %collective-permute-start.25 = (bf16[192,1024]{1,0:T(8,128)(2,1)}, bf16[192,1024]{1,0:T(8,128)(2,1)S(1)}, u32[]{:S(2)}, u32[]{:S(2)}) collective-permute-start(bf16[192,1024]{1,0:T(8,128)(2,1)} %get-tuple-element.225), channel_id=1, source_target_pairs={{0,8},{8,0},{16,24},{24,16},{1,9},{9,1},{17,25},{25,17},{2,10},{10... | collective-permute-start | bytes 1179656 | tf_op jit(solution)/shard_map/ppermute | solution.py:895
  326.3 41.8 %collective-permute-start.26 = (bf16[192,1024]{1,0:T(8,128)(2,1)}, bf16[192,1024]{1,0:T(8,128)(2,1)S(1)}, u32[]{:S(2)}, u32[]{:S(2)}) collective-permute-start(bf16[192,1024]{1,0:T(8,128)(2,1)} %get-tuple-element.226), channel_id=1, source_target_pairs={{0,16},{8,24},{16,0},{24,8},{1,17},{9,25},{17,1},{25,9},{2,18},{10... | collective-permute-start | bytes 1179656 | tf_op jit(solution)/shard_map/ppermute | solution.py:895
  326.8 41.3 %collective-permute-start.27 = (bf16[192,1024]{1,0:T(8,128)(2,1)}, bf16[192,1024]{1,0:T(8,128)(2,1)}, u32[]{:S(2)}, u32[]{:S(2)}) collective-permute-start(bf16[192,1024]{1,0:T(8,128)(2,1)} %get-tuple-element.227), channel_id=1, source_target_pairs={{0,24},{8,16},{16,8},{24,0},{1,25},{9,17},{17,9},{25,1},{2,26},{10... | collective-permute-start | bytes 1179656 | tf_op jit(solution)/shard_map/ppermute | solution.py:895
  368.1 0.9 copy-start.6
  369.0 1.9 collective-permute-start.30
  374.5 34.2 %all-to-all-start.3 = ((bf16[8,96,768]{2,1,0:T(8,128)(2,1)}), bf16[8,96,768]{2,1,0:T(8,128)(2,1)}, u32[]{:S(2)}, u32[]{:S(2)}) async-start(bf16[8,96,768]{2,1,0:T(8,128)(2,1)} %bitcast.23), calls=%async_computation.3 | async-start | bytes 2359296 | tf_op jit(solution)/shard_map/all_to_all | solution.py:969
  380.5 11.9 %collective-permute-start.31 = (bf16[192,1024]{1,0:T(8,128)(2,1)}, bf16[192,1024]{1,0:T(8,128)(2,1)S(1)}, u32[]{:S(2)}, u32[]{:S(2)}) collective-permute-start(bf16[192,1024]{1,0:T(8,128)(2,1)} %get-tuple-element.243), channel_id=1, source_target_pairs={{0,8},{8,0},{16,24},{24,16},{1,9},{9,1},{17,25},{25,17},{2,10},{10... | collective-permute-start | bytes 1179656 | tf_op jit(solution)/shard_map/ppermute | solution.py:895
  381.0 11.4 %collective-permute-start.32 = (bf16[192,1024]{1,0:T(8,128)(2,1)}, bf16[192,1024]{1,0:T(8,128)(2,1)S(1)}, u32[]{:S(2)}, u32[]{:S(2)}) collective-permute-start(bf16[192,1024]{1,0:T(8,128)(2,1)} %get-tuple-element.244), channel_id=1, source_target_pairs={{0,16},{8,24},{16,0},{24,8},{1,17},{9,25},{17,1},{25,9},{2,18},{10... | collective-permute-start | bytes 1179656 | tf_op jit(solution)/shard_map/ppermute | solution.py:895
  381.5 19.4 %collective-permute-start.33 = (bf16[192,1024]{1,0:T(8,128)(2,1)}, bf16[192,1024]{1,0:T(8,128)(2,1)}, u32[]{:S(2)}, u32[]{:S(2)}) collective-permute-start(bf16[192,1024]{1,0:T(8,128)(2,1)} %get-tuple-element.245), channel_id=1, source_target_pairs={{0,24},{8,16},{16,8},{24,0},{1,25},{9,17},{17,9},{25,1},{2,26},{10... | collective-permute-start | bytes 1179656 | tf_op jit(solution)/shard_map/ppermute | solution.py:895
  392.3 16.4 %copy-start.7 = (bf16[192,1024]{1,0:T(8,128)(2,1)}, bf16[192,1024]{1,0:T(8,128)(2,1)S(1)}, u32[]{:S(2)}) copy-start(bf16[192,1024]{1,0:T(8,128)(2,1)S(1)} %collective-permute-done.31.refs_1_.refs_2_) | copy-start | bytes 1179652
  392.3 16.4 %copy-start.8 = (bf16[192,1024]{1,0:T(8,128)(2,1)}, bf16[192,1024]{1,0:T(8,128)(2,1)S(1)}, u32[]{:S(2)}) copy-start(bf16[192,1024]{1,0:T(8,128)(2,1)S(1)} %collective-permute-done.32.refs_2_.refs_3_) | copy-start | bytes 1179652
  410.8 10.6 %collective-permute-start.34 = (bf16[96,768]{1,0:T(8,128)(2,1)}, bf16[96,768]{1,0:T(8,128)(2,1)S(1)}, u32[]{:S(2)}, u32[]{:S(2)}) collective-permute-start(bf16[96,768]{1,0:T(8,128)(2,1)} %sum_owned.1.refs_3_), channel_id=1, source_target_pairs={{0,8},{8,0},{16,24},{24,16},{1,9},{9,1},{17,25},{25,17},{2,10},{10... | collective-permute-start | bytes 442376 | tf_op jit(solution)/shard_map/ppermute | solution.py:895
  412.1 9.4 %collective-permute-start.35 = (bf16[96,768]{1,0:T(8,128)(2,1)}, bf16[96,768]{1,0:T(8,128)(2,1)S(1)}, u32[]{:S(2)}, u32[]{:S(2)}) collective-permute-start(bf16[96,768]{1,0:T(8,128)(2,1)} %sum_owned.1.refs_3_), channel_id=1, source_target_pairs={{0,16},{8,24},{16,0},{24,8},{1,17},{9,25},{17,1},{25,9},{2,18},{10... | collective-permute-start | bytes 442376 | tf_op jit(solution)/shard_map/ppermute | solution.py:895
  412.6 8.9 %collective-permute-start.36 = (bf16[96,768]{1,0:T(8,128)(2,1)}, bf16[96,768]{1,0:T(8,128)(2,1)S(1)}, u32[]{:S(2)}, u32[]{:S(2)}) collective-permute-start(bf16[96,768]{1,0:T(8,128)(2,1)} %sum_owned.1.refs_3_), channel_id=1, source_target_pairs={{0,24},{8,16},{16,8},{24,0},{1,25},{9,17},{17,9},{25,1},{2,26},{10... | collective-permute-start | bytes 442376 | tf_op jit(solution)/shard_map/ppermute | solution.py:895
  (10 other events, 7.2 us)
Sparse Core Ops, SparseCore 0:
  42.4 64.4 all-gather.1
